TPU v7x, 32 devices: a whole 2x2x4 slice. The times are simulated.
32 devices in a mesh: dp: 2 (over x), mp: 16 (over z, y, core).
Axes of the slice: x: 2, y: 2, z: 4, core: 2. Of those that a mesh axis runs over, the one named last changes fastest.
Arguments:
- hidden_in: bfloat16 [1024, 8192], P('dp', 'mp'), may hold values from -6 to 6
- queries: bfloat16 [1024, 8192], P('dp', 'mp'), may hold values from -100 to 100
- key_rows: bfloat16 [1024, 1024], P('dp'), may hold values from -5.5 to 5.5
- value_rows: bfloat16 [1024, 1024], P('dp'), may hold values from -6 to 6
- teacher_proj: bfloat16 [8192, 8192], P('mp'), may hold values from -0.0625 to 0.0625
- mixer_in: bfloat16 [2, 8192, 8192], P(None, 'dp', 'mp'), may hold values from -0.0625 to 0.0625
- shared_in: bfloat16 [8192, 384], P('mp'), may hold values from -0.0625 to 0.0625
- dt_bias: float32 [128], P('mp'), may hold values from -3 to 1
- a_log: float32 [128], P('mp'), may hold values from -6.9 to 0
- d_skip: float32 [128], P('mp'), may hold values from 0.5 to 1.5
- norm_gain: float32 [8192], P('mp'), may hold values from 0.1 to 1.9
- mixer_out: bfloat16 [8192, 8192], P('mp'), may hold values from -0.0625 to 0.0625
Outputs:
- misfit: bfloat16 [1024, 8192], P(('dp', 'mp'))
All inputs are finite; a program needn't handle non-finite values.
Results may differ from a plain program's by a relative error of at most 0.0051.
Values may be sent and summed in bfloat16 or wider, within the bound.
No kernel may reach another device: no remote copies, remote signals or barrier semaphores. Data moves between devices by JAX's collectives and lax.ppermute only.
A program may use at most 192 MiB of HBM per device.

v0:
```python
import jax
import jax.numpy as jnp
from jax import lax
from jax.sharding import PartitionSpec as P

QHEADS = 64
KVHEADS = 8
HEAD = 128
SHEADS = 128
SHEAD = 64
STATE = 128
BLOCK = 128


norm_eps = 1e-05


def ssd_block(carry_state, block_in):
    x_block, b_block, c_block, step_block, decay_block = block_in
    running = jnp.cumsum(decay_block, axis=0)
    spans = running[:, None, :] - running[None, :, :]
    size_here = x_block.shape[0]
    lower_mask = (jnp.arange(size_here)[:, None] >= jnp.arange(size_here)[None, :])[:, :, None]
    decay_mat = jnp.exp(jnp.where(lower_mask, spans, -jnp.inf))
    contact = jnp.dot(c_block, b_block.T, precision=lax.Precision.HIGHEST)
    weight = contact[:, :, None] * decay_mat * step_block[None, :, :]
    within = jnp.einsum("tsh,shp->thp", weight, x_block, precision=lax.Precision.HIGHEST)
    carried = (
        jnp.einsum("tn,hpn->thp", c_block, carry_state, precision=lax.Precision.HIGHEST)
        * jnp.exp(running)[:, :, None]
    )
    tail_weight = jnp.exp(running[-1][None, :] - running) * step_block
    carry_state = carry_state * jnp.exp(running[-1])[:, None, None] + jnp.einsum(
        "sh,shp,sn->hpn", tail_weight, x_block, b_block, precision=lax.Precision.HIGHEST
    )
    return (carry_state, within + carried)


def local(
    hidden_in,
    queries,
    key_rows,
    value_rows,
    teacher_proj,
    mixer_in,
    shared_in,
    dt_bias,
    a_log,
    d_skip,
    norm_gain,
    mixer_out,
):
    my_index = lax.axis_index("mp")
    heads_here = dt_bias.shape[0]
    features_all = lax.all_gather(hidden_in, "mp", axis=1, tiled=True)
    length = features_all.shape[0]
    channels = mixer_in.shape[2]
    projected = jnp.einsum(
        "td,kdc->ktc",
        features_all,
        lax.all_gather(mixer_in, "dp", axis=1, tiled=True),
        preferred_element_type=jnp.float32,
    )
    shared = lax.psum(jnp.dot(hidden_in, shared_in, preferred_element_type=jnp.float32), "mp")
    b_in = shared[:, :STATE]
    c_out = shared[:, STATE : 2 * STATE]
    dt_raw = lax.dynamic_slice_in_dim(shared, 2 * STATE + my_index * heads_here, heads_here, 1)
    step_size = jax.nn.softplus(dt_raw + dt_bias)
    log_decay = -step_size * jnp.exp(a_log)
    x_heads = projected[0].reshape(length, heads_here, SHEAD)
    blocks = length // BLOCK

    def split_blocks(source):
        return source.reshape((blocks, BLOCK) + source.shape[1:])

    start_state = jnp.zeros((heads_here, SHEAD, STATE), jnp.float32)
    final_state, ssd_parts = lax.scan(
        ssd_block,
        start_state,
        (
            split_blocks(x_heads),
            split_blocks(b_in),
            split_blocks(c_out),
            split_blocks(step_size),
            split_blocks(log_decay),
        ),
    )
    ssd_out = ssd_parts.reshape(length, heads_here, SHEAD) + d_skip[None, :, None] * x_heads
    gated = ssd_out.reshape(length, channels) * jax.nn.silu(projected[1])
    sum_squares = lax.psum(jnp.sum(gated * gated, axis=1), "mp")
    normed = (
        gated * lax.rsqrt(sum_squares / (SHEADS * SHEAD) + norm_eps)[:, None] * norm_gain
    ).astype(jnp.bfloat16)
    head_count = queries.shape[1] // HEAD
    kv_head = my_index * head_count // (QHEADS // KVHEADS)
    key_sel = lax.dynamic_slice_in_dim(key_rows, kv_head * HEAD, HEAD, 1)
    value_sel = lax.dynamic_slice_in_dim(value_rows, kv_head * HEAD, HEAD, 1)
    query_heads = queries.reshape(length, head_count, HEAD)
    scores = jnp.einsum(
        "thd,sd->hts", query_heads, key_sel, preferred_element_type=jnp.float32
    ) * HEAD ** (-0.5)
    causal = jnp.arange(length)[:, None] >= jnp.arange(length)[None, :]
    attn_probs = jax.nn.softmax(jnp.where(causal[None], scores, -jnp.inf), axis=-1).astype(
        jnp.bfloat16
    )
    context = jnp.einsum("hts,sd->thd", attn_probs, value_sel, preferred_element_type=jnp.float32)
    context = context.astype(jnp.bfloat16).reshape(length, head_count * HEAD)
    mismatch = lax.psum_scatter(
        jnp.dot(normed, mixer_out, preferred_element_type=jnp.float32)
        - jnp.dot(context, teacher_proj, preferred_element_type=jnp.float32),
        "mp",
        scatter_dimension=0,
        tiled=True,
    )
    return mismatch.astype(jnp.bfloat16)


def solution(mesh):
    placed = (
        P("dp", "mp"),
        P("dp", "mp"),
        P("dp", None),
        P("dp", None),
        P("mp", None),
        P(None, "dp", "mp"),
        P("mp", None),
        P("mp"),
        P("mp"),
        P("mp"),
        P("mp"),
        P("mp", None),
    )
    return jax.shard_map(
        local, mesh=mesh, in_specs=placed, out_specs=P(("dp", "mp"), None), check_vma=False
    )
```

profile of v0, /device:TPU:0, one launch (start us, length us, event | category | flops | bytes accessed | tf_op | source)
XLA Modules:
  0.0 666.8 jit_solution(16243662364924715187)
XLA Ops:
  6.5 2.6 fusion.81
  9.1 0.0 all-reduce.2.cloned.1.call-update
  9.1 0.0 all-gather.5.cloned.1.call-start
  9.2 0.7 all-gather.5.cloned.1.call-update
  9.9 0.0 all-gather.3.cloned.1.call-start
  9.9 11.3 %copy.33 = bf16[2,4096,512]{1,2,0:T(8,128)(2,1)} copy(bf16[2,4096,512]{2,1,0:T(8,128)(2,1)} %param.19) | data formatting | bytes 16777216 | tf_op args[5]
  21.2 0.0 reduce-scatter.2.cloned.1.call-start
  21.4 0.5 copy-done.9
  21.9 0.1 mul.116
  22.0 0.1 mul.117
  22.0 0.1 iota_compare_fusion.1
  22.1 0.2 copy-done.4
  22.3 0.7 fusion.58
  23.0 2.1 fusion.80
  25.2 2.2 fusion.48
  27.3 78.2 %all-reduce.2.cloned.1.call-done = f32[512,384]{0,1:T(8,128)} async-done(((f32[512,384]{0,1:T(8,128)}), f32[512,384]{0,1:T(8,128)}) %all-reduce.2.cloned.1.call-update) | async-done | bytes 786448 | tf_op jit(solution)/shard_map/psum | solution.py:64
  105.5 1.1 fusion.79
  106.6 0.1 copy.48
  106.7 0.1 copy.49
  106.9 0.8 fusion.69
  107.7 77.3 %all-gather.5.cloned.1.call-done = bf16[512,8192]{1,0:T(8,128)(2,1)} async-done(((bf16[512,512]{1,0:T(8,128)(2,1)}), bf16[512,8192]{1,0:T(8,128)(2,1)}) %all-gather.5.cloned.1.call-update) | async-done | bytes 8388624 | tf_op jit(solution)/shard_map/all_gather | solution.py:55
  185.0 198.7 %all-gather.3.cloned.1.call-done = bf16[2,8192,512]{1,2,0:T(8,128)(2,1)} async-done(((bf16[2,4096,512]{1,2,0:T(8,128)(2,1)}), bf16[2,8192,512]{1,2,0:T(8,128)(2,1)}) %all-gather.3.cloned.1.call-update) | async-done | bytes 16777232 | tf_op jit(solution)/shard_map/all_gather | solution.py:61
  383.7 14.2 %fusion.45 = f32[2,512,512]{1,2,0:T(8,128)S(1)} fusion(bf16[2,8192,512]{1,2,0:T(8,128)(2,1)} %all-gather.3.cloned.1.call-done, bf16[512,8192]{1,0:T(8,128)(2,1)} %all-gather.5.cloned.1.call-done), kind=kOutput, calls=%fused_computation.58 | convolution fusion | flops 8589934592 | bytes 27262976 | tf_op jit(solution)/shard_map/td,kdc->ktc/dot_general | solution.py:58
  397.9 1.3 fusion.78
  399.2 0.4 copy-done.2
  399.6 0.4 reshape_reshape_squeeze.3
  400.0 0.1 copy.36
  400.1 14.9 %while.13 = (s32[]{:T(128)}, f32[8,64,128]{2,1,0:T(8,128)S(1)}, f32[4,128,8,64]{1,3,2,0:T(8,128)}, f32[4,128,8]{1,2,0:T(8,128)S(1)}, f32[4,128,8]{1,2,0:T(8,128)...) while((s32[]{:T(128)}, f32[8,64,128]{2,1,0:T(8,128)S(1)}, ...), condition=%wide.region_3.4_spmd.clone, body=%wide.region_1.3_spmd.clone.sunk | while | flops 328287232 | bytes 2629412 | solution.py:77
  400.1 0.1 copy.69
  400.2 0.2 reduce_window_sum.13
  400.4 0.3 fusion.109
  400.8 1.2 convolution_bitcast_fusion.2
  401.9 0.1 copy.70
  402.1 1.1 fusion.110
  403.3 0.5 convolution_add_fusion.2
  403.8 0.1 copy.69
  403.9 0.2 reduce_window_sum.13
  404.2 0.3 fusion.109
  404.5 1.2 convolution_bitcast_fusion.2
  405.7 0.1 copy.70
  405.8 1.1 fusion.110
  407.0 0.5 convolution_add_fusion.2
  407.5 0.1 copy.69
  407.6 0.2 reduce_window_sum.13
  407.9 0.3 fusion.109
  408.2 1.2 convolution_bitcast_fusion.2
  409.4 0.1 copy.70
  409.5 1.1 fusion.110
  410.7 0.5 convolution_add_fusion.2
  411.3 0.1 copy.69
  411.4 0.2 reduce_window_sum.13
  411.6 0.3 fusion.109
  411.9 1.2 convolution_bitcast_fusion.2
  413.1 0.1 copy.70
  413.3 1.1 fusion.110
  414.4 0.5 convolution_add_fusion.2
  415.0 2.6 squeeze.27
  417.6 1.9 copy.39
  419.5 1.6 multiply_reduce_fusion
  421.2 33.4 %psum.15 = f32[512]{0:T(512)S(1)} all-reduce(f32[512]{0:T(512)S(1)} %bitcast.147), channel_id=1, replica_groups=mesh['dp'=2,'mp'=16] {'mp'}, use_global_device_ids=true, to_apply=%region_5.6 | all-reduce | flops 512 | bytes 4096 | tf_op jit(solution)/shard_map/psum | solution.py:90
  454.6 14.6 %fusion.56 = f32[512,8192]{1,0:T(8,128)} fusion(bf16[512,8192]{1,0:T(8,128)(2,1)} %param.25, f32[64,8,4,128]{3,2,1,0:T(4,128)S(1)} %bitcast.141, f32[512]{0:T(512)S(1)} %copy-done.6, f32[512]{0:T(512)S(1)} %add_rsqrt_fusion, f32[512]{0:T(512)S(1)} %mul.117, f32[2,512,512]{1,2,0:T(8,128)} %copy-done.2), kind=kOutput, calls=%fused_computation.73 | convolution fusion | flops 4297588736 | bytes 28317696 | tf_op jit(solution)/shard_map/dot_general | solution.py:109
  469.2 14.0 %convolution_subtract_fusion = f32[512,8192]{1,0:T(8,128)} fusion(f32[512,8192]{1,0:T(8,128)} %fusion.56, bf16[512,512]{0,1:T(8,128)(2,1)S(1)} %bitcast.145, bf16[512,8192]{1,0:T(8,128)(2,1)} %param.18), kind=kOutput, calls=%fused_computation.47 | convolution fusion | flops 4299161600 | bytes 42467328 | tf_op jit(solution)/shard_map/dot_general | solution.py:110
  483.2 175.0 %reduce-scatter.2.cloned.1.call-done = f32[32,8192]{1,0:T(8,128)} async-done(((f32[512,8192]{1,0:T(8,128)}), f32[32,8192]{1,0:T(8,128)}) %reduce-scatter.2.cloned.1.call-update) | async-done | bytes 1048592 | tf_op jit(solution)/shard_map/reduce_scatter | solution.py:108
  658.2 2.1 convert_element_type.19
  (56 shorter events, 0.9 us)
Async XLA Ops:
  6.5 15.6 %copy-start = (bf16[512,1024]{1,0:T(8,128)(2,1)S(1)}, bf16[512,1024]{1,0:T(8,128)(2,1)}, u32[]{:S(2)}) copy-start(bf16[512,1024]{1,0:T(8,128)(2,1)} %param.16) | copy-start | bytes 3145732
  6.5 99.0 %all-reduce.2.cloned.1.call-start = ((), (), s32[]{:S(2)}) async-start(), calls=%async_computation.1 | async-start | bytes 1572864 | tf_op jit(solution)/shard_map/psum | solution.py:64
  9.1 175.9 %all-gather.5.cloned.1.call-start = ((), (), s32[]{:S(2)}) async-start(), calls=%async_computation.3 | async-start | bytes 8912896 | tf_op jit(solution)/shard_map/all_gather | solution.py:55
  9.9 373.8 %all-gather.3.cloned.1.call-start = ((), (), s32[]{:S(2)}) async-start(), calls=%async_computation.2 | async-start | bytes 25165824 | tf_op jit(solution)/shard_map/all_gather | solution.py:61
  21.2 0.7 copy-start.9
  21.2 0.7 copy-start.7
  21.2 1.1 copy-start.4
  21.2 636.9 %reduce-scatter.2.cloned.1.call-start = ((), (), s32[]{:S(2)}) async-start(), calls=%async_computation.4 | async-start | bytes 17825792 | tf_op jit(solution)/shard_map/reduce_scatter | solution.py:108
  25.2 81.7 %copy-start.8 = (f32[8]{0:T(128)S(1)}, f32[8]{0:T(128)}, u32[]{:S(2)}) copy-start(f32[8]{0:T(128)} %param.21) | copy-start | bytes 100
  397.9 1.7 copy-start.2
  415.0 4.6 copy-start.3
  415.0 39.6 %copy-start.6 = (f32[512]{0:T(512)S(1)}, f32[512]{0:T(512)}, u32[]{:S(2)}) copy-start(f32[512]{0:T(512)} %param.24) | copy-start | bytes 6148
  454.5 14.6 %copy-start.5 = (bf16[128,4,512]{2,0,1:T(8,128)(2,1)S(1)}, bf16[128,4,512]{2,0,1:T(8,128)(2,1)}, u32[]{:S(2)}) copy-start(bf16[128,4,512]{2,0,1:T(8,128)(2,1)} %fusion.48) | copy-start | bytes 1572868
  483.1 177.1 %copy-start.1 = (bf16[512,1024]{1,0:T(8,128)(2,1)S(1)}, bf16[512,1024]{1,0:T(8,128)(2,1)}, u32[]{:S(2)}) copy-start(bf16[512,1024]{1,0:T(8,128)(2,1)} %param.16) | copy-start | bytes 3145732
Sparse Core Ops, SparseCore 0:
  10.7 94.7 all-reduce.1
  107.9 77.0 all-gather.4
  186.7 197.0 all-gather.2
  483.3 174.8 reduce-scatter.1
where the time goes:
time: 667 us
  waiting for transfers between devices  530 us (79%)
  matrix products  60.5 us (9%)
  blocking collectives  33.4 us (5%)
  local copies, waits for them, and re-layouts  21.7 us (3%)
  between operations  13.3 us (2%)
  other arithmetic  7.59 us (1%)
    all_gather x1, waiting for transfers between devices, local(): lax.all_gather(mixer_in, 'dp', axis=1, tiled=True)  199 us
    reduce_scatter x1, waiting for transfers between devices, local(): lax.psum_scatter(jnp.dot(normed, mixer_out, preferred_element_type=jnp.fl...  175 us
    psum x1, waiting for transfers between devices, local(): lax.psum(jnp.dot(hidden_in, shared_in, preferred_element_type=jnp.float32...  78.2 us
    all_gather x1, waiting for transfers between devices, local(): features_all = lax.all_gather(hidden_in, 'mp', axis=1, tiled=True)  77.3 us
    psum x1, blocking collectives, local(): sum_squares = lax.psum(jnp.sum(gated * gated, axis=1), 'mp')  33.4 us
    dot_general x1, matrix products, local(): jnp.dot(normed, mixer_out, preferred_element_type=jnp.float32)  14.6 us
    dot_general x1, matrix products, local(): jnp.einsum('td,kdc->ktc', features_all, lax.all_gather(mixer_in, 'dp', ax...  14.2 us
    dot_general x1, matrix products, local(): jnp.dot(context, teacher_proj, preferred_element_type=jnp.float32)  14 us
  transfers between devices with their start and end apart: 4, of which 4 were waited for; matrix products, arithmetic and copies ran while one was open for 3% of the time, Pallas kernels for 0%

commit v1 on v0

v1 whole, which is shorter than its diff:
```python
import functools

import jax
import jax.numpy as jnp
from jax import lax
from jax.experimental import pallas as pl
from jax.experimental.pallas import tpu as pltpu
from jax.sharding import PartitionSpec as P

HEAD = 128
SHEAD = 64
STATE = 128
LANES = 128
OUT_CHUNKS = 4
OUT_TILE = 512
VMEM = 56 * 1024 * 1024

norm_eps = 1e-05
f32 = jnp.float32
bf16 = jnp.bfloat16


def cost(flops, moved):
    return pl.CostEstimate(flops=flops, bytes_accessed=moved, transcendentals=0)


def pick(parts, index):
    chosen = parts[0]
    for m in range(1, len(parts)):
        chosen = jnp.where(index == m, parts[m], chosen)
    return chosen


def reorder_weights(mixer_in, block, spot):
    kinds, rows, channels = mixer_in.shape

    def body(spot_ref, source, target):
        target[...] = source[0]

    return pl.pallas_call(
        body,
        grid_spec=pltpu.PrefetchScalarGridSpec(
            num_scalar_prefetch=1,
            grid=(rows // block, kinds),
            in_specs=[pl.BlockSpec((1, block, channels), lambda r, k, s: (k, s[0] ^ r, 0))],
            out_specs=pl.BlockSpec((block, channels), lambda r, k, s: (r, k)),
        ),
        out_shape=jax.ShapeDtypeStruct((rows, kinds * channels), mixer_in.dtype),
        cost_estimate=cost(0, 4 * mixer_in.size),
        name="reorder_weights",
    )(spot, mixer_in)


def scan_weights(n, rows, b_in, c_out, run_col, run_row, step_row):
    heads = run_row.shape[0]
    pairs = heads // 2
    wide = 2 * rows

    def body(b_ref, c_ref, col_ref, row_ref, step_ref, out_ref):
        below = lax.broadcasted_iota(jnp.int32, (rows, rows), 0) >= lax.broadcasted_iota(
            jnp.int32, (rows, rows), 1
        )
        for j in range(n + 1):
            contact = lax.dot_general(
                c_ref[...],
                b_ref[j * rows : (j + 1) * rows],
                (((1,), (1,)), ((), ())),
                precision=lax.Precision.HIGHEST,
                preferred_element_type=f32,
            )
            for h in range(heads):
                span = col_ref[:, h : h + 1] - row_ref[j, h : h + 1, :]
                if j == n:
                    span = jnp.where(below, span, -jnp.inf)
                weight = contact * jnp.exp(span) * step_ref[j, h : h + 1, :]
                high = weight.astype(bf16)
                low = (weight - high.astype(f32)).astype(bf16)
                at = (h % 2) * rows
                out_ref[h // 2, at : at + rows, j * wide : (j + 1) * wide] = jnp.concatenate(
                    [high, low], axis=1
                )

    grown = (n + 1) * rows
    by_chunk = lambda a: a[:, :grown].reshape(heads, n + 1, rows).transpose(1, 0, 2)
    return pl.pallas_call(
        body,
        out_shape=jax.ShapeDtypeStruct((pairs, wide, (n + 1) * wide), bf16),
        compiler_params=pltpu.CompilerParams(vmem_limit_bytes=VMEM),
        cost_estimate=cost(12 * grown * rows * STATE, 4 * heads * grown * rows),
        name="scan_weights",
    )(
        b_in[:grown],
        c_out[n * rows : grown],
        run_col[n * rows : grown],
        by_chunk(run_row),
        by_chunk(step_row),
    )


def scan_chunk(n, rows, weights, own, others, earlier, skip, gain):
    pairs, wide, _ = weights.shape
    channels = skip.shape[1]

    def body(*refs):
        weights_ref, own_ref, skip_ref, gain_ref = refs[:4]
        other_refs = refs[4 : 4 + len(others)]
        earlier_refs = refs[4 + len(others) : 4 + len(others) + n]
        split_ref, gated_ref, squares_ref = refs[4 + len(others) + n :]
        left = lax.broadcasted_iota(jnp.int32, (rows, LANES), 1) < SHEAD
        squares = jnp.zeros((rows, 1), f32)
        for p in range(pairs):
            lane = slice(p * LANES, (p + 1) * LANES)
            gate_lane = slice(channels + p * LANES, channels + (p + 1) * LANES)
            x = own_ref[:, lane]
            gate = own_ref[:, gate_lane]
            for other in other_refs:
                x = x + other[:, lane].astype(f32)
                gate = gate + other[:, gate_lane].astype(f32)
            high = x.astype(bf16)
            low = (x - high.astype(f32)).astype(bf16)
            both = jnp.concatenate([high, low], axis=1)
            split_ref[p] = jnp.concatenate([both, both], axis=0)
            total = jnp.dot(
                weights_ref[p, :, n * wide : (n + 1) * wide],
                split_ref[p],
                preferred_element_type=f32,
            )
            for j in range(n):
                total = total + jnp.dot(
                    weights_ref[p, :, j * wide : (j + 1) * wide],
                    earlier_refs[j][p],
                    preferred_element_type=f32,
                )
            total = total[:, :LANES] + total[:, LANES:]
            scanned = jnp.where(left, total[:rows], total[rows:])
            gated = (scanned + skip_ref[:, lane] * x) * (gate / (1.0 + jnp.exp(-gate)))
            squares = squares + jnp.sum(gated * gated, axis=1, keepdims=True)
            gated_ref[:, lane] = (gated * gain_ref[:, lane]).astype(bf16)
        squares_ref[...] = squares

    return pl.pallas_call(
        body,
        out_shape=(
            jax.ShapeDtypeStruct((pairs, wide, 2 * LANES), bf16),
            jax.ShapeDtypeStruct((rows, channels), bf16),
            jax.ShapeDtypeStruct((rows, 1), f32),
        ),
        compiler_params=pltpu.CompilerParams(vmem_limit_bytes=VMEM),
        cost_estimate=cost(2 * pairs * wide * wide * 2 * LANES * (n + 1), 8 * rows * channels * 2),
        name="scan_chunk",
    )(weights, own, skip, gain, *others, *earlier)


def project_out(n, width, spots, gated, gated_other, weight, weight_other, scale, teacher):
    length, channels = gated.shape
    half = weight_other.shape[1]
    far = scale.shape[0]
    tile = min(OUT_TILE, width)
    steps = width // tile
    part = length // (2 * far)

    def body(spot_ref, g_ref, go_ref, w_ref, wo_ref, r_ref, t_ref, keep_ref, send_ref):
        z, y = spot_ref[0], spot_ref[1]
        value = jnp.dot(g_ref[...], w_ref[...], preferred_element_type=f32) + jnp.dot(
            go_ref[...], wo_ref[...], preferred_element_type=f32
        )
        value = value.reshape(far, 2, part, tile)
        for zt in range(far):
            near = value[zt, 0] * r_ref[zt, 0] - t_ref[zt, 0]
            away = value[zt, 1] * r_ref[zt, 1] - t_ref[zt, 1]
            keep_ref[zt ^ z] = jnp.where(y == 0, near, away)
            send_ref[zt ^ z] = jnp.where(y == 0, away, near).astype(bf16)

    return pl.pallas_call(
        body,
        grid_spec=pltpu.PrefetchScalarGridSpec(
            num_scalar_prefetch=1,
            grid=(steps,),
            in_specs=[
                pl.BlockSpec((length, channels), lambda t, s: (0, 0)),
                pl.BlockSpec((length, channels), lambda t, s: (0, 0)),
                pl.BlockSpec(
                    (channels, tile), lambda t, s: (0, s[2] * (half // tile) + n * steps + t)
                ),
                pl.BlockSpec((channels, tile), lambda t, s: (0, n * steps + t)),
                pl.BlockSpec((far, 2, part, 1), lambda t, s: (0, 0, 0, 0)),
                pl.BlockSpec((far, 2, part, tile), lambda t, s: (0, 0, 0, n * steps + t)),
            ],
            out_specs=[
                pl.BlockSpec((far, part, tile), lambda t, s: (0, 0, t)),
                pl.BlockSpec((far, part, tile), lambda t, s: (0, 0, t)),
            ],
        ),
        out_shape=(
            jax.ShapeDtypeStruct((far, part, width), f32),
            jax.ShapeDtypeStruct((far, part, width), bf16),
        ),
        compiler_params=pltpu.CompilerParams(vmem_limit_bytes=VMEM),
        cost_estimate=cost(4 * length * channels * width, 8 * channels * width + 6 * length * width),
        name="project_out",
    )(spots, gated, gated_other, weight, weight_other, scale, teacher)


def add_near(keep, came):
    far, part, width = keep.shape

    def body(keep_ref, came_ref, *outs):
        for k in range(far):
            total = keep_ref[k] + came_ref[k].astype(f32)
            outs[k][...] = total.astype(outs[k].dtype)

    return pl.pallas_call(
        body,
        out_shape=tuple(
            jax.ShapeDtypeStruct((part, width), f32 if k == 0 else bf16) for k in range(far)
        ),
        compiler_params=pltpu.CompilerParams(vmem_limit_bytes=VMEM),
        cost_estimate=cost(keep.size, 8 * keep.size),
        name="add_near",
    )(keep, came)


def add_far(kept, came):
    def body(kept_ref, *refs):
        total = kept_ref[...]
        for ref in refs[:-1]:
            total = total + ref[...].astype(f32)
        refs[-1][...] = total.astype(bf16)

    return pl.pallas_call(
        body,
        out_shape=jax.ShapeDtypeStruct(kept.shape, bf16),
        cost_estimate=cost(kept.size, 12 * kept.size),
        name="add_far",
    )(kept, *came)


def local(
    ndp,
    nmp,
    hidden_in,
    queries,
    key_rows,
    value_rows,
    teacher_proj,
    mixer_in,
    shared_in,
    dt_bias,
    a_log,
    d_skip,
    norm_gain,
    mixer_out,
):
    far = nmp // 4
    group = far // ndp
    me = lax.axis_index("mp")
    seq = lax.axis_index("dp")
    core, y, z = me % 2, (me // 2) % 2, me // 4

    def swap(source, k):
        return lax.ppermute(source, "mp", [(s, s ^ k) for s in range(nmp)])

    def cross(source, k):
        return lax.ppermute(source, "dp", [(s, s ^ k) for s in range(ndp)])

    length, block = hidden_in.shape
    channels = mixer_in.shape[2]
    heads = dt_bias.shape[0]
    rows = length // far
    spots = jnp.stack([z, y, core]).astype(jnp.int32)

    def at(source, index):
        return lax.dynamic_index_in_dim(source, index, 0, False)

    part = jnp.dot(hidden_in, shared_in, preferred_element_type=f32)
    part = part.reshape(2, length // 2, -1)
    part = at(part, core) + swap(at(part, 1 - core), 1)
    part = part.reshape(2, length // 4, -1)
    part = at(part, y) + swap(at(part, 1 - y), 2)
    part = part.reshape(far, length // nmp, -1)
    share = at(part, z)
    for k in range(1, far):
        share = share + swap(at(part, z ^ k), 4 * k)
    shares = jnp.stack([share] + [swap(share, 4 * k) for k in range(1, far)])
    shared = jnp.concatenate([at(shares, m ^ z) for m in range(far)])
    came = swap(shared, 2)
    shared = jnp.concatenate([jnp.where(y == 0, shared, came), jnp.where(y == 0, came, shared)])
    came = swap(shared, 1)
    shared = jnp.concatenate(
        [jnp.where(core == 0, shared, came), jnp.where(core == 0, came, shared)]
    )

    turn = (z // group) ^ seq
    spot = (me % (4 * group)).astype(jnp.int32).reshape(1)
    weights_in = reorder_weights(mixer_in, block, spot)
    own_parts, other_parts = [], []
    for n in range(far):
        mine = hidden_in[n * rows : (n + 1) * rows]
        line = [mine] + [swap(mine, 4 * k) for k in range(1, far)]
        line = [jnp.stack(line[m * group : (m + 1) * group]) for m in range(ndp)]
        square = [pick(line, turn ^ d) for d in range(ndp)]
        square = jnp.stack([square[0]] + [cross(square[d], d) for d in range(1, ndp)], 1)
        both = [square, swap(square, 2)]
        all_four = [[q, swap(q, 1)] for q in both]
        features = jnp.concatenate(
            [all_four[b][c][k] for k in range(group) for b in range(2) for c in range(2)], axis=-1
        )
        projected = jnp.dot(
            features.reshape(ndp * rows, -1), weights_in, preferred_element_type=f32
        ).reshape(ndp, rows, -1)
        own_parts.append(projected[0])
        other_parts.append([cross(projected[d].astype(bf16), d) for d in range(1, ndp)])

    head_count = queries.shape[1] // HEAD
    query_heads_all = head_count * nmp
    kv_heads = key_rows.shape[1] // HEAD
    kv_head = me * head_count // (query_heads_all // kv_heads)
    key_sel = lax.dynamic_slice_in_dim(key_rows, kv_head * HEAD, HEAD, 1)
    value_sel = lax.dynamic_slice_in_dim(value_rows, kv_head * HEAD, HEAD, 1)
    query_heads = queries.reshape(length, head_count, HEAD)
    scores = jnp.einsum(
        "thd,sd->hts", query_heads, key_sel, preferred_element_type=f32
    ) * HEAD ** (-0.5)
    causal = jnp.arange(length)[:, None] >= jnp.arange(length)[None, :]
    attn_probs = jax.nn.softmax(jnp.where(causal[None], scores, -jnp.inf), axis=-1).astype(bf16)
    context = jnp.einsum("hts,sd->thd", attn_probs, value_sel, preferred_element_type=f32)
    context = context.astype(bf16).reshape(length, head_count * HEAD)

    half = mixer_out.shape[1] // 2

    def halves(weight):
        return lax.dynamic_slice_in_dim(weight, (1 - core) * half, half, 1)

    mixer_other = swap(halves(mixer_out), 1)
    teacher_other = swap(halves(teacher_proj), 1)
    teacher_own = lax.dynamic_slice_in_dim(teacher_proj, core * half, half, 1)
    teacher = jnp.dot(context, teacher_own, preferred_element_type=f32) + jnp.dot(
        swap(context, 1), teacher_other, preferred_element_type=f32
    )
    teacher = teacher.reshape(far, 2, rows // 2, half)

    b_in = shared[:, :STATE]
    c_out = shared[:, STATE : 2 * STATE]
    dt_raw = lax.dynamic_slice_in_dim(shared, 2 * STATE + me * heads, heads, 1)
    step_size = jax.nn.softplus(dt_raw + dt_bias)
    log_decay = -step_size * jnp.exp(a_log)
    running = jnp.dot(causal.astype(f32), log_decay, precision=lax.Precision.HIGHEST)
    run_row, step_row = running.T, step_size.T
    skip = jnp.repeat(d_skip, SHEAD)[None, :]
    earlier, gated, gated_other, squares = [], [], [], []
    for n in range(far):
        weights = scan_weights(n, rows, b_in, c_out, running, run_row, step_row)
        split, gated_n, squares_n = scan_chunk(
            n, rows, weights, own_parts[n], other_parts[n], earlier, skip, norm_gain[None, :]
        )
        earlier.append(split)
        gated.append(gated_n)
        gated_other.append(swap(gated_n, 1))
        squares.append(squares_n.reshape(1, rows))
    gated = jnp.concatenate(gated)
    gated_other = jnp.concatenate(gated_other)
    squares = jnp.concatenate(squares)
    k = 1
    while k < nmp:
        squares = squares + swap(squares, k)
        k *= 2
    scale = lax.rsqrt(squares / (channels * nmp) + norm_eps).reshape(far, 2, rows // 2, 1)

    width = half // OUT_CHUNKS
    done = []
    for n in range(OUT_CHUNKS):
        keep, send = project_out(
            n, width, spots, gated, gated_other, mixer_out, mixer_other, scale, teacher
        )
        sums = add_near(keep, swap(send, 2))
        done.append(add_far(sums[0], [swap(sums[k], 4 * k) for k in range(1, far)]))
    total = jnp.concatenate(done, axis=1).reshape(2, rows // 4, half)
    stay = at(total, core)
    came = swap(at(total, 1 - core), 1)
    return jnp.concatenate(
        [jnp.where(core == 0, stay, came), jnp.where(core == 0, came, stay)], axis=1
    )


def solution(mesh):
    placed = (
        P("dp", "mp"),
        P("dp", "mp"),
        P("dp", None),
        P("dp", None),
        P("mp", None),
        P(None, "dp", "mp"),
        P("mp", None),
        P("mp"),
        P("mp"),
        P("mp"),
        P("mp"),
        P("mp", None),
    )
    return jax.shard_map(
        functools.partial(local, mesh.shape["dp"], mesh.shape["mp"]),
        mesh=mesh,
        in_specs=placed,
        out_specs=P(("dp", "mp"), None),
        check_vma=False,
    )
```

time: 667 us -> 352 us (0.53)
  waiting for transfers between devices: 530 us -> 124 us
  starting transfers between devices: 0.12 us -> 77.1 us
  Pallas kernels: 0 us -> 72.3 us
  blocking collectives: 33.4 us -> 0 us
  matrix products: 60.5 us -> 32.6 us
  between operations: 13.3 us -> 1.28 us
  local copies, waits for them, and re-layouts: 21.7 us -> 33.1 us
    all_gather x2 -> x0, waiting for transfers between devices: 276 us -> none  [the longest x1 199 us: local(): lax.all_gather(mixer_in, 'dp', axis=1, tiled=True)]
    reduce_scatter x1 -> x0, waiting for transfers between devices: 175 us -> none  [local(): lax.psum_scatter(jnp.dot(normed, mixer_out, preferred_element_type=jnp.fl...]
    ppermute x0 -> x70, waiting for transfers between devices: none -> 124 us  [the longest x62 103 us: swap(): return lax.ppermute(source, 'mp', [(s, s ^ k) for s in range(nmp)])]
    psum x1 -> x0, waiting for transfers between devices: 78.2 us -> none  [local(): lax.psum(jnp.dot(hidden_in, shared_in, preferred_element_type=jnp.float32...]
    ppermute x0 -> x70, starting transfers between devices: none -> 77.1 us  [the longest x62 66.9 us: swap(): return lax.ppermute(source, 'mp', [(s, s ^ k) for s in range(nmp)])]
    pallas_call x0 -> x21, Pallas kernels: none -> 72.3 us  [the longest x4 21 us: project_out(): pl.pallas_call(body, grid_spec=pltpu.PrefetchScalarGridSpec(num_scalar_pr...]
    psum x1 -> x0, blocking collectives: 33.4 us -> none  [local(): sum_squares = lax.psum(jnp.sum(gated * gated, axis=1), 'mp')]
    dot_general x22 -> x10, matrix products: 60.5 us -> 32.6 us  [the longest x1 10.6 us: local(): jnp.dot(swap(context, 1), teacher_other, preferred_element_type=f32)]
  transfers between devices with their start and end apart: 4 -> 70, of which waited for: 4 -> 28; matrix products, arithmetic and copies ran while one was open for 3% -> 19% of each run, Pallas kernels for 0% -> 19%
where the time goes in v1:
time: 352 us; the launch traced here: 351 us
  waiting for transfers between devices  124 us (35%)
  starting transfers between devices  77.1 us (22%)
  Pallas kernels  72.3 us (21%)
  local copies, waits for them, and re-layouts  33.1 us (9%)
  matrix products  32.6 us (9%)
  other arithmetic  10.6 us (3%)
    ppermute x62, waiting for transfers between devices, swap(): return lax.ppermute(source, 'mp', [(s, s ^ k) for s in range(nmp)])  103 us
    ppermute x62, starting transfers between devices, swap(): return lax.ppermute(source, 'mp', [(s, s ^ k) for s in range(nmp)])  66.9 us
    pallas_call x4, Pallas kernels, project_out(): pl.pallas_call(body, grid_spec=pltpu.PrefetchScalarGridSpec(num_scalar_pr...  21 us
    ppermute x8, waiting for transfers between devices, cross(): return lax.ppermute(source, 'dp', [(s, s ^ k) for s in range(ndp)])  20.7 us
    pallas_call x4, Pallas kernels, scan_chunk(): pl.pallas_call(body, out_shape=(jax.ShapeDtypeStruct((pairs, wide, 2 * LA...  12.1 us
    pallas_call x1, Pallas kernels, reorder_weights(): pl.pallas_call(body, grid_spec=pltpu.PrefetchScalarGridSpec(num_scalar_pr...  12 us
    pallas_call x4, Pallas kernels, scan_weights(): pl.pallas_call(body, out_shape=jax.ShapeDtypeStruct((pairs, wide, (n + 1)...  10.9 us
    dot_general x1, matrix products, local(): jnp.dot(swap(context, 1), teacher_other, preferred_element_type=f32)  10.6 us
  transfers between devices with their start and end apart: 70, of which 28 were waited for; matrix products, arithmetic and copies ran while one was open for 19% of the time, Pallas kernels for 19%

profile of v1, /device:TPU:0, one launch (start us, length us, event | category | flops | bytes accessed | tf_op | source)
XLA Modules:
  0.0 351.0 jit_solution(13988445696362358635)
XLA Ops:
  0.0 2.0 slice_bitcast_fusion.4
  2.0 4.0 %collective-permute-start.34 = (bf16[128,512]{1,0:T(8,128)(2,1)}, bf16[128,512]{1,0:T(8,128)(2,1)S(1)}, u32[]{:S(2)}, u32[]{:S(2)}) collective-permute-start(bf16[128,512]{1,0:T(8,128)(2,1)} %get-tuple-element.97), channel_id=1, source_target_pairs={{0,8},{1,9},{2,10},{3,11},{4,12},{5,13},{6,14},{7,15},{8,0},{9,1},... | collective-permute-start | bytes 393224 | tf_op jit(solution)/shard_map/ppermute | solution.py:261
  7.7 2.8 collective-permute-start.26
  12.0 5.0 %constant_dynamic-slice_fusion = bf16[512,4096]{1,0:T(8,128)(2,1)} fusion(bf16[512,8192]{1,0:T(8,128)(2,1)} %param.16, s32[]{:T(128)S(6)} %select_n.219), kind=kLoop, calls=%fused_computation.147 | loop fusion | bytes 8388612 | tf_op jit(solution)/shard_map/dynamic_slice | solution.py:332
  18.1 2.3 constant_dynamic-slice_fusion.1
  21.1 4.0 %fusion.57 = (f32[4,512]{1,0:T(4,128)S(1)}, f32[4,512,512]{1,2,0:T(8,128)}) fusion(f32[512,512,4]{1,0,2:T(8,128)S(1)} %fusion.9, pred[512,512]{0,1:T(8,128)(4,1)S(1)} %iota_compare_fusion), kind=kOutput, calls=%fused_computation.182 | output fusion | flops 6291967 | bytes 8658944 | tf_op jit(solution)/shard_map/sub | solution.py:325
  25.1 2.7 fusion.8
  28.7 8.0 %fusion.1 = f32[512,4096]{1,0:T(8,128)} fusion(bf16[512,512]{0,1:T(8,128)(2,1)S(1)} %bitcast.274, bf16[512,8192]{1,0:T(8,128)(2,1)} %param.16, s32[]{:T(128)S(6)} %select_n.223), kind=kOutput, calls=%fused_computation.3 | convolution fusion | flops 2147483648 | bytes 13107204 | tf_op jit(solution)/shard_map/dot_general | solution.py:337
  38.7 12.0 %reorder_weights.1 = bf16[4096,1024]{1,0:T(8,128)(2,1)} custom-call(s32[1]{0:T(128)} %bitcast.45.spot_ref, bf16[2,4096,512]{2,1,0:T(8,128)(2,1)} %source.1), custom_call_target="tpu_custom_call" | custom-call | bytes 16777216 | tf_op jit(solution)/shard_map/reorder_weights/pallas_call | solution.py:40
  50.7 3.1 collective-permute-start.18
  55.3 3.0 collective-permute-start.10
  59.8 3.9 %collective-permute-done.18 = bf16[128,512]{1,0:T(8,128)(2,1)S(1)} collective-permute-done((bf16[128,512]{1,0:T(8,128)(2,1)S(1)}, bf16[128,512]{1,0:T(8,128)(2,1)S(1)}, u32[]{:S(2)}, u32[]{:S(2)}) %collective-permute-start.18) | collective-permute-done | bytes 131104 | tf_op jit(solution)/shard_map/ppermute | solution.py:261
  66.3 7.4 %collective-permute-done.10 = bf16[128,512]{1,0:T(8,128)(2,1)S(1)} collective-permute-done((bf16[128,512]{1,0:T(8,128)(2,1)S(1)}, bf16[128,512]{1,0:T(8,128)(2,1)S(1)}, u32[]{:S(2)}, u32[]{:S(2)}) %collective-permute-start.10) | collective-permute-done | bytes 131104 | tf_op jit(solution)/shard_map/ppermute | solution.py:261
  76.5 6.8 %collective-permute-done.29 = bf16[2,128,512]{2,1,0:T(8,128)(2,1)S(1)} collective-permute-done((bf16[2,128,512]{2,1,0:T(8,128)(2,1)S(1)}, bf16[2,128,512]{2,1,0:T(8,128)(2,1)S(1)}, u32[]{:S(2)}, u32[]{:S(2)}) %collective-permute-start.29) | collective-permute-done | bytes 262176 | tf_op jit(solution)/shard_map/ppermute | solution.py:264
  85.0 4.0 %collective-permute-done.21 = bf16[2,128,512]{2,1,0:T(8,128)(2,1)S(1)} collective-permute-done((bf16[2,128,512]{2,1,0:T(8,128)(2,1)S(1)}, bf16[2,128,512]{2,1,0:T(8,128)(2,1)S(1)}, u32[]{:S(2)}, u32[]{:S(2)}) %collective-permute-start.21) | collective-permute-done | bytes 262176 | tf_op jit(solution)/shard_map/ppermute | solution.py:264
  89.2 1.6 collective-permute-start.1
  90.8 2.9 collective-permute-done.13
  95.0 3.3 collective-permute-start.2
  100.9 3.1 collective-permute-done.3
  107.5 2.4 collective-permute-start.7
  113.4 1.6 collective-permute-start.8
  115.1 13.5 %collective-permute-done.8 = f32[128,384]{1,0:T(8,128)S(1)} collective-permute-done((f32[128,384]{1,0:T(8,128)S(1)}, f32[128,384]{1,0:T(8,128)S(1)}, u32[]{:S(2)}, u32[]{:S(2)}) %collective-permute-start.8) | collective-permute-done | bytes 196640 | tf_op jit(solution)/shard_map/ppermute | solution.py:261
  128.6 1.6 collective-permute-start.31
  132.1 11.4 %collective-permute-done.31 = bf16[2,2,128,512]{3,2,0,1:T(8,128)(2,1)S(1)} collective-permute-done((bf16[2,2,128,512]{3,2,0,1:T(8,128)(2,1)S(1)}, bf16[2,2,128,512]{3,2,0,1:T(8,128)(2,1)S(1)}, u32[]{:S(2)}, u32[]{:S(2)}) %collective-permute-start.31) | collective-permute-done | bytes 524320 | tf_op jit(solution)/shard_map/ppermute | solution.py:261
  143.6 1.6 collective-permute-start.15
  145.2 9.4 %collective-permute-done.23 = bf16[2,2,128,512]{3,2,0,1:T(8,128)(2,1)S(1)} collective-permute-done((bf16[2,2,128,512]{3,2,0,1:T(8,128)(2,1)S(1)}, bf16[2,2,128,512]{3,2,0,1:T(8,128)(2,1)S(1)}, u32[]{:S(2)}, u32[]{:S(2)}) %collective-permute-start.23) | collective-permute-done | bytes 524320 | tf_op jit(solution)/shard_map/ppermute | solution.py:261
  155.4 10.1 %collective-permute-done.15 = bf16[2,2,128,512]{3,2,0,1:T(8,128)(2,1)S(1)} collective-permute-done((bf16[2,2,128,512]{3,2,0,1:T(8,128)(2,1)S(1)}, bf16[2,2,128,512]{3,2,0,1:T(8,128)(2,1)S(1)}, u32[]{:S(2)}, u32[]{:S(2)}) %collective-permute-start.15) | collective-permute-done | bytes 524320 | tf_op jit(solution)/shard_map/ppermute | solution.py:261
  170.3 2.4 fusion.62
  175.1 2.4 fusion.61
  179.0 2.4 fusion.59
  183.2 2.6 fusion.60
  186.6 6.9 %collective-permute-done.17.refs_4_ = bf16[128,1024]{1,0:T(8,128)(2,1)S(1)} collective-permute-done((bf16[128,1024]{1,0:T(8,128)(2,1)S(1)}, bf16[128,1024]{1,0:T(8,128)(2,1)S(1)}, u32[]{:S(2)}, u32[]{:S(2)}) %collective-permute-start.17) | collective-permute-done | bytes 262176 | tf_op jit(solution)/shard_map/ppermute | solution.py:264
  202.0 2.0 scan_weights.4.refs_0_
  204.1 2.5 scan_weights.5.refs_0_
  206.6 2.9 scan_weights.6.refs_0_
  210.2 3.4 scan_weights.7.refs_0_
  217.1 2.3 scan_chunk.4
  219.5 2.8 scan_chunk.5
  222.3 3.2 scan_chunk.6
  225.5 3.8 %scan_chunk.7 = (bf16[4,256,256]{2,1,0:T(8,128)(2,1)}, bf16[128,512]{1,0:T(8,128)(2,1)}, f32[128,1]{1,0:T(8,128)}) custom-call(bf16[4,256,1024]{2,1,0:T(8,128)(2,1)} %scan_weights.7.refs_0_, f32[128,1024]{1,0:T(8,128)} %slice.338.refs_1_, f32[1,512]{1,0:T(1,128)} %broadcast_in_dim_reshape.3.refs_2_, f32[1,512]{1,0:T(1,128)} %bitcast.314, ...), custom_call_target="tpu_custom_call" | custom-call | flops 536870912 | bytes 1048576 | tf_op jit(solution)/shard_map/scan_chunk/pallas_call | solution.py:141
  233.6 2.1 collective-permute-done.48
  236.1 3.2 collective-permute-done.49
  240.6 3.2 collective-permute-done.50
  247.0 10.6 %convolution_add_fusion = f32[512,4096]{1,0:T(8,128)} fusion(f32[512,4096]{1,0:T(8,128)} %fusion.1, bf16[512,512]{0,1:T(8,128)(2,1)S(1)} %collective-permute-done.51, bf16[512,4096]{1,0:T(8,128)(2,1)} %collective-permute-done.52), kind=kOutput, calls=%fused_computation.1 | convolution fusion | flops 2149580800 | bytes 21495808 | tf_op jit(solution)/shard_map/dot_general | solution.py:337
  257.6 5.2 %project_out.4 = (f32[4,64,1024]{2,1,0:T(8,128)}, bf16[4,64,1024]{2,1,0:T(8,128)(2,1)}) custom-call(s32[3]{0:T(128)} %pad_add_fusion.spot_ref, bf16[512,512]{1,0:T(8,128)(2,1)} %copy-done.4, bf16[512,512]{1,0:T(8,128)(2,1)} %copy-done.3, bf16[512,8192]{1,0:T(8,128)(2,1)} %w_ref.7, bf16[512,4096]{1,0:T(8,128)(2,1)} %collective-permute-done.46.wo_ref, ...), custom_call_target="tpu_custom_call" | custom-call | flops 1073741824 | bytes 7340032 | tf_op jit(solution)/shard_map/project_out/pallas_call | solution.py:174
  264.3 5.2 %project_out.5 = (f32[4,64,1024]{2,1,0:T(8,128)}, bf16[4,64,1024]{2,1,0:T(8,128)(2,1)}) custom-call(s32[3]{0:T(128)} %pad_add_fusion.spot_ref, bf16[512,512]{1,0:T(8,128)(2,1)} %copy-done.4, bf16[512,512]{1,0:T(8,128)(2,1)} %copy-done.3, bf16[512,8192]{1,0:T(8,128)(2,1)} %w_ref.7, bf16[512,4096]{1,0:T(8,128)(2,1)} %collective-permute-done.46.wo_ref, ...), custom_call_target="tpu_custom_call" | custom-call | flops 1073741824 | bytes 7340032 | tf_op jit(solution)/shard_map/project_out/pallas_call | solution.py:174
  270.0 5.2 %project_out.6 = (f32[4,64,1024]{2,1,0:T(8,128)}, bf16[4,64,1024]{2,1,0:T(8,128)(2,1)}) custom-call(s32[3]{0:T(128)} %pad_add_fusion.spot_ref, bf16[512,512]{1,0:T(8,128)(2,1)} %copy-done.4, bf16[512,512]{1,0:T(8,128)(2,1)} %copy-done.3, bf16[512,8192]{1,0:T(8,128)(2,1)} %w_ref.7, bf16[512,4096]{1,0:T(8,128)(2,1)} %collective-permute-done.46.wo_ref, ...), custom_call_target="tpu_custom_call" | custom-call | flops 1073741824 | bytes 7340032 | tf_op jit(solution)/shard_map/project_out/pallas_call | solution.py:174
  276.7 5.5 %project_out.7 = (f32[4,64,1024]{2,1,0:T(8,128)}, bf16[4,64,1024]{2,1,0:T(8,128)(2,1)}) custom-call(s32[3]{0:T(128)} %pad_add_fusion.spot_ref, bf16[512,512]{1,0:T(8,128)(2,1)} %copy-done.4, bf16[512,512]{1,0:T(8,128)(2,1)} %copy-done.3, bf16[512,8192]{1,0:T(8,128)(2,1)} %w_ref.7, bf16[512,4096]{1,0:T(8,128)(2,1)} %collective-permute-done.46.wo_ref, ...), custom_call_target="tpu_custom_call" | custom-call | flops 1073741824 | bytes 7340032 | tf_op jit(solution)/shard_map/project_out/pallas_call | solution.py:174
  283.5 2.3 add_near.4
  290.3 2.2 add_near.5
  292.6 7.6 %collective-permute-done.61.came_ref = bf16[4,64,1024]{2,1,0:T(8,128)(2,1)S(1)} collective-permute-done((bf16[4,64,1024]{2,1,0:T(8,128)(2,1)}, bf16[4,64,1024]{2,1,0:T(8,128)(2,1)S(1)}, u32[]{:S(2)}, u32[]{:S(2)}) %collective-permute-start.61) | collective-permute-done | bytes 524320 | tf_op jit(solution)/shard_map/ppermute | solution.py:261
  301.0 2.2 add_near.6
  303.2 7.7 %collective-permute-done.65.came_ref = bf16[4,64,1024]{2,1,0:T(8,128)(2,1)S(1)} collective-permute-done((bf16[4,64,1024]{2,1,0:T(8,128)(2,1)}, bf16[4,64,1024]{2,1,0:T(8,128)(2,1)S(1)}, u32[]{:S(2)}, u32[]{:S(2)}) %collective-permute-start.65) | collective-permute-done | bytes 524320 | tf_op jit(solution)/shard_map/ppermute | solution.py:261
  311.2 2.4 collective-permute-start.60
  314.3 2.2 add_near.7
  317.9 2.4 collective-permute-start.64
  320.2 6.3 %collective-permute-done.59.refs_1_ = bf16[64,1024]{1,0:T(8,128)(2,1)S(1)} collective-permute-done((bf16[64,1024]{1,0:T(8,128)(2,1)}, bf16[64,1024]{1,0:T(8,128)(2,1)S(1)}, u32[]{:S(2)}, u32[]{:S(2)}) %collective-permute-start.59) | collective-permute-done | bytes 131104 | tf_op jit(solution)/shard_map/ppermute | solution.py:261
  326.6 4.8 %collective-permute-start.67 = (bf16[64,1024]{1,0:T(8,128)(2,1)}, bf16[64,1024]{1,0:T(8,128)(2,1)S(1)}, u32[]{:S(2)}, u32[]{:S(2)}) collective-permute-start(bf16[64,1024]{1,0:T(8,128)(2,1)} %get-tuple-element.73), channel_id=1, source_target_pairs={{0,8},{1,9},{2,10},{3,11},{4,12},{5,13},{6,14},{7,15},{8,0},{9,1},... | collective-permute-start | bytes 393224 | tf_op jit(solution)/shard_map/ppermute | solution.py:261
  331.4 2.4 collective-permute-start.68
  333.8 1.8 add_far.4
  335.6 1.9 add_far.5
  338.2 1.8 add_far.6
  340.0 4.9 %collective-permute-done.67.refs_1_ = bf16[64,1024]{1,0:T(8,128)(2,1)S(1)} collective-permute-done((bf16[64,1024]{1,0:T(8,128)(2,1)}, bf16[64,1024]{1,0:T(8,128)(2,1)S(1)}, u32[]{:S(2)}, u32[]{:S(2)}) %collective-permute-start.67) | collective-permute-done | bytes 131104 | tf_op jit(solution)/shard_map/ppermute | solution.py:261
  345.6 1.8 add_far.7
  (339 shorter events, 81.7 us)
Async XLA Ops:
  2.0 35.2 %collective-permute-start.34 = (bf16[128,512]{1,0:T(8,128)(2,1)}, bf16[128,512]{1,0:T(8,128)(2,1)S(1)}, u32[]{:S(2)}, u32[]{:S(2)}) collective-permute-start(bf16[128,512]{1,0:T(8,128)(2,1)} %get-tuple-element.97), channel_id=1, source_target_pairs={{0,8},{1,9},{2,10},{3,11},{4,12},{5,13},{6,14},{7,15},{8,0},{9,1},... | collective-permute-start | bytes 393224 | tf_op jit(solution)/shard_map/ppermute | solution.py:261
  6.1 44.6 %collective-permute-start.35 = (bf16[128,512]{1,0:T(8,128)(2,1)}, bf16[128,512]{1,0:T(8,128)(2,1)S(1)}, u32[]{:S(2)}, u32[]{:S(2)}) collective-permute-start(bf16[128,512]{1,0:T(8,128)(2,1)} %get-tuple-element.97), channel_id=1, source_target_pairs={{0,12},{1,13},{2,14},{3,15},{4,8},{5,9},{6,10},{7,11},{8,4},{9,5},... | collective-permute-start | bytes 393224 | tf_op jit(solution)/shard_map/ppermute | solution.py:261
  7.4 46.4 %collective-permute-start.36 = (bf16[128,512]{1,0:T(8,128)(2,1)}, bf16[128,512]{1,0:T(8,128)(2,1)S(1)}, u32[]{:S(2)}, u32[]{:S(2)}) collective-permute-start(bf16[128,512]{1,0:T(8,128)(2,1)} %get-tuple-element.97), channel_id=1, source_target_pairs={{0,4},{1,5},{2,6},{3,7},{4,0},{5,1},{6,2},{7,3},{8,12},{9,13},{10,... | collective-permute-start | bytes 393224 | tf_op jit(solution)/shard_map/ppermute | solution.py:261
  7.7 47.5 %collective-permute-start.26 = (bf16[128,512]{1,0:T(8,128)(2,1)}, bf16[128,512]{1,0:T(8,128)(2,1)S(1)}, u32[]{:S(2)}, u32[]{:S(2)}) collective-permute-start(bf16[128,512]{1,0:T(8,128)(2,1)} %get-tuple-element.98), channel_id=1, source_target_pairs={{0,8},{1,9},{2,10},{3,11},{4,12},{5,13},{6,14},{7,15},{8,0},{9,1},... | collective-permute-start | bytes 393224 | tf_op jit(solution)/shard_map/ppermute | solution.py:261
  10.5 44.8 %collective-permute-start.27 = (bf16[128,512]{1,0:T(8,128)(2,1)}, bf16[128,512]{1,0:T(8,128)(2,1)S(1)}, u32[]{:S(2)}, u32[]{:S(2)}) collective-permute-start(bf16[128,512]{1,0:T(8,128)(2,1)} %get-tuple-element.98), channel_id=1, source_target_pairs={{0,12},{1,13},{2,14},{3,15},{4,8},{5,9},{6,10},{7,11},{8,4},{9,5},... | collective-permute-start | bytes 393224 | tf_op jit(solution)/shard_map/ppermute | solution.py:261
  37.2 21.1 %collective-permute-start.28 = (bf16[128,512]{1,0:T(8,128)(2,1)}, bf16[128,512]{1,0:T(8,128)(2,1)S(1)}, u32[]{:S(2)}, u32[]{:S(2)}) collective-permute-start(bf16[128,512]{1,0:T(8,128)(2,1)} %get-tuple-element.98), channel_id=1, source_target_pairs={{0,4},{1,5},{2,6},{3,7},{4,0},{5,1},{6,2},{7,3},{8,12},{9,13},{10,... | collective-permute-start | bytes 393224 | tf_op jit(solution)/shard_map/ppermute | solution.py:261
  50.7 13.0 %collective-permute-start.18 = (bf16[128,512]{1,0:T(8,128)(2,1)S(1)}, bf16[128,512]{1,0:T(8,128)(2,1)S(1)}, u32[]{:S(2)}, u32[]{:S(2)}) collective-permute-start(bf16[128,512]{1,0:T(8,128)(2,1)S(1)} %copy-done.22), channel_id=1, source_target_pairs={{0,8},{1,9},{2,10},{3,11},{4,12},{5,13},{6,14},{7,15},{8,0},{9,1},... | collective-permute-start | bytes 393224 | tf_op jit(solution)/shard_map/ppermute | solution.py:261
  53.8 10.8 %collective-permute-start.19 = (bf16[128,512]{1,0:T(8,128)(2,1)S(1)}, bf16[128,512]{1,0:T(8,128)(2,1)S(1)}, u32[]{:S(2)}, u32[]{:S(2)}) collective-permute-start(bf16[128,512]{1,0:T(8,128)(2,1)S(1)} %copy-done.22), channel_id=1, source_target_pairs={{0,12},{1,13},{2,14},{3,15},{4,8},{5,9},{6,10},{7,11},{8,4},{9,5},... | collective-permute-start | bytes 393224 | tf_op jit(solution)/shard_map/ppermute | solution.py:261
  55.2 9.4 %collective-permute-start.20 = (bf16[128,512]{1,0:T(8,128)(2,1)S(1)}, bf16[128,512]{1,0:T(8,128)(2,1)S(1)}, u32[]{:S(2)}, u32[]{:S(2)}) collective-permute-start(bf16[128,512]{1,0:T(8,128)(2,1)S(1)} %copy-done.22), channel_id=1, source_target_pairs={{0,4},{1,5},{2,6},{3,7},{4,0},{5,1},{6,2},{7,3},{8,12},{9,13},{10,... | collective-permute-start | bytes 393224 | tf_op jit(solution)/shard_map/ppermute | solution.py:261
  55.3 18.4 %collective-permute-start.10 = (bf16[128,512]{1,0:T(8,128)(2,1)S(1)}, bf16[128,512]{1,0:T(8,128)(2,1)S(1)}, u32[]{:S(2)}, u32[]{:S(2)}) collective-permute-start(bf16[128,512]{1,0:T(8,128)(2,1)S(1)} %copy-done.21), channel_id=1, source_target_pairs={{0,8},{1,9},{2,10},{3,11},{4,12},{5,13},{6,14},{7,15},{8,0},{9,1},... | collective-permute-start | bytes 393224 | tf_op jit(solution)/shard_map/ppermute | solution.py:261
  58.3 15.4 %collective-permute-start.11 = (bf16[128,512]{1,0:T(8,128)(2,1)S(1)}, bf16[128,512]{1,0:T(8,128)(2,1)S(1)}, u32[]{:S(2)}, u32[]{:S(2)}) collective-permute-start(bf16[128,512]{1,0:T(8,128)(2,1)S(1)} %copy-done.21), channel_id=1, source_target_pairs={{0,12},{1,13},{2,14},{3,15},{4,8},{5,9},{6,10},{7,11},{8,4},{9,5},... | collective-permute-start | bytes 393224 | tf_op jit(solution)/shard_map/ppermute | solution.py:261
  63.7 10.5 %collective-permute-start.12 = (bf16[128,512]{1,0:T(8,128)(2,1)S(1)}, bf16[128,512]{1,0:T(8,128)(2,1)S(1)}, u32[]{:S(2)}, u32[]{:S(2)}) collective-permute-start(bf16[128,512]{1,0:T(8,128)(2,1)S(1)} %copy-done.21), channel_id=1, source_target_pairs={{0,4},{1,5},{2,6},{3,7},{4,0},{5,1},{6,2},{7,3},{8,12},{9,13},{10,... | collective-permute-start | bytes 393224 | tf_op jit(solution)/shard_map/ppermute | solution.py:261
  64.6 24.5 %collective-permute-start = (f32[256,384]{1,0:T(8,128)S(1)}, f32[256,384]{1,0:T(8,128)S(1)}, u32[]{:S(2)}, u32[]{:S(2)}) collective-permute-start(f32[256,384]{1,0:T(8,128)S(1)} %dynamic-slice_bitcast_fusion), channel_id=1, source_target_pairs={{0,1},{1,0},{2,3},{3,2},{4,5},{5,4},{6,7},{7,6},{8,9},{9,8},{10,11... | collective-permute-start | bytes 1179656 | tf_op jit(solution)/shard_map/ppermute | solution.py:261
  64.6 11.2 %collective-permute-start.37 = (bf16[2,128,512]{2,1,0:T(8,128)(2,1)S(1)}, bf16[2,128,512]{2,1,0:T(8,128)(2,1)S(1)}, u32[]{:S(2)}, u32[]{:S(2)}) collective-permute-start(bf16[2,128,512]{2,1,0:T(8,128)(2,1)S(1)} %maximum_select_fusion.4), channel_id=1, source_target_pairs={{0,16},{16,0},{1,17},{17,1},{2,18},{18,2},{3,19},{19,3},{4,20},{20... | collective-permute-start | bytes 786440 | tf_op jit(solution)/shard_map/ppermute | solution.py:264
  73.7 173.3 %collective-permute-start.52 = (bf16[512,4096]{1,0:T(8,128)(2,1)}, bf16[512,4096]{1,0:T(8,128)(2,1)}, u32[]{:S(2)}, u32[]{:S(2)}) collective-permute-start(bf16[512,4096]{1,0:T(8,128)(2,1)} %constant_dynamic-slice_fusion), channel_id=1, source_target_pairs={{0,1},{1,0},{2,3},{3,2},{4,5},{5,4},{6,7},{7,6},{8,9},{9,8},{10,11... | collective-permute-start | bytes 12582920 | tf_op jit(solution)/shard_map/ppermute | solution.py:261
  73.7 183.9 %collective-permute-start.46 = (bf16[512,4096]{1,0:T(8,128)(2,1)}, bf16[512,4096]{1,0:T(8,128)(2,1)}, u32[]{:S(2)}, u32[]{:S(2)}) collective-permute-start(bf16[512,4096]{1,0:T(8,128)(2,1)} %constant_dynamic-slice_fusion.1), channel_id=1, source_target_pairs={{0,1},{1,0},{2,3},{3,2},{4,5},{5,4},{6,7},{7,6},{8,9},{9,8},{10,11... | collective-permute-start | bytes 12582920 | tf_op jit(solution)/shard_map/ppermute | solution.py:261
  74.2 9.2 %collective-permute-start.29 = (bf16[2,128,512]{2,1,0:T(8,128)(2,1)S(1)}, bf16[2,128,512]{2,1,0:T(8,128)(2,1)S(1)}, u32[]{:S(2)}, u32[]{:S(2)}) collective-permute-start(bf16[2,128,512]{2,1,0:T(8,128)(2,1)S(1)} %maximum_select_fusion.3), channel_id=1, source_target_pairs={{0,16},{16,0},{1,17},{17,1},{2,18},{18,2},{3,19},{19,3},{4,20},{20... | collective-permute-start | bytes 786440 | tf_op jit(solution)/shard_map/ppermute | solution.py:264
  75.8 13.2 %collective-permute-start.21 = (bf16[2,128,512]{2,1,0:T(8,128)(2,1)S(1)}, bf16[2,128,512]{2,1,0:T(8,128)(2,1)S(1)}, u32[]{:S(2)}, u32[]{:S(2)}) collective-permute-start(bf16[2,128,512]{2,1,0:T(8,128)(2,1)S(1)} %maximum_select_fusion.2), channel_id=1, source_target_pairs={{0,16},{16,0},{1,17},{17,1},{2,18},{18,2},{3,19},{19,3},{4,20},{20... | collective-permute-start | bytes 786440 | tf_op jit(solution)/shard_map/ppermute | solution.py:264
  83.4 10.4 %collective-permute-start.13 = (bf16[2,128,512]{2,1,0:T(8,128)(2,1)S(1)}, bf16[2,128,512]{2,1,0:T(8,128)(2,1)S(1)}, u32[]{:S(2)}, u32[]{:S(2)}) collective-permute-start(bf16[2,128,512]{2,1,0:T(8,128)(2,1)S(1)} %maximum_select_fusion), channel_id=1, source_target_pairs={{0,16},{16,0},{1,17},{17,1},{2,18},{18,2},{3,19},{19,3},{4,20},{20... | collective-permute-start | bytes 786440 | tf_op jit(solution)/shard_map/ppermute | solution.py:264
  89.2 5.7 %collective-permute-start.1 = (f32[128,384]{1,0:T(8,128)S(1)}, f32[128,384]{1,0:T(8,128)S(1)}, u32[]{:S(2)}, u32[]{:S(2)}) collective-permute-start(f32[128,384]{1,0:T(8,128)S(1)} %dynamic-slice_bitcast_fusion.2), channel_id=1, source_target_pairs={{0,2},{1,3},{2,0},{3,1},{4,6},{5,7},{6,4},{7,5},{8,10},{9,11},{10,... | collective-permute-start | bytes 589832 | tf_op jit(solution)/shard_map/ppermute | solution.py:261
  95.0 5.9 %collective-permute-start.2 = (f32[32,384]{1,0:T(8,128)S(1)}, f32[32,384]{1,0:T(8,128)S(1)}, u32[]{:S(2)}, u32[]{:S(2)}) collective-permute-start(f32[32,384]{1,0:T(8,128)S(1)} %get-tuple-element.134), channel_id=1, source_target_pairs={{0,4},{1,5},{2,6},{3,7},{4,0},{5,1},{6,2},{7,3},{8,12},{9,13},{10,... | collective-permute-start | bytes 147464 | tf_op jit(solution)/shard_map/ppermute | solution.py:261
  98.3 5.6 %collective-permute-start.3 = (f32[32,384]{1,0:T(8,128)S(1)}, f32[32,384]{1,0:T(8,128)S(1)}, u32[]{:S(2)}, u32[]{:S(2)}) collective-permute-start(f32[32,384]{1,0:T(8,128)S(1)} %get-tuple-element.136), channel_id=1, source_target_pairs={{0,8},{1,9},{2,10},{3,11},{4,12},{5,13},{6,14},{7,15},{8,0},{9,1},... | collective-permute-start | bytes 147464 | tf_op jit(solution)/shard_map/ppermute | solution.py:261
  99.4 6.0 %collective-permute-start.4 = (f32[32,384]{1,0:T(8,128)S(1)}, f32[32,384]{1,0:T(8,128)S(1)}, u32[]{:S(2)}, u32[]{:S(2)}) collective-permute-start(f32[32,384]{1,0:T(8,128)S(1)} %get-tuple-element.135), channel_id=1, source_target_pairs={{0,12},{1,13},{2,14},{3,15},{4,8},{5,9},{6,10},{7,11},{8,4},{9,5},... | collective-permute-start | bytes 147464 | tf_op jit(solution)/shard_map/ppermute | solution.py:261
  105.4 4.5 %collective-permute-start.5 = (f32[32,384]{1,0:T(8,128)S(1)}, f32[32,384]{1,0:T(8,128)S(1)}, u32[]{:S(2)}, u32[]{:S(2)}) collective-permute-start(f32[32,384]{1,0:T(8,128)S(1)} %fusion.35), channel_id=1, source_target_pairs={{0,4},{1,5},{2,6},{3,7},{4,0},{5,1},{6,2},{7,3},{8,12},{9,13},{10,... | collective-permute-start | bytes 147464 | tf_op jit(solution)/shard_map/ppermute | solution.py:261
  106.1 5.0 %collective-permute-start.6 = (f32[32,384]{1,0:T(8,128)S(1)}, f32[32,384]{1,0:T(8,128)S(1)}, u32[]{:S(2)}, u32[]{:S(2)}) collective-permute-start(f32[32,384]{1,0:T(8,128)S(1)} %fusion.35), channel_id=1, source_target_pairs={{0,8},{1,9},{2,10},{3,11},{4,12},{5,13},{6,14},{7,15},{8,0},{9,1},... | collective-permute-start | bytes 147464 | tf_op jit(solution)/shard_map/ppermute | solution.py:261
  107.5 5.9 %collective-permute-start.7 = (f32[32,384]{1,0:T(8,128)S(1)}, f32[32,384]{1,0:T(8,128)S(1)}, u32[]{:S(2)}, u32[]{:S(2)}) collective-permute-start(f32[32,384]{1,0:T(8,128)S(1)} %fusion.35), channel_id=1, source_target_pairs={{0,12},{1,13},{2,14},{3,15},{4,8},{5,9},{6,10},{7,11},{8,4},{9,5},... | collective-permute-start | bytes 147464 | tf_op jit(solution)/shard_map/ppermute | solution.py:261
  109.9 18.7 %collective-permute-start.38 = (bf16[2,2,128,512]{3,2,0,1:T(8,128)(2,1)S(1)}, bf16[2,2,128,512]{3,2,0,1:T(8,128)(2,1)S(1)}, u32[]{:S(2)}, u32[]{:S(2)}) collective-permute-start(bf16[2,2,128,512]{3,2,0,1:T(8,128)(2,1)S(1)} %pad_maximum_fusion.3), channel_id=1, source_target_pairs={{0,1},{1,0},{2,3},{3,2},{4,5},{5,4},{6,7},{7,6},{8,9},{9,8},{10,11... | collective-permute-start | bytes 1572872 | tf_op jit(solution)/shard_map/ppermute | solution.py:261
  111.1 19.2 %collective-permute-start.39 = (bf16[2,2,128,512]{3,2,0,1:T(8,128)(2,1)S(1)}, bf16[2,2,128,512]{3,2,0,1:T(8,128)(2,1)S(1)}, u32[]{:S(2)}, u32[]{:S(2)}) collective-permute-start(bf16[2,2,128,512]{3,2,0,1:T(8,128)(2,1)S(1)} %pad_maximum_fusion.3), channel_id=1, source_target_pairs={{0,2},{1,3},{2,0},{3,1},{4,6},{5,7},{6,4},{7,5},{8,10},{9,11},{10,... | collective-permute-start | bytes 1572872 | tf_op jit(solution)/shard_map/ppermute | solution.py:261
  113.4 15.1 %collective-permute-start.8 = (f32[128,384]{1,0:T(8,128)S(1)}, f32[128,384]{1,0:T(8,128)S(1)}, u32[]{:S(2)}, u32[]{:S(2)}) collective-permute-start(f32[128,384]{1,0:T(8,128)S(1)} %pad_maximum_fusion.9), channel_id=1, source_target_pairs={{0,2},{1,3},{2,0},{3,1},{4,6},{5,7},{6,4},{7,5},{8,10},{9,11},{10,... | collective-permute-start | bytes 589832 | tf_op jit(solution)/shard_map/ppermute | solution.py:261
  128.6 14.8 %collective-permute-start.31 = (bf16[2,2,128,512]{3,2,0,1:T(8,128)(2,1)S(1)}, bf16[2,2,128,512]{3,2,0,1:T(8,128)(2,1)S(1)}, u32[]{:S(2)}, u32[]{:S(2)}) collective-permute-start(bf16[2,2,128,512]{3,2,0,1:T(8,128)(2,1)S(1)} %pad_maximum_fusion.2), channel_id=1, source_target_pairs={{0,2},{1,3},{2,0},{3,1},{4,6},{5,7},{6,4},{7,5},{8,10},{9,11},{10,... | collective-permute-start | bytes 1572872 | tf_op jit(solution)/shard_map/ppermute | solution.py:261
  130.3 13.3 %collective-permute-start.22 = (bf16[2,2,128,512]{3,2,0,1:T(8,128)(2,1)S(1)}, bf16[2,2,128,512]{3,2,0,1:T(8,128)(2,1)S(1)}, u32[]{:S(2)}, u32[]{:S(2)}) collective-permute-start(bf16[2,2,128,512]{3,2,0,1:T(8,128)(2,1)S(1)} %pad_maximum_fusion.1), channel_id=1, source_target_pairs={{0,1},{1,0},{2,3},{3,2},{4,5},{5,4},{6,7},{7,6},{8,9},{9,8},{10,11... | collective-permute-start | bytes 1572872 | tf_op jit(solution)/shard_map/ppermute | solution.py:261
  130.6 24.0 %collective-permute-start.23 = (bf16[2,2,128,512]{3,2,0,1:T(8,128)(2,1)S(1)}, bf16[2,2,128,512]{3,2,0,1:T(8,128)(2,1)S(1)}, u32[]{:S(2)}, u32[]{:S(2)}) collective-permute-start(bf16[2,2,128,512]{3,2,0,1:T(8,128)(2,1)S(1)} %pad_maximum_fusion.1), channel_id=1, source_target_pairs={{0,2},{1,3},{2,0},{3,1},{4,6},{5,7},{6,4},{7,5},{8,10},{9,11},{10,... | collective-permute-start | bytes 1572872 | tf_op jit(solution)/shard_map/ppermute | solution.py:261
  143.4 11.3 %collective-permute-start.14 = (bf16[2,2,128,512]{3,2,0,1:T(8,128)(2,1)S(1)}, bf16[2,2,128,512]{3,2,0,1:T(8,128)(2,1)S(1)}, u32[]{:S(2)}, u32[]{:S(2)}) collective-permute-start(bf16[2,2,128,512]{3,2,0,1:T(8,128)(2,1)S(1)} %pad_maximum_fusion), channel_id=1, source_target_pairs={{0,1},{1,0},{2,3},{3,2},{4,5},{5,4},{6,7},{7,6},{8,9},{9,8},{10,11... | collective-permute-start | bytes 1572872 | tf_op jit(solution)/shard_map/ppermute | solution.py:261
  143.6 22.0 %collective-permute-start.15 = (bf16[2,2,128,512]{3,2,0,1:T(8,128)(2,1)S(1)}, bf16[2,2,128,512]{3,2,0,1:T(8,128)(2,1)S(1)}, u32[]{:S(2)}, u32[]{:S(2)}) collective-permute-start(bf16[2,2,128,512]{3,2,0,1:T(8,128)(2,1)S(1)} %pad_maximum_fusion), channel_id=1, source_target_pairs={{0,2},{1,3},{2,0},{3,1},{4,6},{5,7},{6,4},{7,5},{8,10},{9,11},{10,... | collective-permute-start | bytes 1572872 | tf_op jit(solution)/shard_map/ppermute | solution.py:261
  154.7 10.9 %collective-permute-start.9 = (f32[256,384]{1,0:T(8,128)S(1)}, f32[256,384]{1,0:T(8,128)S(1)}, u32[]{:S(2)}, u32[]{:S(2)}) collective-permute-start(f32[256,384]{1,0:T(8,128)S(1)} %pad_maximum_fusion.6), channel_id=1, source_target_pairs={{0,1},{1,0},{2,3},{3,2},{4,5},{5,4},{6,7},{7,6},{8,9},{9,8},{10,11... | collective-permute-start | bytes 1179656 | tf_op jit(solution)/shard_map/ppermute | solution.py:261
  154.9 15.1 %collective-permute-start.40 = (bf16[2,2,128,512]{3,2,0,1:T(8,128)(2,1)S(1)}, bf16[2,2,128,512]{3,2,0,1:T(8,128)(2,1)S(1)}, u32[]{:S(2)}, u32[]{:S(2)}) collective-permute-start(bf16[2,2,128,512]{3,2,0,1:T(8,128)(2,1)S(1)} %collective-permute-done.39), channel_id=1, source_target_pairs={{0,1},{1,0},{2,3},{3,2},{4,5},{5,4},{6,7},{7,6},{8,9},{9,8},{10,11... | collective-permute-start | bytes 1572872 | tf_op jit(solution)/shard_map/ppermute | solution.py:261
  165.5 7.9 %collective-permute-start.32 = (bf16[2,2,128,512]{3,2,0,1:T(8,128)(2,1)S(1)}, bf16[2,2,128,512]{3,2,0,1:T(8,128)(2,1)S(1)}, u32[]{:S(2)}, u32[]{:S(2)}) collective-permute-start(bf16[2,2,128,512]{3,2,0,1:T(8,128)(2,1)S(1)} %collective-permute-done.31), channel_id=1, source_target_pairs={{0,1},{1,0},{2,3},{3,2},{4,5},{5,4},{6,7},{7,6},{8,9},{9,8},{10,11... | collective-permute-start | bytes 1572872 | tf_op jit(solution)/shard_map/ppermute | solution.py:261
  165.6 15.8 %collective-permute-start.24 = (bf16[2,2,128,512]{3,2,0,1:T(8,128)(2,1)S(1)}, bf16[2,2,128,512]{3,2,0,1:T(8,128)(2,1)S(1)}, u32[]{:S(2)}, u32[]{:S(2)}) collective-permute-start(bf16[2,2,128,512]{3,2,0,1:T(8,128)(2,1)S(1)} %collective-permute-done.23), channel_id=1, source_target_pairs={{0,1},{1,0},{2,3},{3,2},{4,5},{5,4},{6,7},{7,6},{8,9},{9,8},{10,11... | collective-permute-start | bytes 1572872 | tf_op jit(solution)/shard_map/ppermute | solution.py:261
  170.0 8.2 %collective-permute-start.16 = (bf16[2,2,128,512]{3,2,0,1:T(8,128)(2,1)S(1)}, bf16[2,2,128,512]{3,2,0,1:T(8,128)(2,1)S(1)}, u32[]{:S(2)}, u32[]{:S(2)}) collective-permute-start(bf16[2,2,128,512]{3,2,0,1:T(8,128)(2,1)S(1)} %collective-permute-done.15), channel_id=1, source_target_pairs={{0,1},{1,0},{2,3},{3,2},{4,5},{5,4},{6,7},{7,6},{8,9},{9,8},{10,11... | collective-permute-start | bytes 1572872 | tf_op jit(solution)/shard_map/ppermute | solution.py:261
  173.4 52.1 %collective-permute-start.41 = (bf16[128,1024]{1,0:T(8,128)(2,1)}, bf16[128,1024]{1,0:T(8,128)(2,1)}, u32[]{:S(2)}, u32[]{:S(2)}) collective-permute-start(bf16[128,1024]{1,0:T(8,128)(2,1)} %slice.410), channel_id=1, source_target_pairs={{0,16},{16,0},{1,17},{17,1},{2,18},{18,2},{3,19},{19,3},{4,20},{20... | collective-permute-start | bytes 786440 | tf_op jit(solution)/shard_map/ppermute | solution.py:264
  178.2 44.0 %collective-permute-start.33 = (bf16[128,1024]{1,0:T(8,128)(2,1)}, bf16[128,1024]{1,0:T(8,128)(2,1)}, u32[]{:S(2)}, u32[]{:S(2)}) collective-permute-start(bf16[128,1024]{1,0:T(8,128)(2,1)} %slice.411), channel_id=1, source_target_pairs={{0,16},{16,0},{1,17},{17,1},{2,18},{18,2},{3,19},{19,3},{4,20},{20... | collective-permute-start | bytes 786440 | tf_op jit(solution)/shard_map/ppermute | solution.py:264
  181.5 12.1 %collective-permute-start.17 = (bf16[128,1024]{1,0:T(8,128)(2,1)S(1)}, bf16[128,1024]{1,0:T(8,128)(2,1)S(1)}, u32[]{:S(2)}, u32[]{:S(2)}) collective-permute-start(bf16[128,1024]{1,0:T(8,128)(2,1)S(1)} %slice.413), channel_id=1, source_target_pairs={{0,16},{16,0},{1,17},{17,1},{2,18},{18,2},{3,19},{19,3},{4,20},{20... | collective-permute-start | bytes 786440 | tf_op jit(solution)/shard_map/ppermute | solution.py:264
  193.5 25.9 %collective-permute-start.25 = (bf16[128,1024]{1,0:T(8,128)(2,1)}, bf16[128,1024]{1,0:T(8,128)(2,1)}, u32[]{:S(2)}, u32[]{:S(2)}) collective-permute-start(bf16[128,1024]{1,0:T(8,128)(2,1)} %slice.412), channel_id=1, source_target_pairs={{0,16},{16,0},{1,17},{17,1},{2,18},{18,2},{3,19},{19,3},{4,20},{20... | collective-permute-start | bytes 786440 | tf_op jit(solution)/shard_map/ppermute | solution.py:264
  219.4 27.6 %collective-permute-start.51 = (bf16[512,512]{0,1:T(8,128)(2,1)S(1)}, bf16[512,512]{0,1:T(8,128)(2,1)S(1)}, u32[]{:S(2)}, u32[]{:S(2)}) collective-permute-start(bf16[512,512]{0,1:T(8,128)(2,1)S(1)} %bitcast.275), channel_id=1, source_target_pairs={{0,1},{1,0},{2,3},{3,2},{4,5},{5,4},{6,7},{7,6},{8,9},{9,8},{10,11... | collective-permute-start | bytes 1572872 | tf_op jit(solution)/shard_map/ppermute | solution.py:261
  231.2 14.1 %collective-permute-start.43 = (bf16[128,512]{1,0:T(8,128)(2,1)S(1)}, bf16[128,512]{1,0:T(8,128)(2,1)S(1)}, u32[]{:S(2)}, u32[]{:S(2)}) collective-permute-start(bf16[128,512]{1,0:T(8,128)(2,1)S(1)} %copy-done.24), channel_id=1, source_target_pairs={{0,1},{1,0},{2,3},{3,2},{4,5},{5,4},{6,7},{7,6},{8,9},{9,8},{10,11... | collective-permute-start | bytes 393224 | tf_op jit(solution)/shard_map/ppermute | solution.py:261
  232.0 3.7 %collective-permute-start.48 = (f32[4,128]{1,0:T(4,128)S(1)}, f32[4,128]{1,0:T(4,128)S(1)}, u32[]{:S(2)}, u32[]{:S(2)}) collective-permute-start(f32[4,128]{1,0:T(4,128)S(1)} %fusion.41), channel_id=1, source_target_pairs={{0,2},{1,3},{2,0},{3,1},{4,6},{5,7},{6,4},{7,5},{8,10},{9,11},{10,... | collective-permute-start | bytes 6152 | tf_op jit(solution)/shard_map/ppermute | solution.py:261
  235.7 3.7 %collective-permute-start.49 = (f32[4,128]{1,0:T(4,128)S(1)}, f32[4,128]{1,0:T(4,128)S(1)}, u32[]{:S(2)}, u32[]{:S(2)}) collective-permute-start(f32[4,128]{1,0:T(4,128)S(1)} %fusion.76), channel_id=1, source_target_pairs={{0,4},{1,5},{2,6},{3,7},{4,0},{5,1},{6,2},{7,3},{8,12},{9,13},{10,... | collective-permute-start | bytes 6152 | tf_op jit(solution)/shard_map/ppermute | solution.py:261
  239.3 4.5 %collective-permute-start.50 = (f32[4,128]{1,0:T(4,128)S(1)}, f32[4,128]{1,0:T(4,128)S(1)}, u32[]{:S(2)}, u32[]{:S(2)}) collective-permute-start(f32[4,128]{1,0:T(4,128)S(1)} %add.137), channel_id=1, source_target_pairs={{0,8},{1,9},{2,10},{3,11},{4,12},{5,13},{6,14},{7,15},{8,0},{9,1},... | collective-permute-start | bytes 6152 | tf_op jit(solution)/shard_map/ppermute | solution.py:261
  262.7 19.9 %collective-permute-start.53 = (bf16[4,64,1024]{2,1,0:T(8,128)(2,1)}, bf16[4,64,1024]{2,1,0:T(8,128)(2,1)S(1)}, u32[]{:S(2)}, u32[]{:S(2)}) collective-permute-start(bf16[4,64,1024]{2,1,0:T(8,128)(2,1)} %get-tuple-element.52), channel_id=1, source_target_pairs={{0,2},{1,3},{2,0},{3,1},{4,6},{5,7},{6,4},{7,5},{8,10},{9,11},{10,... | collective-permute-start | bytes 1572872 | tf_op jit(solution)/shard_map/ppermute | solution.py:261
  269.4 19.5 %collective-permute-start.57 = (bf16[4,64,1024]{2,1,0:T(8,128)(2,1)}, bf16[4,64,1024]{2,1,0:T(8,128)(2,1)S(1)}, u32[]{:S(2)}, u32[]{:S(2)}) collective-permute-start(bf16[4,64,1024]{2,1,0:T(8,128)(2,1)} %get-tuple-element.58), channel_id=1, source_target_pairs={{0,2},{1,3},{2,0},{3,1},{4,6},{5,7},{6,4},{7,5},{8,10},{9,11},{10,... | collective-permute-start | bytes 1572872 | tf_op jit(solution)/shard_map/ppermute | solution.py:261
  275.1 25.0 %collective-permute-start.61 = (bf16[4,64,1024]{2,1,0:T(8,128)(2,1)}, bf16[4,64,1024]{2,1,0:T(8,128)(2,1)S(1)}, u32[]{:S(2)}, u32[]{:S(2)}) collective-permute-start(bf16[4,64,1024]{2,1,0:T(8,128)(2,1)} %get-tuple-element.64), channel_id=1, source_target_pairs={{0,2},{1,3},{2,0},{3,1},{4,6},{5,7},{6,4},{7,5},{8,10},{9,11},{10,... | collective-permute-start | bytes 1572872 | tf_op jit(solution)/shard_map/ppermute | solution.py:261
  282.2 28.7 %collective-permute-start.65 = (bf16[4,64,1024]{2,1,0:T(8,128)(2,1)}, bf16[4,64,1024]{2,1,0:T(8,128)(2,1)S(1)}, u32[]{:S(2)}, u32[]{:S(2)}) collective-permute-start(bf16[4,64,1024]{2,1,0:T(8,128)(2,1)} %get-tuple-element.70), channel_id=1, source_target_pairs={{0,2},{1,3},{2,0},{3,1},{4,6},{5,7},{6,4},{7,5},{8,10},{9,11},{10,... | collective-permute-start | bytes 1572872 | tf_op jit(solution)/shard_map/ppermute | solution.py:261
  285.7 25.5 %collective-permute-start.54 = (bf16[64,1024]{1,0:T(8,128)(2,1)}, bf16[64,1024]{1,0:T(8,128)(2,1)S(1)}, u32[]{:S(2)}, u32[]{:S(2)}) collective-permute-start(bf16[64,1024]{1,0:T(8,128)(2,1)} %get-tuple-element.54), channel_id=1, source_target_pairs={{0,4},{1,5},{2,6},{3,7},{4,0},{5,1},{6,2},{7,3},{8,12},{9,13},{10,... | collective-permute-start | bytes 393224 | tf_op jit(solution)/shard_map/ppermute | solution.py:261
  286.1 27.5 %collective-permute-start.55 = (bf16[64,1024]{1,0:T(8,128)(2,1)}, bf16[64,1024]{1,0:T(8,128)(2,1)S(1)}, u32[]{:S(2)}, u32[]{:S(2)}) collective-permute-start(bf16[64,1024]{1,0:T(8,128)(2,1)} %get-tuple-element.55), channel_id=1, source_target_pairs={{0,8},{1,9},{2,10},{3,11},{4,12},{5,13},{6,14},{7,15},{8,0},{9,1},... | collective-permute-start | bytes 393224 | tf_op jit(solution)/shard_map/ppermute | solution.py:261
  288.9 27.6 %collective-permute-start.56 = (bf16[64,1024]{1,0:T(8,128)(2,1)}, bf16[64,1024]{1,0:T(8,128)(2,1)S(1)}, u32[]{:S(2)}, u32[]{:S(2)}) collective-permute-start(bf16[64,1024]{1,0:T(8,128)(2,1)} %get-tuple-element.56), channel_id=1, source_target_pairs={{0,12},{1,13},{2,14},{3,15},{4,8},{5,9},{6,10},{7,11},{8,4},{9,5},... | collective-permute-start | bytes 393224 | tf_op jit(solution)/shard_map/ppermute | solution.py:261
  300.2 17.7 %collective-permute-start.58 = (bf16[64,1024]{1,0:T(8,128)(2,1)}, bf16[64,1024]{1,0:T(8,128)(2,1)S(1)}, u32[]{:S(2)}, u32[]{:S(2)}) collective-permute-start(bf16[64,1024]{1,0:T(8,128)(2,1)} %get-tuple-element.60), channel_id=1, source_target_pairs={{0,4},{1,5},{2,6},{3,7},{4,0},{5,1},{6,2},{7,3},{8,12},{9,13},{10,... | collective-permute-start | bytes 393224 | tf_op jit(solution)/shard_map/ppermute | solution.py:261
  310.8 15.8 %collective-permute-start.59 = (bf16[64,1024]{1,0:T(8,128)(2,1)}, bf16[64,1024]{1,0:T(8,128)(2,1)S(1)}, u32[]{:S(2)}, u32[]{:S(2)}) collective-permute-start(bf16[64,1024]{1,0:T(8,128)(2,1)} %get-tuple-element.61), channel_id=1, source_target_pairs={{0,8},{1,9},{2,10},{3,11},{4,12},{5,13},{6,14},{7,15},{8,0},{9,1},... | collective-permute-start | bytes 393224 | tf_op jit(solution)/shard_map/ppermute | solution.py:261
  311.2 15.4 %collective-permute-start.60 = (bf16[64,1024]{1,0:T(8,128)(2,1)}, bf16[64,1024]{1,0:T(8,128)(2,1)S(1)}, u32[]{:S(2)}, u32[]{:S(2)}) collective-permute-start(bf16[64,1024]{1,0:T(8,128)(2,1)} %get-tuple-element.62), channel_id=1, source_target_pairs={{0,12},{1,13},{2,14},{3,15},{4,8},{5,9},{6,10},{7,11},{8,4},{9,5},... | collective-permute-start | bytes 393224 | tf_op jit(solution)/shard_map/ppermute | solution.py:261
  313.6 17.8 %collective-permute-start.62 = (bf16[64,1024]{1,0:T(8,128)(2,1)}, bf16[64,1024]{1,0:T(8,128)(2,1)S(1)}, u32[]{:S(2)}, u32[]{:S(2)}) collective-permute-start(bf16[64,1024]{1,0:T(8,128)(2,1)} %get-tuple-element.66), channel_id=1, source_target_pairs={{0,4},{1,5},{2,6},{3,7},{4,0},{5,1},{6,2},{7,3},{8,12},{9,13},{10,... | collective-permute-start | bytes 393224 | tf_op jit(solution)/shard_map/ppermute | solution.py:261
  316.6 20.9 %collective-permute-start.63 = (bf16[64,1024]{1,0:T(8,128)(2,1)}, bf16[64,1024]{1,0:T(8,128)(2,1)S(1)}, u32[]{:S(2)}, u32[]{:S(2)}) collective-permute-start(bf16[64,1024]{1,0:T(8,128)(2,1)} %get-tuple-element.67), channel_id=1, source_target_pairs={{0,8},{1,9},{2,10},{3,11},{4,12},{5,13},{6,14},{7,15},{8,0},{9,1},... | collective-permute-start | bytes 393224 | tf_op jit(solution)/shard_map/ppermute | solution.py:261
  317.9 19.6 %collective-permute-start.64 = (bf16[64,1024]{1,0:T(8,128)(2,1)}, bf16[64,1024]{1,0:T(8,128)(2,1)S(1)}, u32[]{:S(2)}, u32[]{:S(2)}) collective-permute-start(bf16[64,1024]{1,0:T(8,128)(2,1)} %get-tuple-element.68), channel_id=1, source_target_pairs={{0,12},{1,13},{2,14},{3,15},{4,8},{5,9},{6,10},{7,11},{8,4},{9,5},... | collective-permute-start | bytes 393224 | tf_op jit(solution)/shard_map/ppermute | solution.py:261
  326.6 13.4 %collective-permute-start.66 = (bf16[64,1024]{1,0:T(8,128)(2,1)}, bf16[64,1024]{1,0:T(8,128)(2,1)S(1)}, u32[]{:S(2)}, u32[]{:S(2)}) collective-permute-start(bf16[64,1024]{1,0:T(8,128)(2,1)} %get-tuple-element.72), channel_id=1, source_target_pairs={{0,4},{1,5},{2,6},{3,7},{4,0},{5,1},{6,2},{7,3},{8,12},{9,13},{10,... | collective-permute-start | bytes 393224 | tf_op jit(solution)/shard_map/ppermute | solution.py:261
  326.6 18.3 %collective-permute-start.67 = (bf16[64,1024]{1,0:T(8,128)(2,1)}, bf16[64,1024]{1,0:T(8,128)(2,1)S(1)}, u32[]{:S(2)}, u32[]{:S(2)}) collective-permute-start(bf16[64,1024]{1,0:T(8,128)(2,1)} %get-tuple-element.73), channel_id=1, source_target_pairs={{0,8},{1,9},{2,10},{3,11},{4,12},{5,13},{6,14},{7,15},{8,0},{9,1},... | collective-permute-start | bytes 393224 | tf_op jit(solution)/shard_map/ppermute | solution.py:261
  331.4 13.5 %collective-permute-start.68 = (bf16[64,1024]{1,0:T(8,128)(2,1)}, bf16[64,1024]{1,0:T(8,128)(2,1)S(1)}, u32[]{:S(2)}, u32[]{:S(2)}) collective-permute-start(bf16[64,1024]{1,0:T(8,128)(2,1)} %get-tuple-element.74), channel_id=1, source_target_pairs={{0,12},{1,13},{2,14},{3,15},{4,8},{5,9},{6,10},{7,11},{8,4},{9,5},... | collective-permute-start | bytes 393224 | tf_op jit(solution)/shard_map/ppermute | solution.py:261
  (56 other events, 412.4 us)

commit v2 on v1

v2 whole, which is shorter than its diff:
```python
import functools

import jax
import jax.numpy as jnp
from jax import lax
from jax.experimental import pallas as pl
from jax.experimental.pallas import tpu as pltpu
from jax.sharding import PartitionSpec as P

HEAD = 128
SHEAD = 64
STATE = 128
LANES = 128
OUT_CHUNKS = 4
SPLIT = (2, 3, 3)
HINT = 16
OUT_TILE = 512
SMALL = 8 * 1024 * 1024
MIDDLE = 14 * 1024 * 1024
LARGE = 58 * 1024 * 1024

norm_eps = 1e-05
f32 = jnp.float32
bf16 = jnp.bfloat16


def cost(flops, moved):
    return pl.CostEstimate(flops=flops // HINT, bytes_accessed=moved // HINT, transcendentals=0)


def after(value, *events):
    return lax.optimization_barrier((value, *events))[0]


def pick(parts, index):
    chosen = parts[0]
    for m in range(1, len(parts)):
        chosen = jnp.where(index == m, parts[m], chosen)
    return chosen


def reorder_weights(mixer_in, block, spot):
    kinds, rows, channels = mixer_in.shape

    def body(spot_ref, source, target):
        for k in range(kinds):
            target[:, k * channels : (k + 1) * channels] = source[k]

    return pl.pallas_call(
        body,
        grid_spec=pltpu.PrefetchScalarGridSpec(
            num_scalar_prefetch=1,
            grid=(rows // block,),
            in_specs=[pl.BlockSpec((kinds, block, channels), lambda r, s: (0, s[0] ^ r, 0))],
            out_specs=pl.BlockSpec((block, kinds * channels), lambda r, s: (r, 0)),
        ),
        out_shape=jax.ShapeDtypeStruct((rows, kinds * channels), mixer_in.dtype),
        compiler_params=pltpu.CompilerParams(vmem_limit_bytes=SMALL),
        cost_estimate=cost(0, 4 * mixer_in.size),
        name="reorder_weights",
    )(spot, mixer_in)


def attention(queries, key_rows, value_rows, kv_head):
    length, columns = queries.shape
    heads = columns // HEAD
    tall = min(length, 128)

    def body(kv_ref, q_ref, k_ref, v_ref, out_ref):
        for r in range(length // tall):
            seen = (r + 1) * tall
            at = slice(r * tall, seen)
            scores = lax.dot_general(
                q_ref[at], k_ref[:seen], (((1,), (1,)), ((), ())), preferred_element_type=f32
            ) * HEAD ** (-0.5)
            row = lax.broadcasted_iota(jnp.int32, (tall, seen), 0) + r * tall
            column = lax.broadcasted_iota(jnp.int32, (tall, seen), 1)
            scores = jnp.where(row >= column, scores, -jnp.inf)
            grown = jnp.exp(scores - jnp.max(scores, axis=1, keepdims=True))
            probs = (grown / jnp.sum(grown, axis=1, keepdims=True)).astype(bf16)
            out_ref[at] = jnp.dot(probs, v_ref[:seen], preferred_element_type=f32).astype(bf16)

    return pl.pallas_call(
        body,
        grid_spec=pltpu.PrefetchScalarGridSpec(
            num_scalar_prefetch=1,
            grid=(heads,),
            in_specs=[
                pl.BlockSpec((length, HEAD), lambda h, s: (0, h)),
                pl.BlockSpec((length, HEAD), lambda h, s: (0, s[0])),
                pl.BlockSpec((length, HEAD), lambda h, s: (0, s[0])),
            ],
            out_specs=pl.BlockSpec((length, HEAD), lambda h, s: (0, h)),
        ),
        out_shape=jax.ShapeDtypeStruct((length, columns), bf16),
        compiler_params=pltpu.CompilerParams(vmem_limit_bytes=SMALL),
        cost_estimate=cost(4 * length * length * columns, 4 * length * columns),
        name="attention",
    )(kv_head, queries, key_rows, value_rows)


def scan_weights(n, rows, shared, run_col, run_row, step_row):
    heads = run_row.shape[0]
    pairs = heads // 2
    wide = 2 * rows
    here = slice(n * rows, (n + 1) * rows)

    def body(shared_ref, col_ref, row_ref, step_ref, out_ref):
        below = lax.broadcasted_iota(jnp.int32, (rows, rows), 0) >= lax.broadcasted_iota(
            jnp.int32, (rows, rows), 1
        )
        for j in range(n + 1):
            there = slice(j * rows, (j + 1) * rows)
            contact = lax.dot_general(
                shared_ref[here, STATE : 2 * STATE],
                shared_ref[there, :STATE],
                (((1,), (1,)), ((), ())),
                precision=lax.Precision.HIGHEST,
                preferred_element_type=f32,
            )
            for h in range(heads):
                span = col_ref[here, h : h + 1] - row_ref[h : h + 1, there]
                if j == n:
                    span = jnp.where(below, span, -jnp.inf)
                weight = contact * jnp.exp(span) * step_ref[h : h + 1, there]
                high = weight.astype(bf16)
                low = (weight - high.astype(f32)).astype(bf16)
                at = (h % 2) * rows
                out_ref[h // 2, at : at + rows, j * wide : (j + 1) * wide] = jnp.concatenate(
                    [high, low], axis=1
                )

    grown = (n + 1) * rows
    return pl.pallas_call(
        body,
        out_shape=jax.ShapeDtypeStruct((pairs, wide, (n + 1) * wide), bf16),
        compiler_params=pltpu.CompilerParams(vmem_limit_bytes=SMALL),
        cost_estimate=cost(12 * grown * rows * STATE, 4 * heads * grown * rows),
        name="scan_weights",
    )(shared, run_col, run_row, step_row)


def scan_chunk(n, rows, weights, pieces, earlier, skip, gain):
    pairs, wide, _ = weights.shape
    channels = skip.shape[1]
    parts = [a for a, _, _ in pieces]
    count = 3 + sum(map(len, parts))

    def body(*refs):
        weights_ref, skip_ref, gain_ref = refs[:3]
        earlier_refs = refs[count : count + n]
        split_ref, gated_ref, squares_ref = refs[count + n :]

        def projected(lane):
            found, at = [], 3
            for arrays, start, stop in pieces:
                total = refs[at][start:stop, lane]
                for m in range(1, len(arrays)):
                    total = total + refs[at + m][start:stop, lane].astype(f32)
                at += len(arrays)
                found.append(total)
            return jnp.concatenate(found, axis=0) if len(found) > 1 else found[0]

        left = lax.broadcasted_iota(jnp.int32, (rows, LANES), 1) < SHEAD
        squares = jnp.zeros((rows, LANES), f32)
        for p in range(pairs):
            lane = slice(p * LANES, (p + 1) * LANES)
            gate_lane = slice(channels + p * LANES, channels + (p + 1) * LANES)
            x = projected(lane)
            gate = projected(gate_lane)
            high = x.astype(bf16)
            low = (x - high.astype(f32)).astype(bf16)
            both = jnp.concatenate([high, low], axis=1)
            split_ref[p] = jnp.concatenate([both, both], axis=0)
            total = jnp.dot(
                weights_ref[p, :, n * wide : (n + 1) * wide],
                split_ref[p],
                preferred_element_type=f32,
            )
            for j in range(n):
                total = total + jnp.dot(
                    weights_ref[p, :, j * wide : (j + 1) * wide],
                    earlier_refs[j][p],
                    preferred_element_type=f32,
                )
            total = total[:, :LANES] + total[:, LANES:]
            scanned = jnp.where(left, total[:rows], total[rows:])
            gated = (scanned + skip_ref[:, lane] * x) * (gate / (1.0 + jnp.exp(-gate)))
            squares = squares + gated * gated
            gated_ref[:, lane] = (gated * gain_ref[:, lane]).astype(bf16)
        squares_ref[...] = lax.dot_general(
            jnp.ones((8, LANES), f32),
            squares,
            (((1,), (1,)), ((), ())),
            precision=lax.Precision.HIGHEST,
            preferred_element_type=f32,
        )[:1]

    return pl.pallas_call(
        body,
        out_shape=(
            jax.ShapeDtypeStruct((pairs, wide, 2 * LANES), bf16),
            jax.ShapeDtypeStruct((rows, channels), bf16),
            jax.ShapeDtypeStruct((1, rows), f32),
        ),
        compiler_params=pltpu.CompilerParams(vmem_limit_bytes=MIDDLE),
        cost_estimate=cost(2 * pairs * wide * wide * 2 * LANES * (n + 1), 8 * rows * channels * 2),
        name="scan_chunk",
    )(weights, skip, gain, *(a for arrays in parts for a in arrays), *earlier)


def project_out(at, width, spots, here, there, weight, weight_there, scale=None, *teacher):
    spots, far = spots
    sets = [(here, there)] + ([teacher[:2]] if teacher else [])
    weights = [weight, weight_there] + list(teacher[2:])
    pieces = [p for pair in sets for group in pair for p in group]
    channels = here[0].shape[1]
    length = sum(p.shape[0] for p in here)
    half = weight_there.shape[1]
    tile = min(OUT_TILE, width)
    steps = width // tile
    part = length // (2 * far)

    def body(spot_ref, *refs):
        weight_refs = refs[len(pieces) : len(pieces) + len(weights)]
        scale_ref = refs[len(pieces) + len(weights)]
        keep_ref, send_ref, rows_ref, tiles_ref, done = refs[-5:]
        z, y = spot_ref[0], spot_ref[1]
        own = pl.multiple_of(spot_ref[2] * half + at, LANES)
        copies = []
        for t in range(steps):
            for m, ref in enumerate(weight_refs):
                column = (own if m % 2 == 0 else at) + t * tile
                copies.append(
                    pltpu.make_async_copy(
                        ref.at[:, pl.ds(pl.multiple_of(column, LANES), tile)],
                        tiles_ref.at[t * len(weights) + m],
                        done.at[t * len(weights) + m],
                    )
                )
        for copy in copies:
            copy.start()
        from_row, slot = 0, 0
        for ref in refs[: len(pieces)]:
            size = ref.shape[0]
            rows_ref[slot, from_row : from_row + size] = ref[...]
            from_row += size
            if from_row == length:
                from_row, slot = 0, slot + 1
        for t in range(steps):
            lane = slice(t * tile, (t + 1) * tile)
            products = []
            for m in range(len(weights)):
                copies[t * len(weights) + m].wait()
            for m in range(0, len(weights), 2):
                first = t * len(weights) + m
                products.append(
                    jnp.dot(rows_ref[m], tiles_ref[first], preferred_element_type=f32)
                    + jnp.dot(rows_ref[m + 1], tiles_ref[first + 1], preferred_element_type=f32)
                )
            for zt in range(far):
                low = zt * 2 * part
                near, away = (
                    products[0][low + e * part : low + (e + 1) * part] for e in range(2)
                )
                if teacher:
                    near = near * scale_ref[zt, 0] - products[1][low : low + part]
                    away = away * scale_ref[zt, 1] - products[1][low + part : low + 2 * part]
                keep_ref[zt ^ z, :, lane] = jnp.where(y == 0, near, away)
                send_ref[zt ^ z, :, lane] = jnp.where(y == 0, away, near).astype(bf16)

    return pl.pallas_call(
        body,
        in_specs=[pl.BlockSpec(memory_space=pltpu.SMEM)]
        + [pl.BlockSpec(memory_space=pltpu.VMEM)] * len(pieces)
        + [pl.BlockSpec(memory_space=pltpu.HBM)] * len(weights)
        + ([pl.BlockSpec(memory_space=pltpu.VMEM)] if teacher else []),
        out_specs=[pl.BlockSpec(memory_space=pltpu.VMEM)] * 2,
        out_shape=(
            jax.ShapeDtypeStruct((far, part, width), f32),
            jax.ShapeDtypeStruct((far, part, width), bf16),
        ),
        scratch_shapes=[
            pltpu.VMEM((len(weights), length, channels), bf16),
            pltpu.VMEM((steps * len(weights), channels, tile), bf16),
            pltpu.SemaphoreType.DMA((steps * len(weights),)),
        ],
        compiler_params=pltpu.CompilerParams(vmem_limit_bytes=LARGE),
        cost_estimate=cost(
            2 * len(weights) * length * channels * width,
            2 * len(weights) * channels * width + 6 * length * width,
        ),
        name="project_out",
    )(spots, *pieces, *weights, *([scale] if teacher else []))


def add_near(keep, came, scale=None, teacher=None, teacher_came=None):
    far, part, width = keep.shape
    stay = far // 2
    extra = [a for a in (scale, teacher, teacher_came) if a is not None]

    def body(keep_ref, came_ref, *refs):
        stay_ref, send_ref = refs[-2:]
        for k in range(far):
            total = keep_ref[k] + came_ref[k].astype(f32)
            if extra:
                total = total * refs[0][k] - (refs[1][k] + refs[2][k].astype(f32))
            if k % 2 == 0:
                stay_ref[k // 2] = total
            else:
                send_ref[k // 2] = total.astype(bf16)

    return pl.pallas_call(
        body,
        out_shape=(
            jax.ShapeDtypeStruct((stay, part, width), f32),
            jax.ShapeDtypeStruct((stay, part, width), bf16),
        ),
        compiler_params=pltpu.CompilerParams(vmem_limit_bytes=SMALL),
        cost_estimate=cost(keep.size, 8 * keep.size),
        name="add_near",
    )(keep, came, *extra)


def finish(spots, kept, came):
    rows, width = kept[0].shape
    rows //= 2
    count = len(kept)

    def body(spot_ref, *refs):
        own_ref, other_ref = refs[-2:]
        core = spot_ref[2]
        for n in range(count):
            total = (refs[n][...] + refs[count + n][...].astype(f32)).astype(bf16)
            low, high = total[:rows], total[rows:]
            lane = slice(n * width, (n + 1) * width)
            own_ref[:, lane] = jnp.where(core == 0, low, high)
            other_ref[:, lane] = jnp.where(core == 0, high, low)

    return pl.pallas_call(
        body,
        in_specs=[pl.BlockSpec(memory_space=pltpu.SMEM)]
        + [pl.BlockSpec(memory_space=pltpu.VMEM)] * (2 * count),
        out_shape=(jax.ShapeDtypeStruct((rows, count * width), bf16),) * 2,
        compiler_params=pltpu.CompilerParams(vmem_limit_bytes=SMALL),
        cost_estimate=cost(kept[0].size * count, 8 * kept[0].size * count),
        name="finish",
    )(spots, *kept, *came)


def local(
    ndp,
    nmp,
    hidden_in,
    queries,
    key_rows,
    value_rows,
    teacher_proj,
    mixer_in,
    shared_in,
    dt_bias,
    a_log,
    d_skip,
    norm_gain,
    mixer_out,
):
    far = nmp // 4
    group = far // ndp
    me = lax.axis_index("mp")
    seq = lax.axis_index("dp")
    core, y, z = me % 2, (me // 2) % 2, me // 4

    def swap(source, k):
        return lax.ppermute(source, "mp", [(s, s ^ k) for s in range(nmp)])

    def cross(source, k):
        return lax.ppermute(source, "dp", [(s, s ^ k) for s in range(ndp)])

    length, block = hidden_in.shape
    channels = mixer_in.shape[2]
    heads = dt_bias.shape[0]
    rows = length // far
    spots = jnp.stack([z, y, core]).astype(jnp.int32)

    def at(source, index):
        return lax.dynamic_index_in_dim(source, index, 0, False)

    head_count = queries.shape[1] // HEAD
    kv_heads = key_rows.shape[1] // HEAD
    kv_head = (me * head_count // (head_count * nmp // kv_heads)).astype(jnp.int32).reshape(1)
    context = attention(queries, key_rows, value_rows, kv_head)

    shared = lax.psum(jnp.dot(hidden_in, shared_in, preferred_element_type=f32), "mp")

    turn = (z // group) ^ seq
    spot = (me % (4 * group)).astype(jnp.int32).reshape(1)
    distances = [0]
    k = far // 2
    while k:
        distances += [d + k for d in distances]
        k //= 2
    order = [distances.index(d) for d in range(far)]
    sizes = [length * share // sum(SPLIT) for share in SPLIT]
    ends = [sum(sizes[: n + 1]) for n in range(len(sizes))]
    before = {}

    def in_turn(step, value):
        return after(value, before[step]) if step in before else value

    half = mixer_out.shape[1] // 2
    width = half // OUT_CHUNKS

    def half_sent(weight):
        return lax.dynamic_slice_in_dim(weight, (1 - core) * half, half, 1)

    weights_in = None
    projected = []
    for n, size in enumerate(sizes):
        line = [hidden_in[ends[n] - size : ends[n]]]
        k = far // 2
        while k:
            packed = in_turn(k, jnp.stack(line))
            if n == 0 and k == 1:
                packed = after(packed, context)
            came = before[k] = swap(packed, 4 * k)
            line = line + [came[m] for m in range(len(line))]
            k //= 2
        line = [line[m] for m in order]
        line = [jnp.stack(line[m * group : (m + 1) * group]) for m in range(ndp)]
        square = [pick(line, turn ^ d) for d in range(ndp)]
        away = in_turn("dp", tuple(square[1:]))
        square = before["dp"] = jnp.stack(
            [square[0]] + [cross(away[d - 1], d) for d in range(1, ndp)], 1
        )
        if weights_in is None:
            weights_in = reorder_weights(after(mixer_in, line[0]), block, spot)
        if n == 0:
            sent = [half_sent(after(weight, square)) for weight in (teacher_proj, mixer_out)]
        if n == 1:
            square = after(square, *sent)
            teacher_there, mixer_there = (swap(weight, 1) for weight in sent)
            teacher = ([context], [swap(context, 1)], teacher_proj, teacher_there)
            first = project_out(0, width, (spots, far), *teacher)
        if n == len(sizes) - 1:
            square = after(square, first[1])
        both = jnp.stack([square, swap(square, 2)])
        all_four = [both, swap(both, 1)]
        features = jnp.concatenate(
            [all_four[c][b][k] for k in range(group) for b in range(2) for c in range(2)],
            axis=-1,
        )
        found = [
            cross(jnp.dot(features[d], weights_in, preferred_element_type=f32).astype(bf16), d)
            for d in range(1, ndp)
        ]
        projected.append([jnp.dot(features[0], weights_in, preferred_element_type=f32)] + found)

    first_came = swap(after(first[1], both), 2)

    shared = after(shared, both)
    dt_raw = lax.dynamic_slice_in_dim(shared, 2 * STATE + me * heads, heads, 1)
    step_size = jax.nn.softplus(dt_raw + dt_bias)
    log_decay = -step_size * jnp.exp(a_log)
    causal = jnp.arange(length)[:, None] >= jnp.arange(length)[None, :]
    running = jnp.dot(causal.astype(f32), log_decay, precision=lax.Precision.HIGHEST)
    run_row, step_row = running.T, step_size.T
    scans = [scan_weights(n, rows, shared, running, run_row, step_row) for n in range(far)]
    skip = jnp.repeat(d_skip, SHEAD)[None, :]
    earlier, gated, gated_other, squares = [], [], [], []
    for n in range(far):
        pieces = []
        for m, size in enumerate(sizes):
            start, stop = ends[m] - size, ends[m]
            low, high = max(start, n * rows), min(stop, (n + 1) * rows)
            if low < high:
                pieces.append((projected[m], low - start, high - start))
        split, gated_n, squares_n = scan_chunk(
            n, rows, scans[n], pieces, earlier, skip, norm_gain[None, :]
        )
        earlier.append(split)
        gated.append(gated_n)
        gated_other.append(swap(gated_n, 1))
        squares.append(squares_n)
    weights = (gated, gated_other, mixer_out, mixer_there)
    gated[-1] = after(gated[-1], first_came)
    keep, send = project_out(0, width, (spots, far), *weights)
    squares = jnp.concatenate(squares)
    k = 1
    while k < nmp:
        if k == 4:
            squares = after(squares, send)
        squares = squares + swap(squares, k)
        k *= 2
    scale = lax.rsqrt(squares / (channels * nmp) + norm_eps).reshape(far, 2, rows // 2, 1)
    scale_kept = jnp.stack([at(at(scale, z ^ k), y) for k in range(far)])

    done, far_came = [], []
    for n in range(OUT_CHUNKS):
        if n == 0:
            keep, send = add_near(keep, swap(send, 2), scale_kept, first[0], first_came)
        else:
            keep, send = project_out(n * width, width, (spots, far), *weights, scale, *teacher)
            came = swap(send, 2)
            if n >= 2:
                came = after(came, far_came[n - 2])
            keep, send = add_near(keep, came)
        k = 1
        while k < far // 2:
            keep, send = add_near(keep, swap(send, 4 * k))
            k *= 2
        far_came.append(swap(send[0], 4 * k))
        done.append(keep[0])
    stay, came = finish(spots, done, far_came)
    came = swap(came, 1)
    return jnp.concatenate(
        [jnp.where(core == 0, stay, came), jnp.where(core == 0, came, stay)], axis=1
    )


def solution(mesh):
    placed = (
        P("dp", "mp"),
        P("dp", "mp"),
        P("dp", None),
        P("dp", None),
        P("mp", None),
        P(None, "dp", "mp"),
        P("mp", None),
        P("mp"),
        P("mp"),
        P("mp"),
        P("mp"),
        P("mp", None),
    )
    return jax.shard_map(
        functools.partial(local, mesh.shape["dp"], mesh.shape["mp"]),
        mesh=mesh,
        in_specs=placed,
        out_specs=P(("dp", "mp"), None),
        check_vma=False,
    )
```

time: 352 us -> 265 us (0.75)
  starting transfers between devices: 77.1 us -> 39.2 us
  waiting for transfers between devices: 124 us -> 102 us
  Pallas kernels: 72.3 us -> 51.3 us
  matrix products: 32.6 us -> 19.4 us
  between operations: 1.28 us -> 14.4 us
  other arithmetic: 10.6 us -> 4.67 us
    ppermute x62 -> x37, starting transfers between devices: 66.9 us -> 32.3 us  [swap(): return lax.ppermute(source, 'mp', [(s, s ^ k) for s in range(nmp)])]
    ppermute x62 -> x37, waiting for transfers between devices: 103 us -> 80.4 us  [swap(): return lax.ppermute(source, 'mp', [(s, s ^ k) for s in range(nmp)])]
    dot_general x9 -> x7, matrix products: 32.2 us -> 18.2 us  [the longest x3 10.4 us: local(): jnp.dot(features[d], weights_in, preferred_element_type=f32).astype(bf16)]
    unnamed x138 -> x107, local copies, waits for them, and re-layouts: 8.38 us -> 21.5 us
    pallas_call x1, Pallas kernels: 12 us -> 1.34 us  [reorder_weights(): pl.pallas_call(body, grid_spec=pltpu.PrefetchScalarGridSpec(num_scalar_pr...]
    pallas_call x4, Pallas kernels: 12.1 us -> 3.92 us  [scan_chunk(): pl.pallas_call(body, out_shape=(jax.ShapeDtypeStruct((pairs, wide, 2 * LA...]
    slice x25 -> x0, local copies, waits for them, and re-layouts: 8.11 us -> none  [the longest x4 3.4 us: local(): own_parts.append(projected[0])]
    pallas_call x4, Pallas kernels: 10.9 us -> 2.87 us  [scan_weights(): pl.pallas_call(body, out_shape=jax.ShapeDtypeStruct((pairs, wide, (n + 1)...]
  transfers between devices with their start and end apart: 70 -> 44, of which waited for: 28 -> 27; matrix products, arithmetic and copies ran while one was open for 19% -> 17% of each run, Pallas kernels for 19% -> 17%
where the time goes in v2:
time: 265 us; the launch traced here: 264 us
  waiting for transfers between devices  102 us (38%)
  Pallas kernels  51.3 us (19%)
  starting transfers between devices  39.2 us (15%)
  local copies, waits for them, and re-layouts  33.1 us (12%)
  matrix products  19.4 us (7%)
  between operations  14.4 us (5%)
  other arithmetic  4.67 us (2%)
    ppermute x37, waiting for transfers between devices, swap(): return lax.ppermute(source, 'mp', [(s, s ^ k) for s in range(nmp)])  80.4 us
    ppermute x37, starting transfers between devices, swap(): return lax.ppermute(source, 'mp', [(s, s ^ k) for s in range(nmp)])  32.3 us
    pallas_call x5, Pallas kernels, project_out(): pl.pallas_call(body, in_specs=[pl.BlockSpec(memory_space=pltpu.SMEM)] + [...  31.3 us
    ppermute x6, waiting for transfers between devices, cross(): return lax.ppermute(source, 'dp', [(s, s ^ k) for s in range(ndp)])  21.6 us
    unnamed x107, local copies, waits for them, and re-layouts  21.5 us
    dot_general x3, matrix products, local(): jnp.dot(features[d], weights_in, preferred_element_type=f32).astype(bf16)  10.4 us
    ppermute x6, starting transfers between devices, cross(): return lax.ppermute(source, 'dp', [(s, s ^ k) for s in range(ndp)])  6.87 us
    dot_general x3, matrix products, local(): jnp.dot(features[0], weights_in, preferred_element_type=f32)  6.47 us
  transfers between devices with their start and end apart: 44, of which 27 were waited for; matrix products, arithmetic and copies ran while one was open for 17% of the time, Pallas kernels for 17%

profile of v2, /device:TPU:0, one launch (start us, length us, event | category | flops | bytes accessed | tf_op | source)
XLA Modules:
  0.0 264.2 jit_solution(2169115679937102101)
XLA Ops:
  7.5 4.1 %collective-permute-start = (bf16[1,128,512]{2,1,0:T(8,128)(2,1)S(1)}, bf16[1,128,512]{2,1,0:T(8,128)(2,1)S(1)}, u32[]{:S(2)}, u32[]{:S(2)}) collective-permute-start(bf16[1,128,512]{2,1,0:T(8,128)(2,1)S(1)} %get-tuple-element.128), channel_id=1, source_target_pairs={{0,8},{1,9},{2,10},{3,11},{4,12},{5,13},{6,14},{7,15},{8,0},{9,1},... | collective-permute-start | bytes 393224 | tf_op jit(solution)/shard_map/ppermute | solution.py:374
  11.6 1.2 copy-done.14
  12.8 1.2 copy-done.15
  15.1 6.2 %attention.1.refs_0_.refs_8_ = bf16[512,512]{1,0:T(8,128)(2,1)S(1)} custom-call(s32[1]{0:T(128)} %bitcast.7.kv_ref, bf16[512,512]{1,0:T(8,128)(2,1)S(1)} %copy-done.18, bf16[512,1024]{1,0:T(8,128)(2,1)S(1)} %copy-done.14, bf16[512,1024]{1,0:T(8,128)(2,1)S(1)} %copy-done.15), custom_call_target="tpu_custom_call" | custom-call | flops 33554432 | bytes 65536 | tf_op jit(solution)/shard_map/attention/pallas_call | solution.py:83
  21.5 1.6 collective-permute-start.3
  23.5 1.3 fusion.46
  25.1 3.4 %copy-done.4 = bf16[2,4096,512]{2,1,0:T(8,128)(2,1)S(1)} copy-done((bf16[2,4096,512]{2,1,0:T(8,128)(2,1)S(1)}, bf16[2,4096,512]{2,1,0:T(8,128)(2,1)}, u32[]{:S(2)}) %copy-start.4) | copy-done | bytes 8388632
  28.5 1.3 reorder_weights.1
  30.5 5.5 %collective-permute-done.1 = bf16[1,192,512]{2,1,0:T(8,128)(2,1)S(1)} collective-permute-done((bf16[1,192,512]{2,1,0:T(8,128)(2,1)S(1)}, bf16[1,192,512]{2,1,0:T(8,128)(2,1)S(1)}, u32[]{:S(2)}, u32[]{:S(2)}) %collective-permute-start.1) | collective-permute-done | bytes 196640 | tf_op jit(solution)/shard_map/ppermute | solution.py:374
  36.1 1.8 collective-permute-start.2
  38.0 1.6 collective-permute-start.6
  39.7 8.3 %collective-permute-done.2 = bf16[1,192,512]{2,1,0:T(8,128)(2,1)S(1)} collective-permute-done((bf16[1,192,512]{2,1,0:T(8,128)(2,1)S(1)}, bf16[1,192,512]{2,1,0:T(8,128)(2,1)S(1)}, u32[]{:S(2)}, u32[]{:S(2)}) %collective-permute-start.2) | collective-permute-done | bytes 196640 | tf_op jit(solution)/shard_map/ppermute | solution.py:374
  48.2 1.6 collective-permute-start.12
  49.7 2.3 constant_dynamic-slice_fusion.5
  52.0 4.1 %collective-permute-done.4 = bf16[2,192,512]{2,1,0:T(8,128)(2,1)S(1)} collective-permute-done((bf16[2,192,512]{2,1,0:T(8,128)(2,1)S(1)}, bf16[2,192,512]{2,1,0:T(8,128)(2,1)S(1)}, u32[]{:S(2)}, u32[]{:S(2)}) %collective-permute-start.4) | collective-permute-done | bytes 393248 | tf_op jit(solution)/shard_map/ppermute | solution.py:374
  57.1 2.2 constant_dynamic-slice_fusion.4
  59.8 1.9 collective-permute-done.12
  61.9 3.8 %collective-permute-done.7 = bf16[2,192,512]{2,1,0:T(8,128)(2,1)S(1)} collective-permute-done((bf16[2,192,512]{2,1,0:T(8,128)(2,1)S(1)}, bf16[2,192,512]{2,1,0:T(8,128)(2,1)S(1)}, u32[]{:S(2)}, u32[]{:S(2)}) %collective-permute-start.7) | collective-permute-done | bytes 393248 | tf_op jit(solution)/shard_map/ppermute | solution.py:377
  65.8 2.2 collective-permute-start.15
  68.0 3.7 %collective-permute-done.5 = bf16[2,192,512]{2,1,0:T(8,128)(2,1)S(1)} collective-permute-done((bf16[2,192,512]{2,1,0:T(8,128)(2,1)S(1)}, bf16[2,192,512]{2,1,0:T(8,128)(2,1)S(1)}, u32[]{:S(2)}, u32[]{:S(2)}) %collective-permute-start.5) | collective-permute-done | bytes 393248 | tf_op jit(solution)/shard_map/ppermute | solution.py:374
  71.8 1.4 collective-permute-start.8
  74.0 8.5 %collective-permute-done.8 = bf16[2,192,512]{2,1,0:T(8,128)(2,1)S(1)} collective-permute-done((bf16[2,192,512]{2,1,0:T(8,128)(2,1)S(1)}, bf16[2,192,512]{2,1,0:T(8,128)(2,1)S(1)}, u32[]{:S(2)}, u32[]{:S(2)}) %collective-permute-start.8) | collective-permute-done | bytes 393248 | tf_op jit(solution)/shard_map/ppermute | solution.py:377
  83.9 1.3 convolution_convert_fusion
  86.3 1.3 fusion.6.refs_3_
  87.7 4.3 %collective-permute-done.16 = bf16[2,2,2,192,512]{4,3,2,1,0:T(8,128)(2,1)S(1)} collective-permute-done((bf16[2,2,2,192,512]{4,3,2,1,0:T(8,128)(2,1)S(1)}, bf16[2,2,2,192,512]{4,3,2,1,0:T(8,128)(2,1)S(1)}, u32[]{:S(2)}, u32[]{:S(2)}) %collective-permute-start.16) | collective-permute-done | bytes 1572896 | tf_op jit(solution)/shard_map/ppermute | solution.py:374
  95.2 5.0 %project_out.5 = (f32[4,64,1024]{2,1,0:T(8,128)}, bf16[4,64,1024]{2,1,0:T(8,128)(2,1)}) custom-call(s32[3]{0:T(128)} %pad_add_fusion.spot_ref, bf16[512,512]{1,0:T(8,128)(2,1)} %copy-done.3, bf16[512,512]{1,0:T(8,128)(2,1)} %copy-done.22, bf16[512,8192]{1,0:T(8,128)(2,1)} %refs_12_.5, bf16[512,4096]{1,0:T(8,128)(2,1)} %collective-permute-done.10.refs_3_.refs_13_), custom_call_target="tpu_custom_call" | custom-call | flops 67108864 | bytes 327680 | tf_op jit(solution)/shard_map/project_out/pallas_call | solution.py:272
  100.2 2.5 collective-permute-start.11
  103.5 1.8 fusion.18
  106.1 1.8 fusion.16
  107.9 14.1 %collective-permute-done.11 = bf16[2,2,192,512]{3,2,1,0:T(8,128)(2,1)S(1)} collective-permute-done((bf16[2,2,192,512]{3,2,1,0:T(8,128)(2,1)S(1)}, bf16[2,2,192,512]{3,2,1,0:T(8,128)(2,1)S(1)}, u32[]{:S(2)}, u32[]{:S(2)}) %collective-permute-start.11) | collective-permute-done | bytes 786464 | tf_op jit(solution)/shard_map/ppermute | solution.py:374
  122.0 1.3 pad_maximum_fusion
  123.3 7.2 %fusion.4 = bf16[192,1024]{1,0:T(8,128)(2,1)} fusion(bf16[4096,1024]{1,0:T(8,128)(2,1)} %copy-done.2, bf16[2,192,4096]{2,1,0:T(8,128)(2,1)} %fusion.16), kind=kOutput, calls=%fused_computation.10 | convolution fusion | flops 1610809344 | bytes 10354688 | tf_op jit(solution)/shard_map/dot_general | solution.py:453
  130.5 3.3 %fusion.3.refs_3_ = f32[192,1024]{1,0:T(8,128)S(1)} fusion(bf16[4096,1024]{1,0:T(8,128)(2,1)S(1)} %bitcast.181, bf16[2,192,4096]{2,1,0:T(8,128)(2,1)} %fusion.16), kind=kOutput, calls=%fused_computation.7 | convolution fusion | flops 1610612736 | bytes 10747904 | tf_op jit(solution)/shard_map/dot_general | solution.py:456
  135.7 1.2 fusion.7
  136.9 1.4 copy.65.shared_ref
  138.4 1.4 collective-permute-start.20
  144.2 1.4 collective-permute-done.17.refs_4_
  146.4 1.5 fusion.15
  151.2 1.8 fusion.5
  154.1 1.8 fusion.1.refs_5_.refs_3_
  156.0 7.9 %collective-permute-done.19.refs_6_.refs_4_ = bf16[192,1024]{1,0:T(8,128)(2,1)S(1)} collective-permute-done((bf16[192,1024]{1,0:T(8,128)(2,1)S(1)}, bf16[192,1024]{1,0:T(8,128)(2,1)S(1)}, u32[]{:S(2)}, u32[]{:S(2)}) %collective-permute-start.19) | collective-permute-done | bytes 393248 | tf_op jit(solution)/shard_map/ppermute | solution.py:377
  164.8 1.6 scan_chunk.7
  167.6 1.5 collective-permute-start.28
  173.3 5.1 %project_out.6 = (f32[4,64,1024]{2,1,0:T(8,128)}, bf16[4,64,1024]{2,1,0:T(8,128)(2,1)}) custom-call(s32[3]{0:T(128)} %pad_add_fusion.spot_ref, bf16[128,512]{1,0:T(8,128)(2,1)} %copy-done.5, bf16[128,512]{1,0:T(8,128)(2,1)} %copy-done.6, bf16[128,512]{1,0:T(8,128)(2,1)} %copy-done.7, bf16[128,512]{1,0:T(8,128)(2,1)} %copy-done.8, ...), custom_call_target="tpu_custom_call" | custom-call | flops 67108864 | bytes 327680 | tf_op jit(solution)/shard_map/project_out/pallas_call | solution.py:272
  179.1 3.0 %collective-permute-done.29 = f32[4,128]{1,0:T(4,128)S(1)} collective-permute-done((f32[4,128]{1,0:T(4,128)S(1)}, f32[4,128]{1,0:T(4,128)S(1)}, u32[]{:S(2)}, u32[]{:S(2)}) %collective-permute-start.29) | collective-permute-done | bytes 2080 | tf_op jit(solution)/shard_map/ppermute | solution.py:374
  182.1 1.4 collective-permute-start.26
  183.5 3.1 %collective-permute-done.30 = f32[4,128]{1,0:T(4,128)S(1)} collective-permute-done((f32[4,128]{1,0:T(4,128)S(1)}, f32[4,128]{1,0:T(4,128)S(1)}, u32[]{:S(2)}, u32[]{:S(2)}) %collective-permute-start.30) | collective-permute-done | bytes 2080 | tf_op jit(solution)/shard_map/ppermute | solution.py:374
  187.5 7.0 %project_out.7 = (f32[4,64,1024]{2,1,0:T(8,128)}, bf16[4,64,1024]{2,1,0:T(8,128)(2,1)}) custom-call(s32[3]{0:T(128)} %pad_add_fusion.spot_ref, bf16[128,512]{1,0:T(8,128)(2,1)} %copy-done.5, bf16[128,512]{1,0:T(8,128)(2,1)} %copy-done.6, bf16[128,512]{1,0:T(8,128)(2,1)} %copy-done.7, bf16[128,512]{1,0:T(8,128)(2,1)} %copy-done.8, ...), custom_call_target="tpu_custom_call" | custom-call | flops 134217728 | bytes 458752 | tf_op jit(solution)/shard_map/project_out/pallas_call | solution.py:272
  194.5 1.5 collective-permute-start.32
  196.0 7.2 %project_out.9 = (f32[4,64,1024]{2,1,0:T(8,128)}, bf16[4,64,1024]{2,1,0:T(8,128)(2,1)}) custom-call(s32[3]{0:T(128)} %pad_add_fusion.spot_ref, bf16[128,512]{1,0:T(8,128)(2,1)} %copy-done.5, bf16[128,512]{1,0:T(8,128)(2,1)} %copy-done.6, bf16[128,512]{1,0:T(8,128)(2,1)} %copy-done.7, bf16[128,512]{1,0:T(8,128)(2,1)} %copy-done.8, ...), custom_call_target="tpu_custom_call" | custom-call | flops 134217728 | bytes 458752 | tf_op jit(solution)/shard_map/project_out/pallas_call | solution.py:272
  203.9 6.9 %project_out.8 = (f32[4,64,1024]{2,1,0:T(8,128)}, bf16[4,64,1024]{2,1,0:T(8,128)(2,1)}) custom-call(s32[3]{0:T(128)} %pad_add_fusion.spot_ref, bf16[128,512]{1,0:T(8,128)(2,1)} %copy-done.5, bf16[128,512]{1,0:T(8,128)(2,1)} %copy-done.6, bf16[128,512]{1,0:T(8,128)(2,1)} %copy-done.7, bf16[128,512]{1,0:T(8,128)(2,1)} %copy-done.8, ...), custom_call_target="tpu_custom_call" | custom-call | flops 134217728 | bytes 458752 | tf_op jit(solution)/shard_map/project_out/pallas_call | solution.py:272
  210.9 1.5 collective-permute-start.34
  213.8 1.4 add_near.8
  217.1 1.4 collective-permute-start.33
  218.5 6.2 %collective-permute-done.31.came_ref = bf16[2,64,1024]{2,1,0:T(8,128)(2,1)S(1)} collective-permute-done((bf16[2,64,1024]{2,1,0:T(8,128)(2,1)S(1)}, bf16[2,64,1024]{2,1,0:T(8,128)(2,1)S(1)}, u32[]{:S(2)}, u32[]{:S(2)}) %collective-permute-start.31) | collective-permute-done | bytes 262176 | tf_op jit(solution)/shard_map/ppermute | solution.py:374
  224.8 3.2 %collective-permute-done.33.came_ref = bf16[2,64,1024]{2,1,0:T(8,128)(2,1)S(1)} collective-permute-done((bf16[2,64,1024]{2,1,0:T(8,128)(2,1)S(1)}, bf16[2,64,1024]{2,1,0:T(8,128)(2,1)S(1)}, u32[]{:S(2)}, u32[]{:S(2)}) %collective-permute-start.33) | collective-permute-done | bytes 262176 | tf_op jit(solution)/shard_map/ppermute | solution.py:374
  229.1 3.2 %collective-permute-done.35.refs_4_ = bf16[64,1024]{1,0:T(8,128)(2,1)S(1)} collective-permute-done((bf16[64,1024]{1,0:T(8,128)(2,1)S(1)}, bf16[64,1024]{1,0:T(8,128)(2,1)S(1)}, u32[]{:S(2)}, u32[]{:S(2)}) %collective-permute-start.35) | collective-permute-done | bytes 131104 | tf_op jit(solution)/shard_map/ppermute | solution.py:374
  235.6 2.6 collective-permute-start.39
  238.2 4.7 %collective-permute-done.36.came_ref = bf16[2,64,1024]{2,1,0:T(8,128)(2,1)S(1)} collective-permute-done((bf16[2,64,1024]{2,1,0:T(8,128)(2,1)S(1)}, bf16[2,64,1024]{2,1,0:T(8,128)(2,1)S(1)}, u32[]{:S(2)}, u32[]{:S(2)}) %collective-permute-start.36) | collective-permute-done | bytes 262176 | tf_op jit(solution)/shard_map/ppermute | solution.py:374
  243.0 3.0 %collective-permute-done.39.came_ref = bf16[2,64,1024]{2,1,0:T(8,128)(2,1)S(1)} collective-permute-done((bf16[2,64,1024]{2,1,0:T(8,128)(2,1)S(1)}, bf16[2,64,1024]{2,1,0:T(8,128)(2,1)S(1)}, u32[]{:S(2)}, u32[]{:S(2)}) %collective-permute-start.39) | collective-permute-done | bytes 262176 | tf_op jit(solution)/shard_map/ppermute | solution.py:374
  246.1 2.2 collective-permute-start.41
  248.3 4.5 %collective-permute-done.40.refs_6_ = bf16[64,1024]{1,0:T(8,128)(2,1)S(1)} collective-permute-done((bf16[64,1024]{1,0:T(8,128)(2,1)S(1)}, bf16[64,1024]{1,0:T(8,128)(2,1)S(1)}, u32[]{:S(2)}, u32[]{:S(2)}) %collective-permute-start.40) | collective-permute-done | bytes 131104 | tf_op jit(solution)/shard_map/ppermute | solution.py:374
  252.8 1.4 collective-permute-done.41.refs_7_
  255.0 1.5 collective-permute-done.42
  (216 shorter events, 43.1 us)
Async XLA Ops:
  6.5 17.0 %copy-start = (bf16[512,384]{1,0:T(8,128)(2,1)S(1)}, bf16[512,384]{1,0:T(8,128)(2,1)}, u32[]{:S(2)}) copy-start(bf16[512,384]{1,0:T(8,128)(2,1)} %param.18) | copy-start | bytes 1179652
  6.5 129.1 %all-reduce.2.cloned.1.call-start = ((), (), s32[]{:S(2)}) async-start(), calls=%async_computation | async-start | bytes 1572864 | tf_op jit(solution)/shard_map/psum | solution.py:393
  7.5 14.0 %collective-permute-start = (bf16[1,128,512]{2,1,0:T(8,128)(2,1)S(1)}, bf16[1,128,512]{2,1,0:T(8,128)(2,1)S(1)}, u32[]{:S(2)}, u32[]{:S(2)}) collective-permute-start(bf16[1,128,512]{2,1,0:T(8,128)(2,1)S(1)} %get-tuple-element.128), channel_id=1, source_target_pairs={{0,8},{1,9},{2,10},{3,11},{4,12},{5,13},{6,14},{7,15},{8,0},{9,1},... | collective-permute-start | bytes 393224 | tf_op jit(solution)/shard_map/ppermute | solution.py:374
  15.1 9.9 %copy-start.37 = (f32[8]{0:T(128)S(1)}, f32[8]{0:T(128)}, u32[]{:S(2)}) copy-start(f32[8]{0:T(128)} %param.20) | copy-start | bytes 100
  15.1 9.9 %copy-start.36 = (f32[8]{0:T(128)S(1)}, f32[8]{0:T(128)}, u32[]{:S(2)}) copy-start(f32[8]{0:T(128)} %param.21) | copy-start | bytes 100
  21.3 8.6 %copy-start.3 = (bf16[512,512]{1,0:T(8,128)(2,1)}, bf16[512,512]{1,0:T(8,128)(2,1)S(1)}, u32[]{:S(2)}) copy-start(bf16[512,512]{1,0:T(8,128)(2,1)S(1)} %attention.1.refs_0_.refs_8_) | copy-start | bytes 1572868
  21.3 73.1 %collective-permute-start.9 = (bf16[512,512]{1,0:T(8,128)(2,1)S(1)}, bf16[512,512]{1,0:T(8,128)(2,1)S(1)}, u32[]{:S(2)}, u32[]{:S(2)}) collective-permute-start(bf16[512,512]{1,0:T(8,128)(2,1)S(1)} %attention.1.refs_0_.refs_8_), channel_id=1, source_target_pairs={{0,1},{1,0},{2,3},{3,2},{4,5},{5,4},{6,7},{7,6},{8,9},{9,8},{10,11... | collective-permute-start | bytes 1572872 | tf_op jit(solution)/shard_map/ppermute | solution.py:374
  21.5 16.3 %collective-permute-start.3 = (bf16[2,128,512]{2,1,0:T(8,128)(2,1)S(1)}, bf16[2,128,512]{2,1,0:T(8,128)(2,1)S(1)}, u32[]{:S(2)}, u32[]{:S(2)}) collective-permute-start(bf16[2,128,512]{2,1,0:T(8,128)(2,1)S(1)} %pad_maximum_fusion.12), channel_id=1, source_target_pairs={{0,4},{1,5},{2,6},{3,7},{4,0},{5,1},{6,2},{7,3},{8,12},{9,13},{10,... | collective-permute-start | bytes 786440 | tf_op jit(solution)/shard_map/ppermute | solution.py:374
  23.2 12.9 %collective-permute-start.1 = (bf16[1,192,512]{2,1,0:T(8,128)(2,1)S(1)}, bf16[1,192,512]{2,1,0:T(8,128)(2,1)S(1)}, u32[]{:S(2)}, u32[]{:S(2)}) collective-permute-start(bf16[1,192,512]{2,1,0:T(8,128)(2,1)S(1)} %get-tuple-element.62), channel_id=1, source_target_pairs={{0,8},{1,9},{2,10},{3,11},{4,12},{5,13},{6,14},{7,15},{8,0},{9,1},... | collective-permute-start | bytes 589832 | tf_op jit(solution)/shard_map/ppermute | solution.py:374
  28.5 21.2 %copy-start.21 = (bf16[512,8192]{1,0:T(8,128)(2,1)S(1)}, bf16[512,8192]{1,0:T(8,128)(2,1)}, u32[]{:S(2)}) copy-start(bf16[512,8192]{1,0:T(8,128)(2,1)} %refs_12_.5) | copy-start | bytes 25165828
  29.9 56.4 %copy-start.2 = (bf16[4096,1024]{1,0:T(8,128)(2,1)}, bf16[4096,1024]{1,0:T(8,128)(2,1)S(1)}, u32[]{:S(2)}) copy-start(bf16[4096,1024]{1,0:T(8,128)(2,1)S(1)} %reorder_weights.1) | copy-start | bytes 25165828
  36.1 12.0 %collective-permute-start.2 = (bf16[1,192,512]{2,1,0:T(8,128)(2,1)S(1)}, bf16[1,192,512]{2,1,0:T(8,128)(2,1)S(1)}, u32[]{:S(2)}, u32[]{:S(2)}) collective-permute-start(bf16[1,192,512]{2,1,0:T(8,128)(2,1)S(1)} %get-tuple-element.63), channel_id=1, source_target_pairs={{0,8},{1,9},{2,10},{3,11},{4,12},{5,13},{6,14},{7,15},{8,0},{9,1},... | collective-permute-start | bytes 589832 | tf_op jit(solution)/shard_map/ppermute | solution.py:374
  37.9 19.2 %slice-start.4 = ((s8[8388608]{0:T(1024)(128)(4,1)}), s8[4194304]{0:T(1024)(128)(4,1)S(1)}, s32[]{:S(2)}) async-start(s8[8388608]{0:T(1024)(128)(4,1)} %bitcast.200), calls=%async_computation.5 | async-start | bytes 8388608
  38.0 10.1 %collective-permute-start.6 = (bf16[2,128,512]{2,1,0:T(8,128)(2,1)S(1)}, bf16[2,128,512]{2,1,0:T(8,128)(2,1)S(1)}, u32[]{:S(2)}, u32[]{:S(2)}) collective-permute-start(bf16[2,128,512]{2,1,0:T(8,128)(2,1)S(1)} %maximum_select_fusion.3), channel_id=1, source_target_pairs={{0,16},{16,0},{1,17},{17,1},{2,18},{18,2},{3,19},{19,3},{4,20},{20... | collective-permute-start | bytes 786440 | tf_op jit(solution)/shard_map/ppermute | solution.py:377
  39.6 16.6 %collective-permute-start.4 = (bf16[2,192,512]{2,1,0:T(8,128)(2,1)S(1)}, bf16[2,192,512]{2,1,0:T(8,128)(2,1)S(1)}, u32[]{:S(2)}, u32[]{:S(2)}) collective-permute-start(bf16[2,192,512]{2,1,0:T(8,128)(2,1)S(1)} %pad_maximum_fusion.10), channel_id=1, source_target_pairs={{0,4},{1,5},{2,6},{3,7},{4,0},{5,1},{6,2},{7,3},{8,12},{9,13},{10,... | collective-permute-start | bytes 1179656 | tf_op jit(solution)/shard_map/ppermute | solution.py:374
  48.1 9.0 %slice-start.5 = ((s8[8388608]{0:T(1024)(128)(4,1)}), s8[4194304]{0:T(1024)(128)(4,1)S(1)}, s32[]{:S(2)}) async-start(s8[8388608]{0:T(1024)(128)(4,1)} %bitcast.200), calls=%async_computation.6 | async-start | bytes 8388608
  48.2 13.6 %collective-permute-start.12 = (bf16[2,2,128,512]{3,2,1,0:T(8,128)(2,1)S(1)}, bf16[2,2,128,512]{3,2,1,0:T(8,128)(2,1)S(1)}, u32[]{:S(2)}, u32[]{:S(2)}) collective-permute-start(bf16[2,2,128,512]{3,2,1,0:T(8,128)(2,1)S(1)} %get-tuple-element.122), channel_id=1, source_target_pairs={{0,2},{1,3},{2,0},{3,1},{4,6},{5,7},{6,4},{7,5},{8,10},{9,11},{10,... | collective-permute-start | bytes 1572872 | tf_op jit(solution)/shard_map/ppermute | solution.py:374
  56.3 9.4 %collective-permute-start.7 = (bf16[2,192,512]{2,1,0:T(8,128)(2,1)S(1)}, bf16[2,192,512]{2,1,0:T(8,128)(2,1)S(1)}, u32[]{:S(2)}, u32[]{:S(2)}) collective-permute-start(bf16[2,192,512]{2,1,0:T(8,128)(2,1)S(1)} %fusion.8), channel_id=1, source_target_pairs={{0,16},{16,0},{1,17},{17,1},{2,18},{18,2},{3,19},{19,3},{4,20},{20... | collective-permute-start | bytes 1179656 | tf_op jit(solution)/shard_map/ppermute | solution.py:377
  59.3 35.1 %collective-permute-start.10 = (bf16[512,4096]{1,0:T(8,128)(2,1)S(1)}, bf16[512,4096]{1,0:T(8,128)(2,1)}, u32[]{:S(2)}, u32[]{:S(2)}) collective-permute-start(bf16[512,4096]{1,0:T(8,128)(2,1)S(1)} %copy-done.25), channel_id=1, source_target_pairs={{0,1},{1,0},{2,3},{3,2},{4,5},{5,4},{6,7},{7,6},{8,9},{9,8},{10,11... | collective-permute-start | bytes 12582920 | tf_op jit(solution)/shard_map/ppermute | solution.py:374
  59.3 12.3 %collective-permute-start.5 = (bf16[2,192,512]{2,1,0:T(8,128)(2,1)S(1)}, bf16[2,192,512]{2,1,0:T(8,128)(2,1)S(1)}, u32[]{:S(2)}, u32[]{:S(2)}) collective-permute-start(bf16[2,192,512]{2,1,0:T(8,128)(2,1)S(1)} %pad_maximum_fusion.8), channel_id=1, source_target_pairs={{0,4},{1,5},{2,6},{3,7},{4,0},{5,1},{6,2},{7,3},{8,12},{9,13},{10,... | collective-permute-start | bytes 1179656 | tf_op jit(solution)/shard_map/ppermute | solution.py:374
  61.8 21.9 %collective-permute-start.13 = (bf16[2,2,2,128,512]{4,3,2,1,0:T(8,128)(2,1)S(1)}, bf16[2,2,2,128,512]{4,3,2,1,0:T(8,128)(2,1)S(1)}, u32[]{:S(2)}, u32[]{:S(2)}) collective-permute-start(bf16[2,2,2,128,512]{4,3,2,1,0:T(8,128)(2,1)S(1)} %pad_maximum_fusion.2), channel_id=1, source_target_pairs={{0,1},{1,0},{2,3},{3,2},{4,5},{5,4},{6,7},{7,6},{8,9},{9,8},{10,11... | collective-permute-start | bytes 3145736 | tf_op jit(solution)/shard_map/ppermute | solution.py:374
  65.8 17.7 %collective-permute-start.15 = (bf16[2,2,192,512]{3,2,1,0:T(8,128)(2,1)S(1)}, bf16[2,2,192,512]{3,2,1,0:T(8,128)(2,1)S(1)}, u32[]{:S(2)}, u32[]{:S(2)}) collective-permute-start(bf16[2,2,192,512]{3,2,1,0:T(8,128)(2,1)S(1)} %pad_maximum_fusion.3), channel_id=1, source_target_pairs={{0,2},{1,3},{2,0},{3,1},{4,6},{5,7},{6,4},{7,5},{8,10},{9,11},{10,... | collective-permute-start | bytes 2359304 | tf_op jit(solution)/shard_map/ppermute | solution.py:374
  71.8 10.8 %collective-permute-start.8 = (bf16[2,192,512]{2,1,0:T(8,128)(2,1)S(1)}, bf16[2,192,512]{2,1,0:T(8,128)(2,1)S(1)}, u32[]{:S(2)}, u32[]{:S(2)}) collective-permute-start(bf16[2,192,512]{2,1,0:T(8,128)(2,1)S(1)} %fusion.9), channel_id=1, source_target_pairs={{0,16},{16,0},{1,17},{17,1},{2,18},{18,2},{3,19},{19,3},{4,20},{20... | collective-permute-start | bytes 1179656 | tf_op jit(solution)/shard_map/ppermute | solution.py:377
  82.5 88.8 %collective-permute-start.25 = (bf16[512,4096]{1,0:T(8,128)(2,1)}, bf16[512,4096]{1,0:T(8,128)(2,1)}, u32[]{:S(2)}, u32[]{:S(2)}) collective-permute-start(bf16[512,4096]{1,0:T(8,128)(2,1)} %constant_dynamic-slice_fusion.4), channel_id=1, source_target_pairs={{0,1},{1,0},{2,3},{3,2},{4,5},{5,4},{6,7},{7,6},{8,9},{9,8},{10,11... | collective-permute-start | bytes 12582920 | tf_op jit(solution)/shard_map/ppermute | solution.py:374
  82.6 52.3 %copy-start.23 = (bf16[2,2,192,512]{3,2,1,0:T(8,128)(2,1)}, bf16[2,2,192,512]{3,2,1,0:T(8,128)(2,1)S(1)}, u32[]{:S(2)}) copy-start(bf16[2,2,192,512]{3,2,1,0:T(8,128)(2,1)S(1)} %pad_maximum_fusion.4) | copy-start | bytes 2359300
  83.6 8.3 %collective-permute-start.16 = (bf16[2,2,2,192,512]{4,3,2,1,0:T(8,128)(2,1)S(1)}, bf16[2,2,2,192,512]{4,3,2,1,0:T(8,128)(2,1)S(1)}, u32[]{:S(2)}, u32[]{:S(2)}) collective-permute-start(bf16[2,2,2,192,512]{4,3,2,1,0:T(8,128)(2,1)S(1)} %pad_maximum_fusion.1), channel_id=1, source_target_pairs={{0,1},{1,0},{2,3},{3,2},{4,5},{5,4},{6,7},{7,6},{8,9},{9,8},{10,11... | collective-permute-start | bytes 4718600 | tf_op jit(solution)/shard_map/ppermute | solution.py:374
  85.3 58.3 %collective-permute-start.14 = (bf16[128,1024]{1,0:T(8,128)(2,1)S(1)}, bf16[128,1024]{1,0:T(8,128)(2,1)S(1)}, u32[]{:S(2)}, u32[]{:S(2)}) collective-permute-start(bf16[128,1024]{1,0:T(8,128)(2,1)S(1)} %convolution_convert_fusion), channel_id=1, source_target_pairs={{0,16},{16,0},{1,17},{17,1},{2,18},{18,2},{3,19},{19,3},{4,20},{20... | collective-permute-start | bytes 786440 | tf_op jit(solution)/shard_map/ppermute | solution.py:377
  100.2 21.7 %collective-permute-start.11 = (bf16[2,2,192,512]{3,2,1,0:T(8,128)(2,1)S(1)}, bf16[2,2,192,512]{3,2,1,0:T(8,128)(2,1)S(1)}, u32[]{:S(2)}, u32[]{:S(2)}) collective-permute-start(bf16[2,2,192,512]{3,2,1,0:T(8,128)(2,1)S(1)} %pad_maximum_fusion.4), channel_id=1, source_target_pairs={{0,2},{1,3},{2,0},{3,1},{4,6},{5,7},{6,4},{7,5},{8,10},{9,11},{10,... | collective-permute-start | bytes 2359304 | tf_op jit(solution)/shard_map/ppermute | solution.py:374
  122.0 8.5 %copy-start.26 = (bf16[2,2,192,512]{3,2,1,0:T(8,128)(2,1)}, bf16[2,2,192,512]{3,2,1,0:T(8,128)(2,1)S(1)}, u32[]{:S(2)}) copy-start(bf16[2,2,192,512]{3,2,1,0:T(8,128)(2,1)S(1)} %collective-permute-done.11) | copy-start | bytes 2359300
  122.0 8.5 %slice-start = ((s8[8388608]{0:T(1024)(128)(4,1)}), s8[4194304]{0:T(1024)(128)(4,1)S(1)}, s32[]{:S(2)}) async-start(s8[8388608]{0:T(1024)(128)(4,1)} %bitcast.180), calls=%async_computation.1 | async-start | bytes 8388608
  123.3 23.1 %collective-permute-start.18 = (bf16[2,2,2,192,512]{4,3,2,1,0:T(8,128)(2,1)}, bf16[2,2,2,192,512]{4,3,2,1,0:T(8,128)(2,1)}, u32[]{:S(2)}, u32[]{:S(2)}) collective-permute-start(bf16[2,2,2,192,512]{4,3,2,1,0:T(8,128)(2,1)} %pad_maximum_fusion), channel_id=1, source_target_pairs={{0,1},{1,0},{2,3},{3,2},{4,5},{5,4},{6,7},{7,6},{8,9},{9,8},{10,11... | collective-permute-start | bytes 4718600 | tf_op jit(solution)/shard_map/ppermute | solution.py:374
  133.8 11.8 %collective-permute-start.17 = (bf16[192,1024]{1,0:T(8,128)(2,1)}, bf16[192,1024]{1,0:T(8,128)(2,1)S(1)}, u32[]{:S(2)}, u32[]{:S(2)}) collective-permute-start(bf16[192,1024]{1,0:T(8,128)(2,1)} %fusion.4), channel_id=1, source_target_pairs={{0,16},{16,0},{1,17},{17,1},{2,18},{18,2},{3,19},{19,3},{4,20},{20... | collective-permute-start | bytes 1179656 | tf_op jit(solution)/shard_map/ppermute | solution.py:377
  138.4 31.2 %collective-permute-start.20 = (bf16[4,64,1024]{2,1,0:T(8,128)(2,1)}, bf16[4,64,1024]{2,1,0:T(8,128)(2,1)S(1)}, u32[]{:S(2)}, u32[]{:S(2)}) collective-permute-start(bf16[4,64,1024]{2,1,0:T(8,128)(2,1)} %get-tuple-element.83), channel_id=1, source_target_pairs={{0,2},{1,3},{2,0},{3,1},{4,6},{5,7},{6,4},{7,5},{8,10},{9,11},{10,... | collective-permute-start | bytes 1572872 | tf_op jit(solution)/shard_map/ppermute | solution.py:374
  141.6 9.6 %slice-start.2 = ((s8[8388608]{0:T(1024)(128)(4,1)}), s8[4194304]{0:T(1024)(128)(4,1)S(1)}, s32[]{:S(2)}) async-start(s8[8388608]{0:T(1024)(128)(4,1)} %bitcast.182), calls=%async_computation.3 | async-start | bytes 8388608
  144.2 24.9 %copy-start.5 = (bf16[128,512]{1,0:T(8,128)(2,1)}, bf16[128,512]{1,0:T(8,128)(2,1)S(1)}, u32[]{:S(2)}) copy-start(bf16[128,512]{1,0:T(8,128)(2,1)S(1)} %get-tuple-element.74.refs_0_) | copy-start | bytes 393220
  146.4 22.8 %copy-start.6 = (bf16[128,512]{1,0:T(8,128)(2,1)}, bf16[128,512]{1,0:T(8,128)(2,1)S(1)}, u32[]{:S(2)}) copy-start(bf16[128,512]{1,0:T(8,128)(2,1)S(1)} %get-tuple-element.78.refs_1_) | copy-start | bytes 393220
  153.1 10.8 %collective-permute-start.19 = (bf16[192,1024]{1,0:T(8,128)(2,1)S(1)}, bf16[192,1024]{1,0:T(8,128)(2,1)S(1)}, u32[]{:S(2)}, u32[]{:S(2)}) collective-permute-start(bf16[192,1024]{1,0:T(8,128)(2,1)S(1)} %fusion.5), channel_id=1, source_target_pairs={{0,16},{16,0},{1,17},{17,1},{2,18},{18,2},{3,19},{19,3},{4,20},{20... | collective-permute-start | bytes 1179656 | tf_op jit(solution)/shard_map/ppermute | solution.py:377
  166.4 1.2 collective-permute-start.27
  167.6 3.7 %collective-permute-start.28 = (f32[4,128]{1,0:T(4,128)S(1)}, f32[4,128]{1,0:T(4,128)S(1)}, u32[]{:S(2)}, u32[]{:S(2)}) collective-permute-start(f32[4,128]{1,0:T(4,128)S(1)} %fusion.44), channel_id=1, source_target_pairs={{0,2},{1,3},{2,0},{3,1},{4,6},{5,7},{6,4},{7,5},{8,10},{9,11},{10,... | collective-permute-start | bytes 6152 | tf_op jit(solution)/shard_map/ppermute | solution.py:374
  169.1 2.2 collective-permute-start.21
  169.1 2.2 collective-permute-start.22
  170.4 1.3 collective-permute-start.24
  171.3 1.3 collective-permute-start.23
  178.4 3.7 %collective-permute-start.29 = (f32[4,128]{1,0:T(4,128)S(1)}, f32[4,128]{1,0:T(4,128)S(1)}, u32[]{:S(2)}, u32[]{:S(2)}) collective-permute-start(f32[4,128]{1,0:T(4,128)S(1)} %fusion.55), channel_id=1, source_target_pairs={{0,4},{1,5},{2,6},{3,7},{4,0},{5,1},{6,2},{7,3},{8,12},{9,13},{10,... | collective-permute-start | bytes 6152 | tf_op jit(solution)/shard_map/ppermute | solution.py:374
  182.1 4.5 %collective-permute-start.30 = (f32[4,128]{1,0:T(4,128)S(1)}, f32[4,128]{1,0:T(4,128)S(1)}, u32[]{:S(2)}, u32[]{:S(2)}) collective-permute-start(f32[4,128]{1,0:T(4,128)S(1)} %add.101), channel_id=1, source_target_pairs={{0,8},{1,9},{2,10},{3,11},{4,12},{5,13},{6,14},{7,15},{8,0},{9,1},... | collective-permute-start | bytes 6152 | tf_op jit(solution)/shard_map/ppermute | solution.py:374
  182.1 30.7 %collective-permute-start.26 = (bf16[4,64,1024]{2,1,0:T(8,128)(2,1)}, bf16[4,64,1024]{2,1,0:T(8,128)(2,1)}, u32[]{:S(2)}, u32[]{:S(2)}) collective-permute-start(bf16[4,64,1024]{2,1,0:T(8,128)(2,1)} %get-tuple-element.86), channel_id=1, source_target_pairs={{0,2},{1,3},{2,0},{3,1},{4,6},{5,7},{6,4},{7,5},{8,10},{9,11},{10,... | collective-permute-start | bytes 1572872 | tf_op jit(solution)/shard_map/ppermute | solution.py:374
  194.5 21.5 %collective-permute-start.32 = (bf16[4,64,1024]{2,1,0:T(8,128)(2,1)}, bf16[4,64,1024]{2,1,0:T(8,128)(2,1)}, u32[]{:S(2)}, u32[]{:S(2)}) collective-permute-start(bf16[4,64,1024]{2,1,0:T(8,128)(2,1)} %get-tuple-element.97), channel_id=1, source_target_pairs={{0,2},{1,3},{2,0},{3,1},{4,6},{5,7},{6,4},{7,5},{8,10},{9,11},{10,... | collective-permute-start | bytes 1572872 | tf_op jit(solution)/shard_map/ppermute | solution.py:374
  203.2 9.6 %copy-start.9 = (f32[4,64,1024]{2,1,0:T(8,128)S(1)}, f32[4,64,1024]{2,1,0:T(8,128)}, u32[]{:S(2)}) copy-start(f32[4,64,1024]{2,1,0:T(8,128)} %get-tuple-element.92.refs_1_) | copy-start | bytes 3145732
  203.2 9.6 %copy-start.10 = (f32[4,64,1024]{2,1,0:T(8,128)S(1)}, f32[4,64,1024]{2,1,0:T(8,128)}, u32[]{:S(2)}) copy-start(f32[4,64,1024]{2,1,0:T(8,128)} %get-tuple-element.85.keep_ref) | copy-start | bytes 3145732
  203.2 30.3 %collective-permute-start.37 = (bf16[4,64,1024]{2,1,0:T(8,128)(2,1)}, bf16[4,64,1024]{2,1,0:T(8,128)(2,1)}, u32[]{:S(2)}, u32[]{:S(2)}) collective-permute-start(bf16[4,64,1024]{2,1,0:T(8,128)(2,1)} %get-tuple-element.109), channel_id=1, source_target_pairs={{0,2},{1,3},{2,0},{3,1},{4,6},{5,7},{6,4},{7,5},{8,10},{9,11},{10,... | collective-permute-start | bytes 1572872 | tf_op jit(solution)/shard_map/ppermute | solution.py:374
  210.9 18.2 %collective-permute-start.34 = (bf16[4,64,1024]{2,1,0:T(8,128)(2,1)}, bf16[4,64,1024]{2,1,0:T(8,128)(2,1)}, u32[]{:S(2)}, u32[]{:S(2)}) collective-permute-start(bf16[4,64,1024]{2,1,0:T(8,128)(2,1)} %get-tuple-element.102), channel_id=1, source_target_pairs={{0,2},{1,3},{2,0},{3,1},{4,6},{5,7},{6,4},{7,5},{8,10},{9,11},{10,... | collective-permute-start | bytes 1572872 | tf_op jit(solution)/shard_map/ppermute | solution.py:374
  213.8 18.5 %copy-start.13 = (f32[4,64,1024]{2,1,0:T(8,128)S(1)}, f32[4,64,1024]{2,1,0:T(8,128)}, u32[]{:S(2)}) copy-start(f32[4,64,1024]{2,1,0:T(8,128)} %get-tuple-element.101.keep_ref) | copy-start | bytes 3145732
  215.2 19.2 %copy-start.11 = (f32[4,64,1024]{2,1,0:T(8,128)S(1)}, f32[4,64,1024]{2,1,0:T(8,128)}, u32[]{:S(2)}) copy-start(f32[4,64,1024]{2,1,0:T(8,128)} %get-tuple-element.108.keep_ref) | copy-start | bytes 3145732
  215.2 9.5 %collective-permute-start.31 = (bf16[2,64,1024]{2,1,0:T(8,128)(2,1)S(1)}, bf16[2,64,1024]{2,1,0:T(8,128)(2,1)S(1)}, u32[]{:S(2)}, u32[]{:S(2)}) collective-permute-start(bf16[2,64,1024]{2,1,0:T(8,128)(2,1)S(1)} %get-tuple-element.94), channel_id=1, source_target_pairs={{0,4},{1,5},{2,6},{3,7},{4,0},{5,1},{6,2},{7,3},{8,12},{9,13},{10,... | collective-permute-start | bytes 786440 | tf_op jit(solution)/shard_map/ppermute | solution.py:374
  217.1 10.9 %collective-permute-start.33 = (bf16[2,64,1024]{2,1,0:T(8,128)(2,1)S(1)}, bf16[2,64,1024]{2,1,0:T(8,128)(2,1)S(1)}, u32[]{:S(2)}, u32[]{:S(2)}) collective-permute-start(bf16[2,64,1024]{2,1,0:T(8,128)(2,1)S(1)} %get-tuple-element.99), channel_id=1, source_target_pairs={{0,4},{1,5},{2,6},{3,7},{4,0},{5,1},{6,2},{7,3},{8,12},{9,13},{10,... | collective-permute-start | bytes 786440 | tf_op jit(solution)/shard_map/ppermute | solution.py:374
  224.7 29.5 %copy-start.20 = (s32[3]{0:T(128)S(1)}, s32[3]{0:T(128)}, u32[]{:S(2)}) copy-start(s32[3]{0:T(128)} %pad_add_fusion.spot_ref) | copy-start | bytes 40
  224.8 7.5 %collective-permute-start.35 = (bf16[64,1024]{1,0:T(8,128)(2,1)S(1)}, bf16[64,1024]{1,0:T(8,128)(2,1)S(1)}, u32[]{:S(2)}, u32[]{:S(2)}) collective-permute-start(bf16[64,1024]{1,0:T(8,128)(2,1)S(1)} %bitcast.197), channel_id=1, source_target_pairs={{0,8},{1,9},{2,10},{3,11},{4,12},{5,13},{6,14},{7,15},{8,0},{9,1},... | collective-permute-start | bytes 393224 | tf_op jit(solution)/shard_map/ppermute | solution.py:374
  228.1 6.3 %collective-permute-start.38 = (bf16[64,1024]{1,0:T(8,128)(2,1)S(1)}, bf16[64,1024]{1,0:T(8,128)(2,1)S(1)}, u32[]{:S(2)}, u32[]{:S(2)}) collective-permute-start(bf16[64,1024]{1,0:T(8,128)(2,1)S(1)} %bitcast.196), channel_id=1, source_target_pairs={{0,8},{1,9},{2,10},{3,11},{4,12},{5,13},{6,14},{7,15},{8,0},{9,1},... | collective-permute-start | bytes 393224 | tf_op jit(solution)/shard_map/ppermute | solution.py:374
  233.4 9.5 %collective-permute-start.36 = (bf16[2,64,1024]{2,1,0:T(8,128)(2,1)S(1)}, bf16[2,64,1024]{2,1,0:T(8,128)(2,1)S(1)}, u32[]{:S(2)}, u32[]{:S(2)}) collective-permute-start(bf16[2,64,1024]{2,1,0:T(8,128)(2,1)S(1)} %get-tuple-element.106), channel_id=1, source_target_pairs={{0,4},{1,5},{2,6},{3,7},{4,0},{5,1},{6,2},{7,3},{8,12},{9,13},{10,... | collective-permute-start | bytes 786440 | tf_op jit(solution)/shard_map/ppermute | solution.py:374
  234.4 22.9 %copy-start.1 = (bf16[512,384]{1,0:T(8,128)(2,1)S(1)}, bf16[512,384]{1,0:T(8,128)(2,1)}, u32[]{:S(2)}) copy-start(bf16[512,384]{1,0:T(8,128)(2,1)} %param.18) | copy-start | bytes 1179652
  235.6 10.4 %collective-permute-start.39 = (bf16[2,64,1024]{2,1,0:T(8,128)(2,1)S(1)}, bf16[2,64,1024]{2,1,0:T(8,128)(2,1)S(1)}, u32[]{:S(2)}, u32[]{:S(2)}) collective-permute-start(bf16[2,64,1024]{2,1,0:T(8,128)(2,1)S(1)} %get-tuple-element.113), channel_id=1, source_target_pairs={{0,4},{1,5},{2,6},{3,7},{4,0},{5,1},{6,2},{7,3},{8,12},{9,13},{10,... | collective-permute-start | bytes 786440 | tf_op jit(solution)/shard_map/ppermute | solution.py:374
  242.9 9.9 %collective-permute-start.40 = (bf16[64,1024]{1,0:T(8,128)(2,1)S(1)}, bf16[64,1024]{1,0:T(8,128)(2,1)S(1)}, u32[]{:S(2)}, u32[]{:S(2)}) collective-permute-start(bf16[64,1024]{1,0:T(8,128)(2,1)S(1)} %bitcast.198), channel_id=1, source_target_pairs={{0,8},{1,9},{2,10},{3,11},{4,12},{5,13},{6,14},{7,15},{8,0},{9,1},... | collective-permute-start | bytes 393224 | tf_op jit(solution)/shard_map/ppermute | solution.py:374
  246.1 8.1 %collective-permute-start.41 = (bf16[64,1024]{1,0:T(8,128)(2,1)S(1)}, bf16[64,1024]{1,0:T(8,128)(2,1)S(1)}, u32[]{:S(2)}, u32[]{:S(2)}) collective-permute-start(bf16[64,1024]{1,0:T(8,128)(2,1)S(1)} %bitcast.199), channel_id=1, source_target_pairs={{0,8},{1,9},{2,10},{3,11},{4,12},{5,13},{6,14},{7,15},{8,0},{9,1},... | collective-permute-start | bytes 393224 | tf_op jit(solution)/shard_map/ppermute | solution.py:374
  254.9 1.6 collective-permute-start.42
  (24 other events, 78.4 us)
Sparse Core Ops, SparseCore 0:
  25.0 98.2 all-reduce.1

commit v3 on v2

--- a/solution.py
+++ b/solution.py
@@ -11,12 +11,13 @@
 SHEAD = 64
 STATE = 128
 LANES = 128
-OUT_CHUNKS = 4
-SPLIT = (2, 3, 3)
+OUT_SPLIT = (1, 1, 1, 1)
+SPLIT = (1, 1)
 HINT = 16
 OUT_TILE = 512
 SMALL = 8 * 1024 * 1024
 MIDDLE = 14 * 1024 * 1024
+WIDE = 50 * 1024 * 1024
 LARGE = 58 * 1024 * 1024
 
 norm_eps = 1e-05
@@ -39,26 +40,88 @@
     return chosen
 
 
-def reorder_weights(mixer_in, block, spot):
-    kinds, rows, channels = mixer_in.shape
-
-    def body(spot_ref, source, target):
-        for k in range(kinds):
-            target[:, k * channels : (k + 1) * channels] = source[k]
+def begin(hidden_in, shared_in, sizes):
+    length, block = hidden_in.shape
+
+    def body(hidden_ref, shared_ref, part_ref, *chunk_refs):
+        at = 0
+        for size, ref in zip(sizes, chunk_refs):
+            ref[...] = hidden_ref[at : at + size]
+            at += size
+        part_ref[...] = jnp.dot(hidden_ref[...], shared_ref[...], preferred_element_type=f32)
 
     return pl.pallas_call(
         body,
-        grid_spec=pltpu.PrefetchScalarGridSpec(
-            num_scalar_prefetch=1,
-            grid=(rows // block,),
-            in_specs=[pl.BlockSpec((kinds, block, channels), lambda r, s: (0, s[0] ^ r, 0))],
-            out_specs=pl.BlockSpec((block, kinds * channels), lambda r, s: (r, 0)),
+        out_shape=(
+            jax.ShapeDtypeStruct((length, shared_in.shape[1]), f32),
+            *(jax.ShapeDtypeStruct((size, block), bf16) for size in sizes),
         ),
-        out_shape=jax.ShapeDtypeStruct((rows, kinds * channels), mixer_in.dtype),
         compiler_params=pltpu.CompilerParams(vmem_limit_bytes=SMALL),
-        cost_estimate=cost(0, 4 * mixer_in.size),
-        name="reorder_weights",
-    )(spot, mixer_in)
+        cost_estimate=cost(2 * hidden_in.size * shared_in.shape[1], 4 * hidden_in.size),
+        name="begin",
+    )(hidden_in, shared_in)
+
+
+def project_in(spot, features, weights):
+    ndp = len(features[0])
+    group, size, block = features[0][0].shape
+    kinds, _, channels = weights.shape
+    places = [(m, k) for m in range(len(features)) for k in range(group)]
+    given = len(features) * ndp
+    shape = (ndp * size, kinds * channels)
+
+    def body(spot_ref, *refs):
+        weights_ref = refs[given]
+        tokens_ref, rows_ref, done = refs[-3:]
+        copies = []
+        for n, (m, k) in enumerate(places):
+            row = pl.multiple_of((spot_ref[0] ^ (k * len(features) + m)) * block, block)
+            for kind in range(kinds):
+                copies.append(
+                    pltpu.make_async_copy(
+                        weights_ref.at[kind, pl.ds(row, block)],
+                        rows_ref.at[kind, pl.ds(n * block, block)],
+                        done.at[n * kinds + kind],
+                    )
+                )
+        for copy in copies:
+            copy.start()
+        for n, (m, k) in enumerate(places):
+            for d in range(ndp):
+                tokens_ref[d * size : (d + 1) * size, n * block : (n + 1) * block] = refs[
+                    m * ndp + d
+                ][k]
+        for copy in copies:
+            copy.wait()
+        for kind in range(kinds):
+            lane = slice(kind * channels, (kind + 1) * channels)
+            total = jnp.dot(tokens_ref[...], rows_ref[kind], preferred_element_type=f32)
+            for d in range(ndp):
+                out = refs[given + 1 + d]
+                out[:, lane] = total[d * size : (d + 1) * size].astype(out.dtype)
+
+    vmem = pl.BlockSpec(memory_space=pltpu.VMEM)
+    outs = [
+        jax.ShapeDtypeStruct((size, shape[1]), f32 if d == 0 else bf16) for d in range(ndp)
+    ]
+    deep = len(places) * block
+    found = pl.pallas_call(
+        body,
+        in_specs=[pl.BlockSpec(memory_space=pltpu.SMEM)]
+        + [vmem] * given
+        + [pl.BlockSpec(memory_space=pltpu.HBM)],
+        out_specs=[vmem] * len(outs),
+        out_shape=outs,
+        scratch_shapes=[
+            pltpu.VMEM((ndp * size, deep), bf16),
+            pltpu.VMEM((kinds, deep, channels), bf16),
+            pltpu.SemaphoreType.DMA((len(places) * kinds,)),
+        ],
+        compiler_params=pltpu.CompilerParams(vmem_limit_bytes=WIDE),
+        cost_estimate=cost(2 * deep * shape[0] * shape[1], 2 * deep * shape[1] + 6 * shape[0] * shape[1]),
+        name="project_in",
+    )(spot, *(a for way in features for a in way), weights)
+    return list(found)
 
 
 def attention(queries, key_rows, value_rows, kv_head):
@@ -216,7 +279,7 @@
     pieces = [p for pair in sets for group in pair for p in group]
     channels = here[0].shape[1]
     length = sum(p.shape[0] for p in here)
-    half = weight_there.shape[1]
+    half = weight_there.shape[1] // 2
     tile = min(OUT_TILE, width)
     steps = width // tile
     part = length // (2 * far)
@@ -230,7 +293,7 @@
         copies = []
         for t in range(steps):
             for m, ref in enumerate(weight_refs):
-                column = (own if m % 2 == 0 else at) + t * tile
+                column = own + t * tile
                 copies.append(
                     pltpu.make_async_copy(
                         ref.at[:, pl.ds(pl.multiple_of(column, LANES), tile)],
@@ -285,7 +348,7 @@
             pltpu.VMEM((steps * len(weights), channels, tile), bf16),
             pltpu.SemaphoreType.DMA((steps * len(weights),)),
         ],
-        compiler_params=pltpu.CompilerParams(vmem_limit_bytes=LARGE),
+        compiler_params=pltpu.CompilerParams(vmem_limit_bytes=LARGE if teacher else WIDE),
         cost_estimate=cost(
             2 * len(weights) * length * channels * width,
             2 * len(weights) * channels * width + 6 * length * width,
@@ -323,9 +386,10 @@
 
 
 def finish(spots, kept, came):
-    rows, width = kept[0].shape
-    rows //= 2
+    rows = kept[0].shape[0] // 2
     count = len(kept)
+    starts = [sum(a.shape[1] for a in kept[:n]) for n in range(count + 1)]
+    width = starts[count]
 
     def body(spot_ref, *refs):
         own_ref, other_ref = refs[-2:]
@@ -333,7 +397,7 @@
         for n in range(count):
             total = (refs[n][...] + refs[count + n][...].astype(f32)).astype(bf16)
             low, high = total[:rows], total[rows:]
-            lane = slice(n * width, (n + 1) * width)
+            lane = slice(starts[n], starts[n + 1])
             own_ref[:, lane] = jnp.where(core == 0, low, high)
             other_ref[:, lane] = jnp.where(core == 0, high, low)
 
@@ -341,9 +405,9 @@
         body,
         in_specs=[pl.BlockSpec(memory_space=pltpu.SMEM)]
         + [pl.BlockSpec(memory_space=pltpu.VMEM)] * (2 * count),
-        out_shape=(jax.ShapeDtypeStruct((rows, count * width), bf16),) * 2,
+        out_shape=(jax.ShapeDtypeStruct((rows, width), bf16),) * 2,
         compiler_params=pltpu.CompilerParams(vmem_limit_bytes=SMALL),
-        cost_estimate=cost(kept[0].size * count, 8 * kept[0].size * count),
+        cost_estimate=cost(rows * 2 * width, 16 * rows * width),
         name="finish",
     )(spots, *kept, *came)
 
@@ -385,13 +449,14 @@
     def at(source, index):
         return lax.dynamic_index_in_dim(source, index, 0, False)
 
+    sizes = [length * share // sum(SPLIT) for share in SPLIT]
+    ends = [sum(sizes[: n + 1]) for n in range(len(sizes))]
+    shared, *chunks = begin(hidden_in, shared_in, sizes)
+    half = mixer_out.shape[1] // 2
+    widths = [half * share // sum(OUT_SPLIT) for share in OUT_SPLIT]
     head_count = queries.shape[1] // HEAD
     kv_heads = key_rows.shape[1] // HEAD
     kv_head = (me * head_count // (head_count * nmp // kv_heads)).astype(jnp.int32).reshape(1)
-    context = attention(queries, key_rows, value_rows, kv_head)
-
-    shared = lax.psum(jnp.dot(hidden_in, shared_in, preferred_element_type=f32), "mp")
-
     turn = (z // group) ^ seq
     spot = (me % (4 * group)).astype(jnp.int32).reshape(1)
     distances = [0]
@@ -400,64 +465,78 @@
         distances += [d + k for d in distances]
         k //= 2
     order = [distances.index(d) for d in range(far)]
-    sizes = [length * share // sum(SPLIT) for share in SPLIT]
-    ends = [sum(sizes[: n + 1]) for n in range(len(sizes))]
     before = {}
 
     def in_turn(step, value):
         return after(value, before[step]) if step in before else value
 
-    half = mixer_out.shape[1] // 2
-    width = half // OUT_CHUNKS
-
-    def half_sent(weight):
-        return lax.dynamic_slice_in_dim(weight, (1 - core) * half, half, 1)
-
-    weights_in = None
-    projected = []
+    def fold(value, k, bit):
+        value = value.reshape(2, value.shape[0] // 2, -1)
+        return at(value, bit) + swap(at(value, 1 - bit), k)
+
+    def unfold(value, k, bit):
+        came = swap(value, k)
+        return jnp.concatenate([jnp.where(bit == 0, value, came), jnp.where(bit == 0, came, value)])
+
+    shared = fold(shared, 1, core)
+    teacher_there, mixer_there = (
+        swap(after(weight, shared), 1) for weight in (teacher_proj, mixer_out)
+    )
+    bits = [1 << e for e in range(far.bit_length() - 1)]
+    context = attention(queries, key_rows, value_rows, kv_head)
+    teacher = ([context], [swap(context, 1)], teacher_proj, teacher_there)
+    projected, aways, squares_in = [], [], []
+    last = len(sizes) - 1
     for n, size in enumerate(sizes):
-        line = [hidden_in[ends[n] - size : ends[n]]]
+        line = [chunks[n]]
         k = far // 2
         while k:
             packed = in_turn(k, jnp.stack(line))
             if n == 0 and k == 1:
                 packed = after(packed, context)
-            came = before[k] = swap(packed, 4 * k)
-            line = line + [came[m] for m in range(len(line))]
+            near = before[k] = swap(packed, 4 * k)
+            if k == far // 2:
+                front = near
+            line = line + [near[m] for m in range(len(line))]
             k //= 2
         line = [line[m] for m in order]
         line = [jnp.stack(line[m * group : (m + 1) * group]) for m in range(ndp)]
         square = [pick(line, turn ^ d) for d in range(ndp)]
         away = in_turn("dp", tuple(square[1:]))
-        square = before["dp"] = jnp.stack(
-            [square[0]] + [cross(away[d - 1], d) for d in range(1, ndp)], 1
-        )
-        if weights_in is None:
-            weights_in = reorder_weights(after(mixer_in, line[0]), block, spot)
+        if n == 1:
+            away = after(away, teacher_there, mixer_there)
         if n == 0:
-            sent = [half_sent(after(weight, square)) for weight in (teacher_proj, mixer_out)]
+            shared = fold(after(shared, front), 2, y)
+        square = [square[0]] + [cross(away[d - 1], d) for d in range(1, ndp)]
+        before["dp"] = square[1:]
         if n == 1:
-            square = after(square, *sent)
-            teacher_there, mixer_there = (swap(weight, 1) for weight in sent)
-            teacher = ([context], [swap(context, 1)], teacher_proj, teacher_there)
-            first = project_out(0, width, (spots, far), *teacher)
-        if n == len(sizes) - 1:
-            square = after(square, first[1])
-        both = jnp.stack([square, swap(square, 2)])
-        all_four = [both, swap(both, 1)]
-        features = jnp.concatenate(
-            [all_four[c][b][k] for k in range(group) for b in range(2) for c in range(2)],
-            axis=-1,
-        )
-        found = [
-            cross(jnp.dot(features[d], weights_in, preferred_element_type=f32).astype(bf16), d)
-            for d in range(1, ndp)
-        ]
-        projected.append([jnp.dot(features[0], weights_in, preferred_element_type=f32)] + found)
-
-    first_came = swap(after(first[1], both), 2)
-
-    shared = after(shared, both)
+            shared = after(shared, front)
+            for k in reversed(bits[1:]):
+                shared = fold(shared, 4 * k, (z // k) % 2)
+            shared = unfold(fold(after(shared, near), 4, z % 2), 4, z % 2)
+            for k in bits[1:]:
+                shared = unfold(shared, 4 * k, (z // k) % 2)
+        aways.append(away)
+        squares_in.append(square)
+    for n, square in enumerate(squares_in):
+        came = []
+        for d in range(ndp):
+            sent = in_turn(("y", d), square[d])
+            if n == last and d == 0:
+                first = project_out(0, widths[0], (spots, far), *teacher)
+            if n == last and d == 1:
+                sent = after(sent, *found)
+            came.append(swap(sent, 2))
+            before["y", d] = came[d]
+        if n == last:
+            shared = unfold(unfold(after(shared, came[0]), 2, y), 1, core)
+        if n < last:
+            came = list(after(tuple(came), *aways[n + 1]))
+        ways = square, [swap(after(a, came[0]), 1) for a in square], came, [swap(a, 1) for a in came]
+        found = project_in(spot, ways, mixer_in)
+        projected.append([found[0]] + [cross(found[d], d) for d in range(1, ndp)])
+    first_came = swap(after(first[1], came), 2)
+
     dt_raw = lax.dynamic_slice_in_dim(shared, 2 * STATE + me * heads, heads, 1)
     step_size = jax.nn.softplus(dt_raw + dt_bias)
     log_decay = -step_size * jnp.exp(a_log)
@@ -483,7 +562,7 @@
         squares.append(squares_n)
     weights = (gated, gated_other, mixer_out, mixer_there)
     gated[-1] = after(gated[-1], first_came)
-    keep, send = project_out(0, width, (spots, far), *weights)
+    keep, send = project_out(0, widths[0], (spots, far), *weights)
     squares = jnp.concatenate(squares)
     k = 1
     while k < nmp:
@@ -495,11 +574,13 @@
     scale_kept = jnp.stack([at(at(scale, z ^ k), y) for k in range(far)])
 
     done, far_came = [], []
-    for n in range(OUT_CHUNKS):
+    for n, width in enumerate(widths):
         if n == 0:
             keep, send = add_near(keep, swap(send, 2), scale_kept, first[0], first_came)
         else:
-            keep, send = project_out(n * width, width, (spots, far), *weights, scale, *teacher)
+            keep, send = project_out(
+                sum(widths[:n]), width, (spots, far), *weights, scale, *teacher
+            )
             came = swap(send, 2)
             if n >= 2:
                 came = after(came, far_came[n - 2])

time: 265 us -> 239 us (0.902)
  Pallas kernels: 51.3 us -> 71.6 us
  matrix products: 19.4 us -> 0.45 us
  local copies, waits for them, and re-layouts: 33.1 us -> 18.4 us
  between operations: 14.4 us -> 0.77 us
  waiting for transfers between devices: 102 us -> 89 us
  starting transfers between devices: 39.2 us -> 47.9 us
  other arithmetic: 4.67 us -> 9.18 us
    ppermute x6 -> x4, waiting for transfers between devices: 21.6 us -> 0.01 us  [cross(): return lax.ppermute(source, 'dp', [(s, s ^ k) for s in range(ndp)])]
    pallas_call x1 -> x3, Pallas kernels: 1.34 us -> 21.9 us  [the longest x2 21.4 us: project_in(): pl.pallas_call(body, in_specs=[pl.BlockSpec(memory_space=pltpu.SMEM)] + [...]
    dot_general x7 -> x0, matrix products: 18.2 us -> none  [the longest x3 10.4 us: local(): jnp.dot(features[d], weights_in, preferred_element_type=f32).astype(bf16)]
    ppermute x37 -> x49, starting transfers between devices: 32.3 us -> 42.9 us  [swap(): return lax.ppermute(source, 'mp', [(s, s ^ k) for s in range(nmp)])]
    ppermute x37 -> x49, waiting for transfers between devices: 80.4 us -> 89 us  [swap(): return lax.ppermute(source, 'mp', [(s, s ^ k) for s in range(nmp)])]
    unnamed x107 -> x78, local copies, waits for them, and re-layouts: 21.5 us -> 14.4 us
    dynamic_slice x2 -> x0, local copies, waits for them, and re-layouts: 4.55 us -> none  [half_sent(): return lax.dynamic_slice_in_dim(weight, (1 - core) * half, half, 1)]
    select_n x0 -> x5, other arithmetic: none -> 4.13 us  [the longest x4 3.32 us: unfold(): jnp.where(bit == 0, value, came)]
  transfers between devices with their start and end apart: 44 -> 53, of which waited for: 27 -> 24; matrix products, arithmetic and copies ran while one was open for 17% -> 5% of each run, Pallas kernels for 17% -> 28%
where the time goes in v3:
time: 239 us; the launch traced here: 237 us
  waiting for transfers between devices  89 us (37%)
  Pallas kernels  71.6 us (30%)
  starting transfers between devices  47.9 us (20%)
  local copies, waits for them, and re-layouts  18.4 us (8%)
  other arithmetic  9.18 us (4%)
    ppermute x49, waiting for transfers between devices, swap(): return lax.ppermute(source, 'mp', [(s, s ^ k) for s in range(nmp)])  89 us
    ppermute x49, starting transfers between devices, swap(): return lax.ppermute(source, 'mp', [(s, s ^ k) for s in range(nmp)])  42.9 us
    pallas_call x5, Pallas kernels, project_out(): pl.pallas_call(body, in_specs=[pl.BlockSpec(memory_space=pltpu.SMEM)] + [...  29 us
    pallas_call x2, Pallas kernels, project_in(): pl.pallas_call(body, in_specs=[pl.BlockSpec(memory_space=pltpu.SMEM)] + [...  21.4 us
    unnamed x78, local copies, waits for them, and re-layouts  14.4 us
    pallas_call x1, Pallas kernels, attention(): pl.pallas_call(body, grid_spec=pltpu.PrefetchScalarGridSpec(num_scalar_pr...  6.2 us
    pallas_call x4, Pallas kernels, scan_chunk(): pl.pallas_call(body, out_shape=(jax.ShapeDtypeStruct((pairs, wide, 2 * LA...  6.09 us
    ppermute x4, starting transfers between devices, cross(): return lax.ppermute(source, 'dp', [(s, s ^ k) for s in range(ndp)])  4.94 us
  transfers between devices with their start and end apart: 53, of which 24 were waited for; matrix products, arithmetic and copies ran while one was open for 5% of the time, Pallas kernels for 28%

profile of v3, /device:TPU:0, one launch (start us, length us, event | category | flops | bytes accessed | tf_op | source)
XLA Modules:
  0.0 237.2 jit_solution(557964063225047547)
XLA Ops:
  0.0 1.0 copy-done.22
  3.0 1.3 collective-permute-done
  5.0 4.0 %collective-permute-start.1 = (bf16[1,256,512]{2,1,0:T(8,128)(2,1)S(1)}, bf16[1,256,512]{2,1,0:T(8,128)(2,1)S(1)}, u32[]{:S(2)}, u32[]{:S(2)}) collective-permute-start(bf16[1,256,512]{2,1,0:T(8,128)(2,1)S(1)} %bitcast.48), channel_id=1, source_target_pairs={{0,8},{1,9},{2,10},{3,11},{4,12},{5,13},{6,14},{7,15},{8,0},{9,1},... | collective-permute-start | bytes 786440 | tf_op jit(solution)/shard_map/ppermute | solution.py:438
  9.0 1.2 copy-done.18
  10.2 1.2 copy-done.19
  11.4 1.0 copy-done.23
  12.5 6.2 %attention.1.refs_0_.refs_8_ = bf16[512,512]{1,0:T(8,128)(2,1)S(1)} custom-call(s32[1]{0:T(128)} %bitcast.14.kv_ref, bf16[512,512]{1,0:T(8,128)(2,1)S(1)} %copy-done.23, bf16[512,1024]{1,0:T(8,128)(2,1)S(1)} %copy-done.18, bf16[512,1024]{1,0:T(8,128)(2,1)S(1)} %copy-done.19), custom_call_target="tpu_custom_call" | custom-call | flops 33554432 | bytes 65536 | tf_op jit(solution)/shard_map/attention/pallas_call | solution.py:146
  18.7 2.5 %collective-permute-done.1 = bf16[1,256,512]{2,1,0:T(8,128)(2,1)S(1)} collective-permute-done((bf16[1,256,512]{2,1,0:T(8,128)(2,1)S(1)}, bf16[1,256,512]{2,1,0:T(8,128)(2,1)S(1)}, u32[]{:S(2)}, u32[]{:S(2)}) %collective-permute-start.1) | collective-permute-done | bytes 262176 | tf_op jit(solution)/shard_map/ppermute | solution.py:438
  21.2 1.6 collective-permute-start.2
  22.9 4.1 %collective-permute-start.5 = (bf16[2,256,512]{2,1,0:T(8,128)(2,1)S(1)}, bf16[2,256,512]{2,1,0:T(8,128)(2,1)S(1)}, u32[]{:S(2)}, u32[]{:S(2)}) collective-permute-start(bf16[2,256,512]{2,1,0:T(8,128)(2,1)S(1)} %pad_maximum_fusion.4), channel_id=1, source_target_pairs={{0,4},{1,5},{2,6},{3,7},{4,0},{5,1},{6,2},{7,3},{8,12},{9,13},{10,... | collective-permute-start | bytes 1572872 | tf_op jit(solution)/shard_map/ppermute | solution.py:438
  27.0 8.6 %collective-permute-done.3 = bf16[1,256,512]{2,1,0:T(8,128)(2,1)S(1)} collective-permute-done((bf16[1,256,512]{2,1,0:T(8,128)(2,1)S(1)}, bf16[1,256,512]{2,1,0:T(8,128)(2,1)S(1)}, u32[]{:S(2)}, u32[]{:S(2)}) %collective-permute-start.3) | collective-permute-done | bytes 262176 | tf_op jit(solution)/shard_map/ppermute | solution.py:438
  35.9 9.0 %collective-permute-done.5 = bf16[2,256,512]{2,1,0:T(8,128)(2,1)S(1)} collective-permute-done((bf16[2,256,512]{2,1,0:T(8,128)(2,1)S(1)}, bf16[2,256,512]{2,1,0:T(8,128)(2,1)S(1)}, u32[]{:S(2)}, u32[]{:S(2)}) %collective-permute-start.5) | collective-permute-done | bytes 524320 | tf_op jit(solution)/shard_map/ppermute | solution.py:438
  46.1 1.5 collective-permute-start.14
  47.6 10.0 %collective-permute-done.6 = bf16[2,256,512]{2,1,0:T(8,128)(2,1)S(1)} collective-permute-done((bf16[2,256,512]{2,1,0:T(8,128)(2,1)S(1)}, bf16[2,256,512]{2,1,0:T(8,128)(2,1)S(1)}, u32[]{:S(2)}, u32[]{:S(2)}) %collective-permute-start.6) | collective-permute-done | bytes 524320 | tf_op jit(solution)/shard_map/ppermute | solution.py:438
  59.5 1.1 fusion.11
  61.9 1.8 collective-permute-start.15
  63.7 1.5 collective-permute-done.7
  66.5 5.4 %collective-permute-done.8 = f32[32,384]{0,1:T(8,128)S(1)} collective-permute-done((f32[32,384]{0,1:T(8,128)S(1)}, f32[32,384]{0,1:T(8,128)S(1)}, u32[]{:S(2)}, u32[]{:S(2)}) %collective-permute-start.8) | collective-permute-done | bytes 49184 | tf_op jit(solution)/shard_map/ppermute | solution.py:438
  72.0 1.3 collective-permute-start.23
  73.4 2.7 %collective-permute-start.9 = (f32[64,384]{0,1:T(8,128)S(1)}, f32[64,384]{0,1:T(8,128)S(1)}, u32[]{:S(2)}, u32[]{:S(2)}) collective-permute-start(f32[64,384]{0,1:T(8,128)S(1)} %pad_maximum_fusion.9), channel_id=1, source_target_pairs={{0,8},{1,9},{2,10},{3,11},{4,12},{5,13},{6,14},{7,15},{8,0},{9,1},... | collective-permute-start | bytes 294920 | tf_op jit(solution)/shard_map/ppermute | solution.py:438
  76.1 8.8 %collective-permute-done.15.refs_5_ = bf16[2,256,512]{2,1,0:T(8,128)(2,1)} collective-permute-done((bf16[2,256,512]{2,1,0:T(8,128)(2,1)}, bf16[2,256,512]{2,1,0:T(8,128)(2,1)}, u32[]{:S(2)}, u32[]{:S(2)}) %collective-permute-start.15) | collective-permute-done | bytes 524320 | tf_op jit(solution)/shard_map/ppermute | solution.py:438
  86.1 1.1 broadcast_select_fusion.11
  89.4 10.8 %project_in.2 = (f32[256,1024]{1,0:T(8,128)}, bf16[256,1024]{1,0:T(8,128)(2,1)S(1)}) custom-call(s32[1]{0:T(128)} %bitcast.21.spot_ref, bf16[2,256,512]{2,1,0:T(8,128)(2,1)S(1)} %get-tuple-element.92.refs_0_, bf16[2,256,512]{2,1,0:T(8,128)(2,1)} %collective-permute-done.14.refs_1_, bf16[2,256,512]{2,1,0:T(8,128)(2,1)} %collective-permute-done.18.refs_2_, ...), custom_call_target="tpu_custom_call" | custom-call | flops 268435456 | bytes 720896 | tf_op jit(solution)/shard_map/project_in/pallas_call | solution.py:108
  101.3 1.1 broadcast_select_fusion.13
  104.2 10.8 %collective-permute-done.26.refs_5_ = bf16[2,256,512]{2,1,0:T(8,128)(2,1)S(1)} collective-permute-done((bf16[2,256,512]{2,1,0:T(8,128)(2,1)S(1)}, bf16[2,256,512]{2,1,0:T(8,128)(2,1)S(1)}, u32[]{:S(2)}, u32[]{:S(2)}) %collective-permute-start.26) | collective-permute-done | bytes 524320 | tf_op jit(solution)/shard_map/ppermute | solution.py:438
  115.8 1.1 broadcast_select_fusion.7
  116.9 1.3 collective-permute-start.22
  118.2 10.6 %project_in.3 = (f32[256,1024]{1,0:T(8,128)}, bf16[256,1024]{1,0:T(8,128)(2,1)}) custom-call(s32[1]{0:T(128)} %bitcast.21.spot_ref, bf16[2,256,512]{2,1,0:T(8,128)(2,1)S(1)} %get-tuple-element.100.refs_0_, bf16[2,256,512]{2,1,0:T(8,128)(2,1)S(1)} %collective-permute-done.23.refs_1_, bf16[2,256,512]{2,1,0:T(8,128)(2,1)} %collective-permute-done.24.refs_2_, ...), custom_call_target="tpu_custom_call" | custom-call | flops 268435456 | bytes 720896 | tf_op jit(solution)/shard_map/project_in/pallas_call | solution.py:108
  131.0 4.0 %project_out.5 = (f32[4,64,1024]{2,1,0:T(8,128)S(1)}, bf16[4,64,1024]{2,1,0:T(8,128)(2,1)}) custom-call(s32[3]{0:T(128)S(1)} %pad_add_fusion.spot_ref, bf16[512,512]{1,0:T(8,128)(2,1)S(1)} %attention.1.refs_0_.refs_8_, bf16[512,512]{1,0:T(8,128)(2,1)S(1)} %collective-permute-done.30.refs_1_.refs_9_, bf16[512,8192]{1,0:T(8,128)(2,1)} %refs_12_.5, ...), custom_call_target="tpu_custom_call" | custom-call | flops 67108864 | bytes 327680 | tf_op jit(solution)/shard_map/project_out/pallas_call | solution.py:335
  138.8 1.0 scan_weights.7.refs_0_
  139.8 1.7 scan_chunk.4
  141.5 1.9 scan_chunk.5
  143.4 1.3 copy-done.3
  145.6 1.7 scan_chunk.7
  147.3 1.1 collective-permute-done.37
  148.5 1.8 collective-permute-start.38
  153.1 4.0 %project_out.6 = (f32[4,64,1024]{2,1,0:T(8,128)S(1)}, bf16[4,64,1024]{2,1,0:T(8,128)(2,1)}) custom-call(s32[3]{0:T(128)S(1)} %pad_add_fusion.spot_ref, bf16[128,512]{1,0:T(8,128)(2,1)S(1)} %get-tuple-element.97.refs_0_, bf16[128,512]{1,0:T(8,128)(2,1)S(1)} %get-tuple-element.99.refs_1_, bf16[128,512]{1,0:T(8,128)(2,1)S(1)} %get-tuple-element.107.refs_2_, ...), custom_call_target="tpu_custom_call" | custom-call | flops 67108864 | bytes 327680 | tf_op jit(solution)/shard_map/project_out/pallas_call | solution.py:335
  157.2 1.5 collective-permute-start.39
  158.8 2.1 collective-permute-done.39
  160.9 2.9 %collective-permute-start.40 = (f32[4,128]{1,0:T(4,128)S(1)}, f32[4,128]{1,0:T(4,128)S(1)}, u32[]{:S(2)}, u32[]{:S(2)}) collective-permute-start(f32[4,128]{1,0:T(4,128)S(1)} %add.158), channel_id=1, source_target_pairs={{0,8},{1,9},{2,10},{3,11},{4,12},{5,13},{6,14},{7,15},{8,0},{9,1},... | collective-permute-start | bytes 6152 | tf_op jit(solution)/shard_map/ppermute | solution.py:438
  166.4 7.0 %project_out.7 = (f32[4,64,1024]{2,1,0:T(8,128)}, bf16[4,64,1024]{2,1,0:T(8,128)(2,1)}) custom-call(s32[3]{0:T(128)} %copy-done.26, bf16[128,512]{1,0:T(8,128)(2,1)} %copy-done.5, bf16[128,512]{1,0:T(8,128)(2,1)} %copy-done.6, bf16[128,512]{1,0:T(8,128)(2,1)} %copy-done.7, bf16[128,512]{1,0:T(8,128)(2,1)} %copy-done.8, bf16[128,512]{1,0:T(8,128)(2,1)} %copy-done.9, ...), custom_call_target="tpu_custom_call" | custom-call | flops 134217728 | bytes 458752 | tf_op jit(solution)/shard_map/project_out/pallas_call | solution.py:335
  174.3 7.0 %project_out.8 = (f32[4,64,1024]{2,1,0:T(8,128)}, bf16[4,64,1024]{2,1,0:T(8,128)(2,1)}) custom-call(s32[3]{0:T(128)} %copy-done.26, bf16[128,512]{1,0:T(8,128)(2,1)} %copy-done.5, bf16[128,512]{1,0:T(8,128)(2,1)} %copy-done.6, bf16[128,512]{1,0:T(8,128)(2,1)} %copy-done.7, bf16[128,512]{1,0:T(8,128)(2,1)} %copy-done.8, bf16[128,512]{1,0:T(8,128)(2,1)} %copy-done.9, ...), custom_call_target="tpu_custom_call" | custom-call | flops 134217728 | bytes 458752 | tf_op jit(solution)/shard_map/project_out/pallas_call | solution.py:335
  181.2 1.2 collective-permute-start.44
  182.5 7.0 %project_out.9 = (f32[4,64,1024]{2,1,0:T(8,128)}, bf16[4,64,1024]{2,1,0:T(8,128)(2,1)}) custom-call(s32[3]{0:T(128)} %copy-done.26, bf16[128,512]{1,0:T(8,128)(2,1)} %copy-done.5, bf16[128,512]{1,0:T(8,128)(2,1)} %copy-done.6, bf16[128,512]{1,0:T(8,128)(2,1)} %copy-done.7, bf16[128,512]{1,0:T(8,128)(2,1)} %copy-done.8, bf16[128,512]{1,0:T(8,128)(2,1)} %copy-done.9, ...), custom_call_target="tpu_custom_call" | custom-call | flops 134217728 | bytes 458752 | tf_op jit(solution)/shard_map/project_out/pallas_call | solution.py:335
  190.9 1.0 copy-done.21
  191.9 1.3 add_near.8
  193.2 1.5 collective-permute-start.41
  194.7 1.2 copy-done.16
  196.0 1.1 add_near.10
  197.7 5.5 %collective-permute-done.41.came_ref = bf16[2,64,1024]{2,1,0:T(8,128)(2,1)S(1)} collective-permute-done((bf16[2,64,1024]{2,1,0:T(8,128)(2,1)S(1)}, bf16[2,64,1024]{2,1,0:T(8,128)(2,1)S(1)}, u32[]{:S(2)}, u32[]{:S(2)}) %collective-permute-start.41) | collective-permute-done | bytes 262176 | tf_op jit(solution)/shard_map/ppermute | solution.py:438
  203.3 2.2 collective-permute-start.45
  206.1 2.9 %collective-permute-start.48 = (bf16[64,1024]{1,0:T(8,128)(2,1)S(1)}, bf16[64,1024]{1,0:T(8,128)(2,1)S(1)}, u32[]{:S(2)}, u32[]{:S(2)}) collective-permute-start(bf16[64,1024]{1,0:T(8,128)(2,1)S(1)} %bitcast.69), channel_id=1, source_target_pairs={{0,8},{1,9},{2,10},{3,11},{4,12},{5,13},{6,14},{7,15},{8,0},{9,1},... | collective-permute-start | bytes 393224 | tf_op jit(solution)/shard_map/ppermute | solution.py:438
  209.0 3.8 %collective-permute-done.45.refs_4_ = bf16[64,1024]{1,0:T(8,128)(2,1)S(1)} collective-permute-done((bf16[64,1024]{1,0:T(8,128)(2,1)S(1)}, bf16[64,1024]{1,0:T(8,128)(2,1)S(1)}, u32[]{:S(2)}, u32[]{:S(2)}) %collective-permute-start.45) | collective-permute-done | bytes 131104 | tf_op jit(solution)/shard_map/ppermute | solution.py:438
  212.8 1.2 copy-done.17
  214.0 1.1 add_near.12
  215.2 1.1 add_near.14
  216.4 2.1 collective-permute-start.49
  218.4 5.6 %collective-permute-done.46.came_ref = bf16[2,64,1024]{2,1,0:T(8,128)(2,1)S(1)} collective-permute-done((bf16[2,64,1024]{2,1,0:T(8,128)(2,1)S(1)}, bf16[2,64,1024]{2,1,0:T(8,128)(2,1)S(1)}, u32[]{:S(2)}, u32[]{:S(2)}) %collective-permute-start.46) | collective-permute-done | bytes 262176 | tf_op jit(solution)/shard_map/ppermute | solution.py:438
  224.1 1.4 collective-permute-start.50
  225.5 1.7 collective-permute-done.49.came_ref
  227.2 1.2 collective-permute-start.51
  228.4 2.5 %collective-permute-done.50.refs_6_ = bf16[64,1024]{1,0:T(8,128)(2,1)S(1)} collective-permute-done((bf16[64,1024]{1,0:T(8,128)(2,1)S(1)}, bf16[64,1024]{1,0:T(8,128)(2,1)S(1)}, u32[]{:S(2)}, u32[]{:S(2)}) %collective-permute-start.50) | collective-permute-done | bytes 131104 | tf_op jit(solution)/shard_map/ppermute | solution.py:438
  230.9 3.1 %collective-permute-done.51.refs_7_ = bf16[64,1024]{1,0:T(8,128)(2,1)S(1)} collective-permute-done((bf16[64,1024]{1,0:T(8,128)(2,1)S(1)}, bf16[64,1024]{1,0:T(8,128)(2,1)S(1)}, u32[]{:S(2)}, u32[]{:S(2)}) %collective-permute-start.51) | collective-permute-done | bytes 131104 | tf_op jit(solution)/shard_map/ppermute | solution.py:438
  234.8 1.5 collective-permute-done.52
  (193 shorter events, 33.2 us)
Async XLA Ops:
  2.5 1.9 collective-permute-start
  4.4 67.5 %collective-permute-start.16 = (bf16[512,8192]{1,0:T(8,128)(2,1)}, bf16[512,8192]{1,0:T(8,128)(2,1)}, u32[]{:S(2)}, u32[]{:S(2)}) collective-permute-start(bf16[512,8192]{1,0:T(8,128)(2,1)} %refs_12_.5), channel_id=1, source_target_pairs={{0,1},{1,0},{2,3},{3,2},{4,5},{5,4},{6,7},{7,6},{8,9},{9,8},{10,11... | collective-permute-start | bytes 25165832 | tf_op jit(solution)/shard_map/ppermute | solution.py:438
  4.9 67.1 %collective-permute-start.17 = (bf16[512,8192]{1,0:T(8,128)(2,1)}, bf16[512,8192]{1,0:T(8,128)(2,1)}, u32[]{:S(2)}, u32[]{:S(2)}) collective-permute-start(bf16[512,8192]{1,0:T(8,128)(2,1)} %refs_10_.5), channel_id=1, source_target_pairs={{0,1},{1,0},{2,3},{3,2},{4,5},{5,4},{6,7},{7,6},{8,9},{9,8},{10,11... | collective-permute-start | bytes 25165832 | tf_op jit(solution)/shard_map/ppermute | solution.py:438
  5.0 16.2 %collective-permute-start.1 = (bf16[1,256,512]{2,1,0:T(8,128)(2,1)S(1)}, bf16[1,256,512]{2,1,0:T(8,128)(2,1)S(1)}, u32[]{:S(2)}, u32[]{:S(2)}) collective-permute-start(bf16[1,256,512]{2,1,0:T(8,128)(2,1)S(1)} %bitcast.48), channel_id=1, source_target_pairs={{0,8},{1,9},{2,10},{3,11},{4,12},{5,13},{6,14},{7,15},{8,0},{9,1},... | collective-permute-start | bytes 786440 | tf_op jit(solution)/shard_map/ppermute | solution.py:438
  18.7 112.3 %copy-start = (bf16[512,512]{1,0:T(8,128)(2,1)}, bf16[512,512]{1,0:T(8,128)(2,1)S(1)}, u32[]{:S(2)}) copy-start(bf16[512,512]{1,0:T(8,128)(2,1)S(1)} %attention.1.refs_0_.refs_8_) | copy-start | bytes 1572868
  21.2 14.5 %collective-permute-start.3 = (bf16[1,256,512]{2,1,0:T(8,128)(2,1)S(1)}, bf16[1,256,512]{2,1,0:T(8,128)(2,1)S(1)}, u32[]{:S(2)}, u32[]{:S(2)}) collective-permute-start(bf16[1,256,512]{2,1,0:T(8,128)(2,1)S(1)} %bitcast.45), channel_id=1, source_target_pairs={{0,8},{1,9},{2,10},{3,11},{4,12},{5,13},{6,14},{7,15},{8,0},{9,1},... | collective-permute-start | bytes 786440 | tf_op jit(solution)/shard_map/ppermute | solution.py:438
  21.2 14.5 %collective-permute-start.2 = (f32[128,384]{1,0:T(8,128)S(1)}, f32[128,384]{1,0:T(8,128)S(1)}, u32[]{:S(2)}, u32[]{:S(2)}) collective-permute-start(f32[128,384]{1,0:T(8,128)S(1)} %dynamic-slice_bitcast_fusion.1), channel_id=1, source_target_pairs={{0,2},{1,3},{2,0},{3,1},{4,6},{5,7},{6,4},{7,5},{8,10},{9,11},{10,... | collective-permute-start | bytes 589832 | tf_op jit(solution)/shard_map/ppermute | solution.py:438
  22.9 22.0 %collective-permute-start.5 = (bf16[2,256,512]{2,1,0:T(8,128)(2,1)S(1)}, bf16[2,256,512]{2,1,0:T(8,128)(2,1)S(1)}, u32[]{:S(2)}, u32[]{:S(2)}) collective-permute-start(bf16[2,256,512]{2,1,0:T(8,128)(2,1)S(1)} %pad_maximum_fusion.4), channel_id=1, source_target_pairs={{0,4},{1,5},{2,6},{3,7},{4,0},{5,1},{6,2},{7,3},{8,12},{9,13},{10,... | collective-permute-start | bytes 1572872 | tf_op jit(solution)/shard_map/ppermute | solution.py:438
  35.8 10.3 %collective-permute-start.4 = (f32[64,384]{1,0:T(8,128)S(1)}, f32[64,384]{1,0:T(8,128)S(1)}, u32[]{:S(2)}, u32[]{:S(2)}) collective-permute-start(f32[64,384]{1,0:T(8,128)S(1)} %dynamic-slice_bitcast_fusion.2), channel_id=1, source_target_pairs={{0,8},{1,9},{2,10},{3,11},{4,12},{5,13},{6,14},{7,15},{8,0},{9,1},... | collective-permute-start | bytes 294920 | tf_op jit(solution)/shard_map/ppermute | solution.py:438
  44.9 12.7 %collective-permute-start.6 = (bf16[2,256,512]{2,1,0:T(8,128)(2,1)S(1)}, bf16[2,256,512]{2,1,0:T(8,128)(2,1)S(1)}, u32[]{:S(2)}, u32[]{:S(2)}) collective-permute-start(bf16[2,256,512]{2,1,0:T(8,128)(2,1)S(1)} %pad_maximum_fusion.2), channel_id=1, source_target_pairs={{0,4},{1,5},{2,6},{3,7},{4,0},{5,1},{6,2},{7,3},{8,12},{9,13},{10,... | collective-permute-start | bytes 1572872 | tf_op jit(solution)/shard_map/ppermute | solution.py:438
  45.8 15.8 %collective-permute-start.10 = (bf16[2,256,512]{2,1,0:T(8,128)(2,1)S(1)}, bf16[2,256,512]{2,1,0:T(8,128)(2,1)S(1)}, u32[]{:S(2)}, u32[]{:S(2)}) collective-permute-start(bf16[2,256,512]{2,1,0:T(8,128)(2,1)S(1)} %get-tuple-element.92.refs_0_), channel_id=1, source_target_pairs={{0,2},{1,3},{2,0},{3,1},{4,6},{5,7},{6,4},{7,5},{8,10},{9,11},{10,... | collective-permute-start | bytes 1572872 | tf_op jit(solution)/shard_map/ppermute | solution.py:438
  46.1 15.8 %collective-permute-start.14 = (bf16[2,256,512]{2,1,0:T(8,128)(2,1)}, bf16[2,256,512]{2,1,0:T(8,128)(2,1)}, u32[]{:S(2)}, u32[]{:S(2)}) collective-permute-start(bf16[2,256,512]{2,1,0:T(8,128)(2,1)} %get-tuple-element.149), channel_id=1, source_target_pairs={{0,16},{16,0},{1,17},{17,1},{2,18},{18,2},{3,19},{19,3},{4,20},{20... | collective-permute-start | bytes 1572872 | tf_op jit(solution)/shard_map/ppermute | solution.py:441
  59.2 6.0 %collective-permute-start.7 = (f32[32,384]{0,1:T(8,128)}, f32[32,384]{0,1:T(8,128)}, u32[]{:S(2)}, u32[]{:S(2)}) collective-permute-start(f32[32,384]{0,1:T(8,128)} %bitcast.17), channel_id=1, source_target_pairs={{0,4},{1,5},{2,6},{3,7},{4,0},{5,1},{6,2},{7,3},{8,12},{9,13},{10,... | collective-permute-start | bytes 147464 | tf_op jit(solution)/shard_map/ppermute | solution.py:438
  61.6 23.9 %collective-permute-start.11 = (bf16[2,256,512]{2,1,0:T(8,128)(2,1)S(1)}, bf16[2,256,512]{2,1,0:T(8,128)(2,1)S(1)}, u32[]{:S(2)}, u32[]{:S(2)}) collective-permute-start(bf16[2,256,512]{2,1,0:T(8,128)(2,1)S(1)} %get-tuple-element.100.refs_0_), channel_id=1, source_target_pairs={{0,2},{1,3},{2,0},{3,1},{4,6},{5,7},{6,4},{7,5},{8,10},{9,11},{10,... | collective-permute-start | bytes 1572872 | tf_op jit(solution)/shard_map/ppermute | solution.py:438
  61.9 23.0 %collective-permute-start.15 = (bf16[2,256,512]{2,1,0:T(8,128)(2,1)}, bf16[2,256,512]{2,1,0:T(8,128)(2,1)}, u32[]{:S(2)}, u32[]{:S(2)}) collective-permute-start(bf16[2,256,512]{2,1,0:T(8,128)(2,1)} %collective-permute-done.14.refs_1_), channel_id=1, source_target_pairs={{0,2},{1,3},{2,0},{3,1},{4,6},{5,7},{6,4},{7,5},{8,10},{9,11},{10,... | collective-permute-start | bytes 1572872 | tf_op jit(solution)/shard_map/ppermute | solution.py:438
  66.2 5.7 %collective-permute-start.8 = (f32[32,384]{0,1:T(8,128)S(1)}, f32[32,384]{0,1:T(8,128)S(1)}, u32[]{:S(2)}, u32[]{:S(2)}) collective-permute-start(f32[32,384]{0,1:T(8,128)S(1)} %bitcast_add_fusion.1), channel_id=1, source_target_pairs={{0,4},{1,5},{2,6},{3,7},{4,0},{5,1},{6,2},{7,3},{8,12},{9,13},{10,... | collective-permute-start | bytes 147464 | tf_op jit(solution)/shard_map/ppermute | solution.py:438
  66.5 48.5 %copy-start.38 = (f32[8]{0:T(128)S(1)}, f32[8]{0:T(128)}, u32[]{:S(2)}) copy-start(f32[8]{0:T(128)} %param.20) | copy-start | bytes 100
  66.5 48.5 %copy-start.37 = (f32[8]{0:T(128)S(1)}, f32[8]{0:T(128)}, u32[]{:S(2)}) copy-start(f32[8]{0:T(128)} %param.21) | copy-start | bytes 100
  71.9 13.6 %copy-start.31 = (f32[32,384]{0,1:T(8,128)}, f32[32,384]{0,1:T(8,128)S(1)}, u32[]{:S(2)}) copy-start(f32[32,384]{0,1:T(8,128)S(1)} %get-tuple-element.164) | copy-start | bytes 147460
  72.0 15.4 %collective-permute-start.23 = (bf16[2,256,512]{2,1,0:T(8,128)(2,1)}, bf16[2,256,512]{2,1,0:T(8,128)(2,1)S(1)}, u32[]{:S(2)}, u32[]{:S(2)}) collective-permute-start(bf16[2,256,512]{2,1,0:T(8,128)(2,1)} %get-tuple-element.90), channel_id=1, source_target_pairs={{0,16},{16,0},{1,17},{17,1},{2,18},{18,2},{3,19},{19,3},{4,20},{20... | collective-permute-start | bytes 1572872 | tf_op jit(solution)/shard_map/ppermute | solution.py:441
  73.4 12.0 %collective-permute-start.9 = (f32[64,384]{0,1:T(8,128)S(1)}, f32[64,384]{0,1:T(8,128)S(1)}, u32[]{:S(2)}, u32[]{:S(2)}) collective-permute-start(f32[64,384]{0,1:T(8,128)S(1)} %pad_maximum_fusion.9), channel_id=1, source_target_pairs={{0,8},{1,9},{2,10},{3,11},{4,12},{5,13},{6,14},{7,15},{8,0},{9,1},... | collective-permute-start | bytes 294920 | tf_op jit(solution)/shard_map/ppermute | solution.py:438
  84.9 3.8 %collective-permute-start.20 = (bf16[2,256,512]{2,1,0:T(8,128)(2,1)S(1)}, bf16[2,256,512]{2,1,0:T(8,128)(2,1)}, u32[]{:S(2)}, u32[]{:S(2)}) collective-permute-start(bf16[2,256,512]{2,1,0:T(8,128)(2,1)S(1)} %collective-permute-done.10.refs_4_), channel_id=1, source_target_pairs={{0,1},{1,0},{2,3},{3,2},{4,5},{5,4},{6,7},{7,6},{8,9},{9,8},{10,11... | collective-permute-start | bytes 1572872 | tf_op jit(solution)/shard_map/ppermute | solution.py:438
  84.9 3.5 %collective-permute-start.18 = (bf16[2,256,512]{2,1,0:T(8,128)(2,1)S(1)}, bf16[2,256,512]{2,1,0:T(8,128)(2,1)}, u32[]{:S(2)}, u32[]{:S(2)}) collective-permute-start(bf16[2,256,512]{2,1,0:T(8,128)(2,1)S(1)} %get-tuple-element.92.refs_0_), channel_id=1, source_target_pairs={{0,1},{1,0},{2,3},{3,2},{4,5},{5,4},{6,7},{7,6},{8,9},{9,8},{10,11... | collective-permute-start | bytes 1572872 | tf_op jit(solution)/shard_map/ppermute | solution.py:438
  85.4 3.2 %collective-permute-start.19 = (bf16[2,256,512]{2,1,0:T(8,128)(2,1)}, bf16[2,256,512]{2,1,0:T(8,128)(2,1)}, u32[]{:S(2)}, u32[]{:S(2)}) collective-permute-start(bf16[2,256,512]{2,1,0:T(8,128)(2,1)} %collective-permute-done.14.refs_1_), channel_id=1, source_target_pairs={{0,1},{1,0},{2,3},{3,2},{4,5},{5,4},{6,7},{7,6},{8,9},{9,8},{10,11... | collective-permute-start | bytes 1572872 | tf_op jit(solution)/shard_map/ppermute | solution.py:438
  86.1 3.3 %collective-permute-start.21 = (bf16[2,256,512]{2,1,0:T(8,128)(2,1)}, bf16[2,256,512]{2,1,0:T(8,128)(2,1)}, u32[]{:S(2)}, u32[]{:S(2)}) collective-permute-start(bf16[2,256,512]{2,1,0:T(8,128)(2,1)} %collective-permute-done.15.refs_5_), channel_id=1, source_target_pairs={{0,1},{1,0},{2,3},{3,2},{4,5},{5,4},{6,7},{7,6},{8,9},{9,8},{10,11... | collective-permute-start | bytes 1572872 | tf_op jit(solution)/shard_map/ppermute | solution.py:438
  87.4 13.9 %copy-start.33 = (f32[128,384]{0,1:T(8,128)}, f32[128,384]{0,1:T(8,128)S(1)}, u32[]{:S(2)}) copy-start(f32[128,384]{0,1:T(8,128)S(1)} %pad_maximum_fusion.10) | copy-start | bytes 589828
  87.4 13.9 %collective-permute-start.12 = (f32[128,384]{0,1:T(8,128)S(1)}, f32[128,384]{0,1:T(8,128)}, u32[]{:S(2)}, u32[]{:S(2)}) collective-permute-start(f32[128,384]{0,1:T(8,128)S(1)} %pad_maximum_fusion.10), channel_id=1, source_target_pairs={{0,2},{1,3},{2,0},{3,1},{4,6},{5,7},{6,4},{7,5},{8,10},{9,11},{10,... | collective-permute-start | bytes 589832 | tf_op jit(solution)/shard_map/ppermute | solution.py:438
  101.0 14.0 %collective-permute-start.26 = (bf16[2,256,512]{2,1,0:T(8,128)(2,1)S(1)}, bf16[2,256,512]{2,1,0:T(8,128)(2,1)S(1)}, u32[]{:S(2)}, u32[]{:S(2)}) collective-permute-start(bf16[2,256,512]{2,1,0:T(8,128)(2,1)S(1)} %collective-permute-done.23.refs_1_), channel_id=1, source_target_pairs={{0,2},{1,3},{2,0},{3,1},{4,6},{5,7},{6,4},{7,5},{8,10},{9,11},{10,... | collective-permute-start | bytes 1572872 | tf_op jit(solution)/shard_map/ppermute | solution.py:438
  103.2 12.0 %collective-permute-start.13 = (f32[256,384]{0,1:T(8,128)}, f32[256,384]{0,1:T(8,128)}, u32[]{:S(2)}, u32[]{:S(2)}) collective-permute-start(f32[256,384]{0,1:T(8,128)} %pad_maximum_fusion.8), channel_id=1, source_target_pairs={{0,1},{1,0},{2,3},{3,2},{4,5},{5,4},{6,7},{7,6},{8,9},{9,8},{10,11... | collective-permute-start | bytes 1179656 | tf_op jit(solution)/shard_map/ppermute | solution.py:438
  103.2 13.7 %collective-permute-start.24 = (bf16[2,256,512]{2,1,0:T(8,128)(2,1)S(1)}, bf16[2,256,512]{2,1,0:T(8,128)(2,1)}, u32[]{:S(2)}, u32[]{:S(2)}) collective-permute-start(bf16[2,256,512]{2,1,0:T(8,128)(2,1)S(1)} %get-tuple-element.100.refs_0_), channel_id=1, source_target_pairs={{0,1},{1,0},{2,3},{3,2},{4,5},{5,4},{6,7},{7,6},{8,9},{9,8},{10,11... | collective-permute-start | bytes 1572872 | tf_op jit(solution)/shard_map/ppermute | solution.py:438
  103.7 14.5 %collective-permute-start.27 = (bf16[2,256,512]{2,1,0:T(8,128)(2,1)S(1)}, bf16[2,256,512]{2,1,0:T(8,128)(2,1)}, u32[]{:S(2)}, u32[]{:S(2)}) collective-permute-start(bf16[2,256,512]{2,1,0:T(8,128)(2,1)S(1)} %collective-permute-done.11.refs_4_), channel_id=1, source_target_pairs={{0,1},{1,0},{2,3},{3,2},{4,5},{5,4},{6,7},{7,6},{8,9},{9,8},{10,11... | collective-permute-start | bytes 1572872 | tf_op jit(solution)/shard_map/ppermute | solution.py:438
  103.7 14.5 %collective-permute-start.25 = (bf16[2,256,512]{2,1,0:T(8,128)(2,1)S(1)}, bf16[2,256,512]{2,1,0:T(8,128)(2,1)}, u32[]{:S(2)}, u32[]{:S(2)}) collective-permute-start(bf16[2,256,512]{2,1,0:T(8,128)(2,1)S(1)} %collective-permute-done.23.refs_1_), channel_id=1, source_target_pairs={{0,1},{1,0},{2,3},{3,2},{4,5},{5,4},{6,7},{7,6},{8,9},{9,8},{10,11... | collective-permute-start | bytes 1572872 | tf_op jit(solution)/shard_map/ppermute | solution.py:438
  115.0 3.3 %collective-permute-start.28 = (bf16[2,256,512]{2,1,0:T(8,128)(2,1)S(1)}, bf16[2,256,512]{2,1,0:T(8,128)(2,1)}, u32[]{:S(2)}, u32[]{:S(2)}) collective-permute-start(bf16[2,256,512]{2,1,0:T(8,128)(2,1)S(1)} %collective-permute-done.26.refs_5_), channel_id=1, source_target_pairs={{0,1},{1,0},{2,3},{3,2},{4,5},{5,4},{6,7},{7,6},{8,9},{9,8},{10,11... | collective-permute-start | bytes 1572872 | tf_op jit(solution)/shard_map/ppermute | solution.py:438
  115.2 37.9 %copy-start.26 = (s32[3]{0:T(128)}, s32[3]{0:T(128)S(1)}, u32[]{:S(2)}) copy-start(s32[3]{0:T(128)S(1)} %pad_add_fusion.spot_ref) | copy-start | bytes 40
  115.2 14.9 %copy-start.36 = (f32[8]{0:T(128)S(1)}, f32[8]{0:T(128)}, u32[]{:S(2)}) copy-start(f32[8]{0:T(128)} %param.19) | copy-start | bytes 100
  115.2 15.7 %collective-permute-start.30 = (bf16[512,512]{1,0:T(8,128)(2,1)S(1)}, bf16[512,512]{1,0:T(8,128)(2,1)S(1)}, u32[]{:S(2)}, u32[]{:S(2)}) collective-permute-start(bf16[512,512]{1,0:T(8,128)(2,1)S(1)} %attention.1.refs_0_.refs_8_), channel_id=1, source_target_pairs={{0,1},{1,0},{2,3},{3,2},{4,5},{5,4},{6,7},{7,6},{8,9},{9,8},{10,11... | collective-permute-start | bytes 1572872 | tf_op jit(solution)/shard_map/ppermute | solution.py:438
  116.9 22.9 %collective-permute-start.22 = (bf16[256,1024]{1,0:T(8,128)(2,1)}, bf16[256,1024]{1,0:T(8,128)(2,1)}, u32[]{:S(2)}, u32[]{:S(2)}) collective-permute-start(bf16[256,1024]{1,0:T(8,128)(2,1)} %copy-done.28), channel_id=1, source_target_pairs={{0,16},{16,0},{1,17},{17,1},{2,18},{18,2},{3,19},{19,3},{4,20},{20... | collective-permute-start | bytes 1572872 | tf_op jit(solution)/shard_map/ppermute | solution.py:441
  128.9 14.5 %collective-permute-start.29 = (bf16[256,1024]{1,0:T(8,128)(2,1)}, bf16[256,1024]{1,0:T(8,128)(2,1)S(1)}, u32[]{:S(2)}, u32[]{:S(2)}) collective-permute-start(bf16[256,1024]{1,0:T(8,128)(2,1)} %get-tuple-element.105), channel_id=1, source_target_pairs={{0,16},{16,0},{1,17},{17,1},{2,18},{18,2},{3,19},{19,3},{4,20},{20... | collective-permute-start | bytes 1572872 | tf_op jit(solution)/shard_map/ppermute | solution.py:441
  136.0 14.8 %collective-permute-start.31 = (bf16[4,64,1024]{2,1,0:T(8,128)(2,1)}, bf16[4,64,1024]{2,1,0:T(8,128)(2,1)S(1)}, u32[]{:S(2)}, u32[]{:S(2)}) collective-permute-start(bf16[4,64,1024]{2,1,0:T(8,128)(2,1)} %get-tuple-element.111), channel_id=1, source_target_pairs={{0,2},{1,3},{2,0},{3,1},{4,6},{5,7},{6,4},{7,5},{8,10},{9,11},{10,... | collective-permute-start | bytes 1572872 | tf_op jit(solution)/shard_map/ppermute | solution.py:438
  141.5 15.7 %copy-start.5 = (bf16[128,512]{1,0:T(8,128)(2,1)}, bf16[128,512]{1,0:T(8,128)(2,1)S(1)}, u32[]{:S(2)}) copy-start(bf16[128,512]{1,0:T(8,128)(2,1)S(1)} %get-tuple-element.97.refs_0_) | copy-start | bytes 393220
  143.4 13.8 %copy-start.6 = (bf16[128,512]{1,0:T(8,128)(2,1)}, bf16[128,512]{1,0:T(8,128)(2,1)S(1)}, u32[]{:S(2)}) copy-start(bf16[128,512]{1,0:T(8,128)(2,1)S(1)} %get-tuple-element.99.refs_1_) | copy-start | bytes 393220
  147.3 1.2 collective-permute-start.37
  148.5 3.7 %collective-permute-start.38 = (f32[4,128]{1,0:T(4,128)S(1)}, f32[4,128]{1,0:T(4,128)S(1)}, u32[]{:S(2)}, u32[]{:S(2)}) collective-permute-start(f32[4,128]{1,0:T(4,128)S(1)} %fusion.9), channel_id=1, source_target_pairs={{0,2},{1,3},{2,0},{3,1},{4,6},{5,7},{6,4},{7,5},{8,10},{9,11},{10,... | collective-permute-start | bytes 6152 | tf_op jit(solution)/shard_map/ppermute | solution.py:438
  150.3 1.9 collective-permute-start.32
  150.3 1.9 collective-permute-start.33
  150.8 2.3 collective-permute-start.35
  151.6 1.5 collective-permute-start.34
  157.2 3.7 %collective-permute-start.39 = (f32[4,128]{1,0:T(4,128)S(1)}, f32[4,128]{1,0:T(4,128)S(1)}, u32[]{:S(2)}, u32[]{:S(2)}) collective-permute-start(f32[4,128]{1,0:T(4,128)S(1)} %fusion.12), channel_id=1, source_target_pairs={{0,4},{1,5},{2,6},{3,7},{4,0},{5,1},{6,2},{7,3},{8,12},{9,13},{10,... | collective-permute-start | bytes 6152 | tf_op jit(solution)/shard_map/ppermute | solution.py:438
  160.9 4.5 %collective-permute-start.40 = (f32[4,128]{1,0:T(4,128)S(1)}, f32[4,128]{1,0:T(4,128)S(1)}, u32[]{:S(2)}, u32[]{:S(2)}) collective-permute-start(f32[4,128]{1,0:T(4,128)S(1)} %add.158), channel_id=1, source_target_pairs={{0,8},{1,9},{2,10},{3,11},{4,12},{5,13},{6,14},{7,15},{8,0},{9,1},... | collective-permute-start | bytes 6152 | tf_op jit(solution)/shard_map/ppermute | solution.py:438
  163.8 27.0 %collective-permute-start.36 = (bf16[4,64,1024]{2,1,0:T(8,128)(2,1)}, bf16[4,64,1024]{2,1,0:T(8,128)(2,1)}, u32[]{:S(2)}, u32[]{:S(2)}) collective-permute-start(bf16[4,64,1024]{2,1,0:T(8,128)(2,1)} %get-tuple-element.114), channel_id=1, source_target_pairs={{0,2},{1,3},{2,0},{3,1},{4,6},{5,7},{6,4},{7,5},{8,10},{9,11},{10,... | collective-permute-start | bytes 1572872 | tf_op jit(solution)/shard_map/ppermute | solution.py:438
  173.3 21.4 %collective-permute-start.42 = (bf16[4,64,1024]{2,1,0:T(8,128)(2,1)}, bf16[4,64,1024]{2,1,0:T(8,128)(2,1)}, u32[]{:S(2)}, u32[]{:S(2)}) collective-permute-start(bf16[4,64,1024]{2,1,0:T(8,128)(2,1)} %get-tuple-element.125), channel_id=1, source_target_pairs={{0,2},{1,3},{2,0},{3,1},{4,6},{5,7},{6,4},{7,5},{8,10},{9,11},{10,... | collective-permute-start | bytes 1572872 | tf_op jit(solution)/shard_map/ppermute | solution.py:438
  181.2 27.8 %collective-permute-start.44 = (bf16[4,64,1024]{2,1,0:T(8,128)(2,1)}, bf16[4,64,1024]{2,1,0:T(8,128)(2,1)}, u32[]{:S(2)}, u32[]{:S(2)}) collective-permute-start(bf16[4,64,1024]{2,1,0:T(8,128)(2,1)} %get-tuple-element.130), channel_id=1, source_target_pairs={{0,2},{1,3},{2,0},{3,1},{4,6},{5,7},{6,4},{7,5},{8,10},{9,11},{10,... | collective-permute-start | bytes 1572872 | tf_op jit(solution)/shard_map/ppermute | solution.py:438
  182.5 51.5 %copy-start.27 = (s32[3]{0:T(128)S(1)}, s32[3]{0:T(128)}, u32[]{:S(2)}) copy-start(s32[3]{0:T(128)} %copy-done.26) | copy-start | bytes 40
  189.5 25.7 %copy-start.15 = (f32[4,64,1024]{2,1,0:T(8,128)S(1)}, f32[4,64,1024]{2,1,0:T(8,128)}, u32[]{:S(2)}) copy-start(f32[4,64,1024]{2,1,0:T(8,128)} %get-tuple-element.136.keep_ref) | copy-start | bytes 3145732
  189.5 25.7 %collective-permute-start.47 = (bf16[4,64,1024]{2,1,0:T(8,128)(2,1)}, bf16[4,64,1024]{2,1,0:T(8,128)(2,1)}, u32[]{:S(2)}, u32[]{:S(2)}) collective-permute-start(bf16[4,64,1024]{2,1,0:T(8,128)(2,1)} %get-tuple-element.137), channel_id=1, source_target_pairs={{0,2},{1,3},{2,0},{3,1},{4,6},{5,7},{6,4},{7,5},{8,10},{9,11},{10,... | collective-permute-start | bytes 1572872 | tf_op jit(solution)/shard_map/ppermute | solution.py:438
  193.2 10.1 %collective-permute-start.41 = (bf16[2,64,1024]{2,1,0:T(8,128)(2,1)S(1)}, bf16[2,64,1024]{2,1,0:T(8,128)(2,1)S(1)}, u32[]{:S(2)}, u32[]{:S(2)}) collective-permute-start(bf16[2,64,1024]{2,1,0:T(8,128)(2,1)S(1)} %get-tuple-element.122), channel_id=1, source_target_pairs={{0,4},{1,5},{2,6},{3,7},{4,0},{5,1},{6,2},{7,3},{8,12},{9,13},{10,... | collective-permute-start | bytes 786440 | tf_op jit(solution)/shard_map/ppermute | solution.py:438
  197.1 9.0 %collective-permute-start.43 = (bf16[2,64,1024]{2,1,0:T(8,128)(2,1)S(1)}, bf16[2,64,1024]{2,1,0:T(8,128)(2,1)S(1)}, u32[]{:S(2)}, u32[]{:S(2)}) collective-permute-start(bf16[2,64,1024]{2,1,0:T(8,128)(2,1)S(1)} %get-tuple-element.127), channel_id=1, source_target_pairs={{0,4},{1,5},{2,6},{3,7},{4,0},{5,1},{6,2},{7,3},{8,12},{9,13},{10,... | collective-permute-start | bytes 786440 | tf_op jit(solution)/shard_map/ppermute | solution.py:438
  203.3 9.4 %collective-permute-start.45 = (bf16[64,1024]{1,0:T(8,128)(2,1)S(1)}, bf16[64,1024]{1,0:T(8,128)(2,1)S(1)}, u32[]{:S(2)}, u32[]{:S(2)}) collective-permute-start(bf16[64,1024]{1,0:T(8,128)(2,1)S(1)} %bitcast.70), channel_id=1, source_target_pairs={{0,8},{1,9},{2,10},{3,11},{4,12},{5,13},{6,14},{7,15},{8,0},{9,1},... | collective-permute-start | bytes 393224 | tf_op jit(solution)/shard_map/ppermute | solution.py:438
  206.1 9.1 %collective-permute-start.48 = (bf16[64,1024]{1,0:T(8,128)(2,1)S(1)}, bf16[64,1024]{1,0:T(8,128)(2,1)S(1)}, u32[]{:S(2)}, u32[]{:S(2)}) collective-permute-start(bf16[64,1024]{1,0:T(8,128)(2,1)S(1)} %bitcast.69), channel_id=1, source_target_pairs={{0,8},{1,9},{2,10},{3,11},{4,12},{5,13},{6,14},{7,15},{8,0},{9,1},... | collective-permute-start | bytes 393224 | tf_op jit(solution)/shard_map/ppermute | solution.py:438
  215.1 8.9 %collective-permute-start.46 = (bf16[2,64,1024]{2,1,0:T(8,128)(2,1)S(1)}, bf16[2,64,1024]{2,1,0:T(8,128)(2,1)S(1)}, u32[]{:S(2)}, u32[]{:S(2)}) collective-permute-start(bf16[2,64,1024]{2,1,0:T(8,128)(2,1)S(1)} %get-tuple-element.134), channel_id=1, source_target_pairs={{0,4},{1,5},{2,6},{3,7},{4,0},{5,1},{6,2},{7,3},{8,12},{9,13},{10,... | collective-permute-start | bytes 786440 | tf_op jit(solution)/shard_map/ppermute | solution.py:438
  216.4 10.8 %collective-permute-start.49 = (bf16[2,64,1024]{2,1,0:T(8,128)(2,1)S(1)}, bf16[2,64,1024]{2,1,0:T(8,128)(2,1)S(1)}, u32[]{:S(2)}, u32[]{:S(2)}) collective-permute-start(bf16[2,64,1024]{2,1,0:T(8,128)(2,1)S(1)} %get-tuple-element.141), channel_id=1, source_target_pairs={{0,4},{1,5},{2,6},{3,7},{4,0},{5,1},{6,2},{7,3},{8,12},{9,13},{10,... | collective-permute-start | bytes 786440 | tf_op jit(solution)/shard_map/ppermute | solution.py:438
  224.1 6.8 %collective-permute-start.50 = (bf16[64,1024]{1,0:T(8,128)(2,1)S(1)}, bf16[64,1024]{1,0:T(8,128)(2,1)S(1)}, u32[]{:S(2)}, u32[]{:S(2)}) collective-permute-start(bf16[64,1024]{1,0:T(8,128)(2,1)S(1)} %bitcast.71), channel_id=1, source_target_pairs={{0,8},{1,9},{2,10},{3,11},{4,12},{5,13},{6,14},{7,15},{8,0},{9,1},... | collective-permute-start | bytes 393224 | tf_op jit(solution)/shard_map/ppermute | solution.py:438
  227.2 6.8 %collective-permute-start.51 = (bf16[64,1024]{1,0:T(8,128)(2,1)S(1)}, bf16[64,1024]{1,0:T(8,128)(2,1)S(1)}, u32[]{:S(2)}, u32[]{:S(2)}) collective-permute-start(bf16[64,1024]{1,0:T(8,128)(2,1)S(1)} %bitcast.72), channel_id=1, source_target_pairs={{0,8},{1,9},{2,10},{3,11},{4,12},{5,13},{6,14},{7,15},{8,0},{9,1},... | collective-permute-start | bytes 393224 | tf_op jit(solution)/shard_map/ppermute | solution.py:438
  234.7 1.6 collective-permute-start.52
  (28 other events, 122.3 us)

commit v4 on v3

--- a/solution.py
+++ b/solution.py
@@ -74,14 +74,14 @@
         weights_ref = refs[given]
         tokens_ref, rows_ref, done = refs[-3:]
         copies = []
-        for n, (m, k) in enumerate(places):
-            row = pl.multiple_of((spot_ref[0] ^ (k * len(features) + m)) * block, block)
-            for kind in range(kinds):
+        for kind in range(kinds):
+            for n, (m, k) in enumerate(places):
+                row = pl.multiple_of((spot_ref[0] ^ (k * len(features) + m)) * block, block)
                 copies.append(
                     pltpu.make_async_copy(
                         weights_ref.at[kind, pl.ds(row, block)],
                         rows_ref.at[kind, pl.ds(n * block, block)],
-                        done.at[n * kinds + kind],
+                        done.at[kind * len(places) + n],
                     )
                 )
         for copy in copies:
@@ -91,9 +91,9 @@
                 tokens_ref[d * size : (d + 1) * size, n * block : (n + 1) * block] = refs[
                     m * ndp + d
                 ][k]
-        for copy in copies:
-            copy.wait()
         for kind in range(kinds):
+            for copy in copies[kind * len(places) : (kind + 1) * len(places)]:
+                copy.wait()
             lane = slice(kind * channels, (kind + 1) * channels)
             total = jnp.dot(tokens_ref[...], rows_ref[kind], preferred_element_type=f32)
             for d in range(ndp):
@@ -564,16 +564,14 @@
     gated[-1] = after(gated[-1], first_came)
     keep, send = project_out(0, widths[0], (spots, far), *weights)
     squares = jnp.concatenate(squares)
-    k = 1
-    while k < nmp:
-        if k == 4:
-            squares = after(squares, send)
+    for k in (1, 2):
         squares = squares + swap(squares, k)
-        k *= 2
+    squares = after(squares, send)
+    squares = sum((swap(squares, 4 * k) for k in range(1, far)), squares)
     scale = lax.rsqrt(squares / (channels * nmp) + norm_eps).reshape(far, 2, rows // 2, 1)
     scale_kept = jnp.stack([at(at(scale, z ^ k), y) for k in range(far)])
 
-    done, far_came = [], []
+    done, near_done, far_came = [], [], []
     for n, width in enumerate(widths):
         if n == 0:
             keep, send = add_near(keep, swap(send, 2), scale_kept, first[0], first_came)
@@ -583,12 +581,13 @@
             )
             came = swap(send, 2)
             if n >= 2:
-                came = after(came, far_came[n - 2])
+                came = after(came, near_done[n - 2], *far_came[: n - 2])
             keep, send = add_near(keep, came)
         k = 1
         while k < far // 2:
             keep, send = add_near(keep, swap(send, 4 * k))
             k *= 2
+        near_done.append(send)
         far_came.append(swap(send[0], 4 * k))
         done.append(keep[0])
     stay, came = finish(spots, done, far_came)

time: 239 us -> 234 us (0.979)
    ppermute x49 -> x50, starting transfers between devices: 42.9 us -> 40.8 us  [swap(): return lax.ppermute(source, 'mp', [(s, s ^ k) for s in range(nmp)])]
    ppermute x49 -> x50, waiting for transfers between devices: 89 us -> 88.9 us  [swap(): return lax.ppermute(source, 'mp', [(s, s ^ k) for s in range(nmp)])]
  transfers between devices with their start and end apart: 53 -> 54, of which waited for: 24 -> 23; matrix products, arithmetic and copies ran while one was open for 5% -> 5% of each run, Pallas kernels for 28% -> 28%
where the time goes in v4:
time: 234 us; the launch traced here: 233 us
  waiting for transfers between devices  88.9 us (38%)
  Pallas kernels  69.5 us (30%)
  starting transfers between devices  45.8 us (20%)
  local copies, waits for them, and re-layouts  18.4 us (8%)
  other arithmetic  9.18 us (4%)
    ppermute x50, waiting for transfers between devices, swap(): return lax.ppermute(source, 'mp', [(s, s ^ k) for s in range(nmp)])  88.9 us
    ppermute x50, starting transfers between devices, swap(): return lax.ppermute(source, 'mp', [(s, s ^ k) for s in range(nmp)])  40.8 us
    pallas_call x5, Pallas kernels, project_out(): pl.pallas_call(body, in_specs=[pl.BlockSpec(memory_space=pltpu.SMEM)] + [...  29 us
    pallas_call x2, Pallas kernels, project_in(): pl.pallas_call(body, in_specs=[pl.BlockSpec(memory_space=pltpu.SMEM)] + [...  19.3 us
    unnamed x78, local copies, waits for them, and re-layouts  14.4 us
    pallas_call x1, Pallas kernels, attention(): pl.pallas_call(body, grid_spec=pltpu.PrefetchScalarGridSpec(num_scalar_pr...  6.2 us
    pallas_call x4, Pallas kernels, scan_chunk(): pl.pallas_call(body, out_shape=(jax.ShapeDtypeStruct((pairs, wide, 2 * LA...  6.09 us
    ppermute x4, starting transfers between devices, cross(): return lax.ppermute(source, 'dp', [(s, s ^ k) for s in range(ndp)])  4.94 us
  transfers between devices with their start and end apart: 54, of which 23 were waited for; matrix products, arithmetic and copies ran while one was open for 5% of the time, Pallas kernels for 28%

profile of v4, /device:TPU:0, one launch (start us, length us, event | category | flops | bytes accessed | tf_op | source)
XLA Modules:
  0.0 233.0 jit_solution(8209788559690855498)
XLA Ops:
  0.0 1.0 copy-done.22
  1.0 1.0 copy-done.24
  3.0 1.3 collective-permute-done
  5.0 4.0 %collective-permute-start.1 = (bf16[1,256,512]{2,1,0:T(8,128)(2,1)S(1)}, bf16[1,256,512]{2,1,0:T(8,128)(2,1)S(1)}, u32[]{:S(2)}, u32[]{:S(2)}) collective-permute-start(bf16[1,256,512]{2,1,0:T(8,128)(2,1)S(1)} %bitcast.48), channel_id=1, source_target_pairs={{0,8},{1,9},{2,10},{3,11},{4,12},{5,13},{6,14},{7,15},{8,0},{9,1},... | collective-permute-start | bytes 786440 | tf_op jit(solution)/shard_map/ppermute | solution.py:438
  9.0 1.2 copy-done.18
  10.2 1.2 copy-done.19
  11.4 1.0 copy-done.23
  12.5 6.2 %attention.1.refs_0_.refs_8_ = bf16[512,512]{1,0:T(8,128)(2,1)S(1)} custom-call(s32[1]{0:T(128)} %bitcast.14.kv_ref, bf16[512,512]{1,0:T(8,128)(2,1)S(1)} %copy-done.23, bf16[512,1024]{1,0:T(8,128)(2,1)S(1)} %copy-done.18, bf16[512,1024]{1,0:T(8,128)(2,1)S(1)} %copy-done.19), custom_call_target="tpu_custom_call" | custom-call | flops 33554432 | bytes 65536 | tf_op jit(solution)/shard_map/attention/pallas_call | solution.py:146
  18.7 2.5 %collective-permute-done.1 = bf16[1,256,512]{2,1,0:T(8,128)(2,1)S(1)} collective-permute-done((bf16[1,256,512]{2,1,0:T(8,128)(2,1)S(1)}, bf16[1,256,512]{2,1,0:T(8,128)(2,1)S(1)}, u32[]{:S(2)}, u32[]{:S(2)}) %collective-permute-start.1) | collective-permute-done | bytes 262176 | tf_op jit(solution)/shard_map/ppermute | solution.py:438
  21.2 1.6 collective-permute-start.2
  22.9 4.1 %collective-permute-start.5 = (bf16[2,256,512]{2,1,0:T(8,128)(2,1)S(1)}, bf16[2,256,512]{2,1,0:T(8,128)(2,1)S(1)}, u32[]{:S(2)}, u32[]{:S(2)}) collective-permute-start(bf16[2,256,512]{2,1,0:T(8,128)(2,1)S(1)} %pad_maximum_fusion.4), channel_id=1, source_target_pairs={{0,4},{1,5},{2,6},{3,7},{4,0},{5,1},{6,2},{7,3},{8,12},{9,13},{10,... | collective-permute-start | bytes 1572872 | tf_op jit(solution)/shard_map/ppermute | solution.py:438
  27.0 8.6 %collective-permute-done.3 = bf16[1,256,512]{2,1,0:T(8,128)(2,1)S(1)} collective-permute-done((bf16[1,256,512]{2,1,0:T(8,128)(2,1)S(1)}, bf16[1,256,512]{2,1,0:T(8,128)(2,1)S(1)}, u32[]{:S(2)}, u32[]{:S(2)}) %collective-permute-start.3) | collective-permute-done | bytes 262176 | tf_op jit(solution)/shard_map/ppermute | solution.py:438
  35.9 9.0 %collective-permute-done.5 = bf16[2,256,512]{2,1,0:T(8,128)(2,1)S(1)} collective-permute-done((bf16[2,256,512]{2,1,0:T(8,128)(2,1)S(1)}, bf16[2,256,512]{2,1,0:T(8,128)(2,1)S(1)}, u32[]{:S(2)}, u32[]{:S(2)}) %collective-permute-start.5) | collective-permute-done | bytes 524320 | tf_op jit(solution)/shard_map/ppermute | solution.py:438
  46.1 1.5 collective-permute-start.14
  47.6 10.0 %collective-permute-done.6 = bf16[2,256,512]{2,1,0:T(8,128)(2,1)S(1)} collective-permute-done((bf16[2,256,512]{2,1,0:T(8,128)(2,1)S(1)}, bf16[2,256,512]{2,1,0:T(8,128)(2,1)S(1)}, u32[]{:S(2)}, u32[]{:S(2)}) %collective-permute-start.6) | collective-permute-done | bytes 524320 | tf_op jit(solution)/shard_map/ppermute | solution.py:438
  59.5 1.1 fusion.11
  62.0 1.8 collective-permute-start.15
  63.7 1.5 collective-permute-done.7
  66.5 5.4 %collective-permute-done.8 = f32[32,384]{0,1:T(8,128)S(1)} collective-permute-done((f32[32,384]{0,1:T(8,128)S(1)}, f32[32,384]{0,1:T(8,128)S(1)}, u32[]{:S(2)}, u32[]{:S(2)}) %collective-permute-start.8) | collective-permute-done | bytes 49184 | tf_op jit(solution)/shard_map/ppermute | solution.py:438
  72.0 1.3 collective-permute-start.23
  73.4 2.7 %collective-permute-start.9 = (f32[64,384]{0,1:T(8,128)S(1)}, f32[64,384]{0,1:T(8,128)S(1)}, u32[]{:S(2)}, u32[]{:S(2)}) collective-permute-start(f32[64,384]{0,1:T(8,128)S(1)} %pad_maximum_fusion.9), channel_id=1, source_target_pairs={{0,8},{1,9},{2,10},{3,11},{4,12},{5,13},{6,14},{7,15},{8,0},{9,1},... | collective-permute-start | bytes 294920 | tf_op jit(solution)/shard_map/ppermute | solution.py:438
  76.1 8.8 %collective-permute-done.15.refs_5_ = bf16[2,256,512]{2,1,0:T(8,128)(2,1)} collective-permute-done((bf16[2,256,512]{2,1,0:T(8,128)(2,1)}, bf16[2,256,512]{2,1,0:T(8,128)(2,1)}, u32[]{:S(2)}, u32[]{:S(2)}) %collective-permute-start.15) | collective-permute-done | bytes 524320 | tf_op jit(solution)/shard_map/ppermute | solution.py:438
  86.1 1.1 broadcast_select_fusion.11
  89.4 9.7 %project_in.2 = (f32[256,1024]{1,0:T(8,128)}, bf16[256,1024]{1,0:T(8,128)(2,1)S(1)}) custom-call(s32[1]{0:T(128)} %bitcast.21.spot_ref, bf16[2,256,512]{2,1,0:T(8,128)(2,1)S(1)} %get-tuple-element.92.refs_0_, bf16[2,256,512]{2,1,0:T(8,128)(2,1)} %collective-permute-done.14.refs_1_, bf16[2,256,512]{2,1,0:T(8,128)(2,1)} %collective-permute-done.18.refs_2_, ...), custom_call_target="tpu_custom_call" | custom-call | flops 268435456 | bytes 720896 | tf_op jit(solution)/shard_map/project_in/pallas_call | solution.py:108
  100.3 1.1 broadcast_select_fusion.13
  103.2 10.8 %collective-permute-done.26.refs_5_ = bf16[2,256,512]{2,1,0:T(8,128)(2,1)S(1)} collective-permute-done((bf16[2,256,512]{2,1,0:T(8,128)(2,1)S(1)}, bf16[2,256,512]{2,1,0:T(8,128)(2,1)S(1)}, u32[]{:S(2)}, u32[]{:S(2)}) %collective-permute-start.26) | collective-permute-done | bytes 524320 | tf_op jit(solution)/shard_map/ppermute | solution.py:438
  114.8 1.1 broadcast_select_fusion.7
  115.9 1.3 collective-permute-start.22
  117.2 9.6 %project_in.3 = (f32[256,1024]{1,0:T(8,128)}, bf16[256,1024]{1,0:T(8,128)(2,1)}) custom-call(s32[1]{0:T(128)} %bitcast.21.spot_ref, bf16[2,256,512]{2,1,0:T(8,128)(2,1)S(1)} %get-tuple-element.100.refs_0_, bf16[2,256,512]{2,1,0:T(8,128)(2,1)S(1)} %collective-permute-done.23.refs_1_, bf16[2,256,512]{2,1,0:T(8,128)(2,1)} %collective-permute-done.24.refs_2_, ...), custom_call_target="tpu_custom_call" | custom-call | flops 268435456 | bytes 720896 | tf_op jit(solution)/shard_map/project_in/pallas_call | solution.py:108
  128.9 4.0 %project_out.5 = (f32[4,64,1024]{2,1,0:T(8,128)S(1)}, bf16[4,64,1024]{2,1,0:T(8,128)(2,1)}) custom-call(s32[3]{0:T(128)S(1)} %pad_add_fusion.spot_ref, bf16[512,512]{1,0:T(8,128)(2,1)S(1)} %attention.1.refs_0_.refs_8_, bf16[512,512]{1,0:T(8,128)(2,1)S(1)} %collective-permute-done.30.refs_1_.refs_9_, bf16[512,8192]{1,0:T(8,128)(2,1)} %refs_12_.5, ...), custom_call_target="tpu_custom_call" | custom-call | flops 67108864 | bytes 327680 | tf_op jit(solution)/shard_map/project_out/pallas_call | solution.py:335
  136.7 1.0 scan_weights.7.refs_0_
  137.7 1.7 scan_chunk.4
  139.4 1.9 scan_chunk.5
  141.3 1.3 copy-done.3
  143.5 1.7 scan_chunk.7
  145.2 1.1 collective-permute-done.37
  146.4 1.8 collective-permute-start.38
  151.1 4.0 %project_out.6 = (f32[4,64,1024]{2,1,0:T(8,128)S(1)}, bf16[4,64,1024]{2,1,0:T(8,128)(2,1)}) custom-call(s32[3]{0:T(128)S(1)} %pad_add_fusion.spot_ref, bf16[128,512]{1,0:T(8,128)(2,1)S(1)} %get-tuple-element.97.refs_0_, bf16[128,512]{1,0:T(8,128)(2,1)S(1)} %get-tuple-element.99.refs_1_, bf16[128,512]{1,0:T(8,128)(2,1)S(1)} %get-tuple-element.107.refs_2_, ...), custom_call_target="tpu_custom_call" | custom-call | flops 67108864 | bytes 327680 | tf_op jit(solution)/shard_map/project_out/pallas_call | solution.py:335
  155.1 3.0 %collective-permute-start.41 = (f32[4,128]{1,0:T(4,128)S(1)}, f32[4,128]{1,0:T(4,128)S(1)}, u32[]{:S(2)}, u32[]{:S(2)}) collective-permute-start(f32[4,128]{1,0:T(4,128)S(1)} %fusion.12), channel_id=1, source_target_pairs={{0,12},{1,13},{2,14},{3,15},{4,8},{5,9},{6,10},{7,11},{8,4},{9,5},... | collective-permute-start | bytes 6152 | tf_op jit(solution)/shard_map/ppermute | solution.py:438
  158.2 1.4 collective-permute-start.39
  160.6 2.0 collective-permute-done.40
  163.6 7.0 %project_out.7 = (f32[4,64,1024]{2,1,0:T(8,128)}, bf16[4,64,1024]{2,1,0:T(8,128)(2,1)}) custom-call(s32[3]{0:T(128)} %copy-done.26, bf16[128,512]{1,0:T(8,128)(2,1)} %copy-done.5, bf16[128,512]{1,0:T(8,128)(2,1)} %copy-done.6, bf16[128,512]{1,0:T(8,128)(2,1)} %copy-done.7, bf16[128,512]{1,0:T(8,128)(2,1)} %copy-done.8, bf16[128,512]{1,0:T(8,128)(2,1)} %copy-done.9, ...), custom_call_target="tpu_custom_call" | custom-call | flops 134217728 | bytes 458752 | tf_op jit(solution)/shard_map/project_out/pallas_call | solution.py:335
  171.5 7.0 %project_out.8 = (f32[4,64,1024]{2,1,0:T(8,128)}, bf16[4,64,1024]{2,1,0:T(8,128)(2,1)}) custom-call(s32[3]{0:T(128)} %copy-done.26, bf16[128,512]{1,0:T(8,128)(2,1)} %copy-done.5, bf16[128,512]{1,0:T(8,128)(2,1)} %copy-done.6, bf16[128,512]{1,0:T(8,128)(2,1)} %copy-done.7, bf16[128,512]{1,0:T(8,128)(2,1)} %copy-done.8, bf16[128,512]{1,0:T(8,128)(2,1)} %copy-done.9, ...), custom_call_target="tpu_custom_call" | custom-call | flops 134217728 | bytes 458752 | tf_op jit(solution)/shard_map/project_out/pallas_call | solution.py:335
  178.5 1.3 collective-permute-start.45
  179.8 7.0 %project_out.9 = (f32[4,64,1024]{2,1,0:T(8,128)}, bf16[4,64,1024]{2,1,0:T(8,128)(2,1)}) custom-call(s32[3]{0:T(128)} %copy-done.26, bf16[128,512]{1,0:T(8,128)(2,1)} %copy-done.5, bf16[128,512]{1,0:T(8,128)(2,1)} %copy-done.6, bf16[128,512]{1,0:T(8,128)(2,1)} %copy-done.7, bf16[128,512]{1,0:T(8,128)(2,1)} %copy-done.8, bf16[128,512]{1,0:T(8,128)(2,1)} %copy-done.9, ...), custom_call_target="tpu_custom_call" | custom-call | flops 134217728 | bytes 458752 | tf_op jit(solution)/shard_map/project_out/pallas_call | solution.py:335
  188.2 1.0 copy-done.21
  189.2 1.3 add_near.8
  191.1 1.2 copy-done.16
  192.4 1.1 add_near.10
  193.5 1.5 collective-permute-start.44
  195.0 6.0 %collective-permute-done.42.came_ref = bf16[2,64,1024]{2,1,0:T(8,128)(2,1)S(1)} collective-permute-done((bf16[2,64,1024]{2,1,0:T(8,128)(2,1)S(1)}, bf16[2,64,1024]{2,1,0:T(8,128)(2,1)S(1)}, u32[]{:S(2)}, u32[]{:S(2)}) %collective-permute-start.42) | collective-permute-done | bytes 262176 | tf_op jit(solution)/shard_map/ppermute | solution.py:438
  201.8 1.2 copy-done.17
  203.0 1.1 add_near.12
  204.1 1.9 collective-permute-start.46
  206.1 1.8 collective-permute-done.44.came_ref
  207.9 1.1 add_near.14
  209.1 1.9 collective-permute-start.49
  211.0 1.1 collective-permute-start.50
  212.1 1.0 collective-permute-done.46.came_ref
  214.1 7.2 %collective-permute-done.49.came_ref = bf16[2,64,1024]{2,1,0:T(8,128)(2,1)S(1)} collective-permute-done((bf16[2,64,1024]{2,1,0:T(8,128)(2,1)S(1)}, bf16[2,64,1024]{2,1,0:T(8,128)(2,1)S(1)}, u32[]{:S(2)}, u32[]{:S(2)}) %collective-permute-start.49) | collective-permute-done | bytes 262176 | tf_op jit(solution)/shard_map/ppermute | solution.py:438
  221.4 1.1 collective-permute-start.52
  222.4 1.9 collective-permute-done.51.refs_6_
  224.3 5.5 %collective-permute-done.52.refs_7_ = bf16[64,1024]{1,0:T(8,128)(2,1)S(1)} collective-permute-done((bf16[64,1024]{1,0:T(8,128)(2,1)S(1)}, bf16[64,1024]{1,0:T(8,128)(2,1)S(1)}, u32[]{:S(2)}, u32[]{:S(2)}) %collective-permute-start.52) | collective-permute-done | bytes 131104 | tf_op jit(solution)/shard_map/ppermute | solution.py:438
  230.6 1.5 collective-permute-done.53
  (194 shorter events, 32.8 us)
Async XLA Ops:
  2.5 1.9 collective-permute-start
  4.4 67.5 %collective-permute-start.16 = (bf16[512,8192]{1,0:T(8,128)(2,1)}, bf16[512,8192]{1,0:T(8,128)(2,1)}, u32[]{:S(2)}, u32[]{:S(2)}) collective-permute-start(bf16[512,8192]{1,0:T(8,128)(2,1)} %refs_12_.5), channel_id=1, source_target_pairs={{0,1},{1,0},{2,3},{3,2},{4,5},{5,4},{6,7},{7,6},{8,9},{9,8},{10,11... | collective-permute-start | bytes 25165832 | tf_op jit(solution)/shard_map/ppermute | solution.py:438
  4.9 67.1 %collective-permute-start.17 = (bf16[512,8192]{1,0:T(8,128)(2,1)}, bf16[512,8192]{1,0:T(8,128)(2,1)}, u32[]{:S(2)}, u32[]{:S(2)}) collective-permute-start(bf16[512,8192]{1,0:T(8,128)(2,1)} %refs_10_.5), channel_id=1, source_target_pairs={{0,1},{1,0},{2,3},{3,2},{4,5},{5,4},{6,7},{7,6},{8,9},{9,8},{10,11... | collective-permute-start | bytes 25165832 | tf_op jit(solution)/shard_map/ppermute | solution.py:438
  5.0 16.2 %collective-permute-start.1 = (bf16[1,256,512]{2,1,0:T(8,128)(2,1)S(1)}, bf16[1,256,512]{2,1,0:T(8,128)(2,1)S(1)}, u32[]{:S(2)}, u32[]{:S(2)}) collective-permute-start(bf16[1,256,512]{2,1,0:T(8,128)(2,1)S(1)} %bitcast.48), channel_id=1, source_target_pairs={{0,8},{1,9},{2,10},{3,11},{4,12},{5,13},{6,14},{7,15},{8,0},{9,1},... | collective-permute-start | bytes 786440 | tf_op jit(solution)/shard_map/ppermute | solution.py:438
  18.7 110.2 %copy-start = (bf16[512,512]{1,0:T(8,128)(2,1)}, bf16[512,512]{1,0:T(8,128)(2,1)S(1)}, u32[]{:S(2)}) copy-start(bf16[512,512]{1,0:T(8,128)(2,1)S(1)} %attention.1.refs_0_.refs_8_) | copy-start | bytes 1572868
  21.2 14.5 %collective-permute-start.3 = (bf16[1,256,512]{2,1,0:T(8,128)(2,1)S(1)}, bf16[1,256,512]{2,1,0:T(8,128)(2,1)S(1)}, u32[]{:S(2)}, u32[]{:S(2)}) collective-permute-start(bf16[1,256,512]{2,1,0:T(8,128)(2,1)S(1)} %bitcast.45), channel_id=1, source_target_pairs={{0,8},{1,9},{2,10},{3,11},{4,12},{5,13},{6,14},{7,15},{8,0},{9,1},... | collective-permute-start | bytes 786440 | tf_op jit(solution)/shard_map/ppermute | solution.py:438
  21.2 14.5 %collective-permute-start.2 = (f32[128,384]{1,0:T(8,128)S(1)}, f32[128,384]{1,0:T(8,128)S(1)}, u32[]{:S(2)}, u32[]{:S(2)}) collective-permute-start(f32[128,384]{1,0:T(8,128)S(1)} %dynamic-slice_bitcast_fusion.1), channel_id=1, source_target_pairs={{0,2},{1,3},{2,0},{3,1},{4,6},{5,7},{6,4},{7,5},{8,10},{9,11},{10,... | collective-permute-start | bytes 589832 | tf_op jit(solution)/shard_map/ppermute | solution.py:438
  22.9 22.0 %collective-permute-start.5 = (bf16[2,256,512]{2,1,0:T(8,128)(2,1)S(1)}, bf16[2,256,512]{2,1,0:T(8,128)(2,1)S(1)}, u32[]{:S(2)}, u32[]{:S(2)}) collective-permute-start(bf16[2,256,512]{2,1,0:T(8,128)(2,1)S(1)} %pad_maximum_fusion.4), channel_id=1, source_target_pairs={{0,4},{1,5},{2,6},{3,7},{4,0},{5,1},{6,2},{7,3},{8,12},{9,13},{10,... | collective-permute-start | bytes 1572872 | tf_op jit(solution)/shard_map/ppermute | solution.py:438
  35.8 10.3 %collective-permute-start.4 = (f32[64,384]{1,0:T(8,128)S(1)}, f32[64,384]{1,0:T(8,128)S(1)}, u32[]{:S(2)}, u32[]{:S(2)}) collective-permute-start(f32[64,384]{1,0:T(8,128)S(1)} %dynamic-slice_bitcast_fusion.2), channel_id=1, source_target_pairs={{0,8},{1,9},{2,10},{3,11},{4,12},{5,13},{6,14},{7,15},{8,0},{9,1},... | collective-permute-start | bytes 294920 | tf_op jit(solution)/shard_map/ppermute | solution.py:438
  44.9 12.7 %collective-permute-start.6 = (bf16[2,256,512]{2,1,0:T(8,128)(2,1)S(1)}, bf16[2,256,512]{2,1,0:T(8,128)(2,1)S(1)}, u32[]{:S(2)}, u32[]{:S(2)}) collective-permute-start(bf16[2,256,512]{2,1,0:T(8,128)(2,1)S(1)} %pad_maximum_fusion.2), channel_id=1, source_target_pairs={{0,4},{1,5},{2,6},{3,7},{4,0},{5,1},{6,2},{7,3},{8,12},{9,13},{10,... | collective-permute-start | bytes 1572872 | tf_op jit(solution)/shard_map/ppermute | solution.py:438
  45.8 15.8 %collective-permute-start.10 = (bf16[2,256,512]{2,1,0:T(8,128)(2,1)S(1)}, bf16[2,256,512]{2,1,0:T(8,128)(2,1)S(1)}, u32[]{:S(2)}, u32[]{:S(2)}) collective-permute-start(bf16[2,256,512]{2,1,0:T(8,128)(2,1)S(1)} %get-tuple-element.92.refs_0_), channel_id=1, source_target_pairs={{0,2},{1,3},{2,0},{3,1},{4,6},{5,7},{6,4},{7,5},{8,10},{9,11},{10,... | collective-permute-start | bytes 1572872 | tf_op jit(solution)/shard_map/ppermute | solution.py:438
  46.1 15.9 %collective-permute-start.14 = (bf16[2,256,512]{2,1,0:T(8,128)(2,1)}, bf16[2,256,512]{2,1,0:T(8,128)(2,1)}, u32[]{:S(2)}, u32[]{:S(2)}) collective-permute-start(bf16[2,256,512]{2,1,0:T(8,128)(2,1)} %get-tuple-element.149), channel_id=1, source_target_pairs={{0,16},{16,0},{1,17},{17,1},{2,18},{18,2},{3,19},{19,3},{4,20},{20... | collective-permute-start | bytes 1572872 | tf_op jit(solution)/shard_map/ppermute | solution.py:441
  59.2 6.0 %collective-permute-start.7 = (f32[32,384]{0,1:T(8,128)}, f32[32,384]{0,1:T(8,128)}, u32[]{:S(2)}, u32[]{:S(2)}) collective-permute-start(f32[32,384]{0,1:T(8,128)} %bitcast.17), channel_id=1, source_target_pairs={{0,4},{1,5},{2,6},{3,7},{4,0},{5,1},{6,2},{7,3},{8,12},{9,13},{10,... | collective-permute-start | bytes 147464 | tf_op jit(solution)/shard_map/ppermute | solution.py:438
  61.6 23.9 %collective-permute-start.11 = (bf16[2,256,512]{2,1,0:T(8,128)(2,1)S(1)}, bf16[2,256,512]{2,1,0:T(8,128)(2,1)S(1)}, u32[]{:S(2)}, u32[]{:S(2)}) collective-permute-start(bf16[2,256,512]{2,1,0:T(8,128)(2,1)S(1)} %get-tuple-element.100.refs_0_), channel_id=1, source_target_pairs={{0,2},{1,3},{2,0},{3,1},{4,6},{5,7},{6,4},{7,5},{8,10},{9,11},{10,... | collective-permute-start | bytes 1572872 | tf_op jit(solution)/shard_map/ppermute | solution.py:438
  62.0 23.0 %collective-permute-start.15 = (bf16[2,256,512]{2,1,0:T(8,128)(2,1)}, bf16[2,256,512]{2,1,0:T(8,128)(2,1)}, u32[]{:S(2)}, u32[]{:S(2)}) collective-permute-start(bf16[2,256,512]{2,1,0:T(8,128)(2,1)} %collective-permute-done.14.refs_1_), channel_id=1, source_target_pairs={{0,2},{1,3},{2,0},{3,1},{4,6},{5,7},{6,4},{7,5},{8,10},{9,11},{10,... | collective-permute-start | bytes 1572872 | tf_op jit(solution)/shard_map/ppermute | solution.py:438
  66.2 5.7 %collective-permute-start.8 = (f32[32,384]{0,1:T(8,128)S(1)}, f32[32,384]{0,1:T(8,128)S(1)}, u32[]{:S(2)}, u32[]{:S(2)}) collective-permute-start(f32[32,384]{0,1:T(8,128)S(1)} %bitcast_add_fusion.1), channel_id=1, source_target_pairs={{0,4},{1,5},{2,6},{3,7},{4,0},{5,1},{6,2},{7,3},{8,12},{9,13},{10,... | collective-permute-start | bytes 147464 | tf_op jit(solution)/shard_map/ppermute | solution.py:438
  66.5 47.4 %copy-start.38 = (f32[8]{0:T(128)S(1)}, f32[8]{0:T(128)}, u32[]{:S(2)}) copy-start(f32[8]{0:T(128)} %param.20) | copy-start | bytes 100
  66.5 47.4 %copy-start.37 = (f32[8]{0:T(128)S(1)}, f32[8]{0:T(128)}, u32[]{:S(2)}) copy-start(f32[8]{0:T(128)} %param.21) | copy-start | bytes 100
  72.0 13.6 %copy-start.31 = (f32[32,384]{0,1:T(8,128)}, f32[32,384]{0,1:T(8,128)S(1)}, u32[]{:S(2)}) copy-start(f32[32,384]{0,1:T(8,128)S(1)} %get-tuple-element.164) | copy-start | bytes 147460
  72.0 15.4 %collective-permute-start.23 = (bf16[2,256,512]{2,1,0:T(8,128)(2,1)}, bf16[2,256,512]{2,1,0:T(8,128)(2,1)S(1)}, u32[]{:S(2)}, u32[]{:S(2)}) collective-permute-start(bf16[2,256,512]{2,1,0:T(8,128)(2,1)} %get-tuple-element.90), channel_id=1, source_target_pairs={{0,16},{16,0},{1,17},{17,1},{2,18},{18,2},{3,19},{19,3},{4,20},{20... | collective-permute-start | bytes 1572872 | tf_op jit(solution)/shard_map/ppermute | solution.py:441
  73.4 12.1 %collective-permute-start.9 = (f32[64,384]{0,1:T(8,128)S(1)}, f32[64,384]{0,1:T(8,128)S(1)}, u32[]{:S(2)}, u32[]{:S(2)}) collective-permute-start(f32[64,384]{0,1:T(8,128)S(1)} %pad_maximum_fusion.9), channel_id=1, source_target_pairs={{0,8},{1,9},{2,10},{3,11},{4,12},{5,13},{6,14},{7,15},{8,0},{9,1},... | collective-permute-start | bytes 294920 | tf_op jit(solution)/shard_map/ppermute | solution.py:438
  84.9 3.8 %collective-permute-start.20 = (bf16[2,256,512]{2,1,0:T(8,128)(2,1)S(1)}, bf16[2,256,512]{2,1,0:T(8,128)(2,1)}, u32[]{:S(2)}, u32[]{:S(2)}) collective-permute-start(bf16[2,256,512]{2,1,0:T(8,128)(2,1)S(1)} %collective-permute-done.10.refs_4_), channel_id=1, source_target_pairs={{0,1},{1,0},{2,3},{3,2},{4,5},{5,4},{6,7},{7,6},{8,9},{9,8},{10,11... | collective-permute-start | bytes 1572872 | tf_op jit(solution)/shard_map/ppermute | solution.py:438
  84.9 3.5 %collective-permute-start.18 = (bf16[2,256,512]{2,1,0:T(8,128)(2,1)S(1)}, bf16[2,256,512]{2,1,0:T(8,128)(2,1)}, u32[]{:S(2)}, u32[]{:S(2)}) collective-permute-start(bf16[2,256,512]{2,1,0:T(8,128)(2,1)S(1)} %get-tuple-element.92.refs_0_), channel_id=1, source_target_pairs={{0,1},{1,0},{2,3},{3,2},{4,5},{5,4},{6,7},{7,6},{8,9},{9,8},{10,11... | collective-permute-start | bytes 1572872 | tf_op jit(solution)/shard_map/ppermute | solution.py:438
  85.4 3.2 %collective-permute-start.19 = (bf16[2,256,512]{2,1,0:T(8,128)(2,1)}, bf16[2,256,512]{2,1,0:T(8,128)(2,1)}, u32[]{:S(2)}, u32[]{:S(2)}) collective-permute-start(bf16[2,256,512]{2,1,0:T(8,128)(2,1)} %collective-permute-done.14.refs_1_), channel_id=1, source_target_pairs={{0,1},{1,0},{2,3},{3,2},{4,5},{5,4},{6,7},{7,6},{8,9},{9,8},{10,11... | collective-permute-start | bytes 1572872 | tf_op jit(solution)/shard_map/ppermute | solution.py:438
  86.1 3.3 %collective-permute-start.21 = (bf16[2,256,512]{2,1,0:T(8,128)(2,1)}, bf16[2,256,512]{2,1,0:T(8,128)(2,1)}, u32[]{:S(2)}, u32[]{:S(2)}) collective-permute-start(bf16[2,256,512]{2,1,0:T(8,128)(2,1)} %collective-permute-done.15.refs_5_), channel_id=1, source_target_pairs={{0,1},{1,0},{2,3},{3,2},{4,5},{5,4},{6,7},{7,6},{8,9},{9,8},{10,11... | collective-permute-start | bytes 1572872 | tf_op jit(solution)/shard_map/ppermute | solution.py:438
  87.4 12.8 %collective-permute-start.12 = (f32[128,384]{0,1:T(8,128)S(1)}, f32[128,384]{0,1:T(8,128)}, u32[]{:S(2)}, u32[]{:S(2)}) collective-permute-start(f32[128,384]{0,1:T(8,128)S(1)} %pad_maximum_fusion.10), channel_id=1, source_target_pairs={{0,2},{1,3},{2,0},{3,1},{4,6},{5,7},{6,4},{7,5},{8,10},{9,11},{10,... | collective-permute-start | bytes 589832 | tf_op jit(solution)/shard_map/ppermute | solution.py:438
  100.0 14.0 %collective-permute-start.26 = (bf16[2,256,512]{2,1,0:T(8,128)(2,1)S(1)}, bf16[2,256,512]{2,1,0:T(8,128)(2,1)S(1)}, u32[]{:S(2)}, u32[]{:S(2)}) collective-permute-start(bf16[2,256,512]{2,1,0:T(8,128)(2,1)S(1)} %collective-permute-done.23.refs_1_), channel_id=1, source_target_pairs={{0,2},{1,3},{2,0},{3,1},{4,6},{5,7},{6,4},{7,5},{8,10},{9,11},{10,... | collective-permute-start | bytes 1572872 | tf_op jit(solution)/shard_map/ppermute | solution.py:438
  102.1 12.1 %collective-permute-start.13 = (f32[256,384]{0,1:T(8,128)}, f32[256,384]{0,1:T(8,128)}, u32[]{:S(2)}, u32[]{:S(2)}) collective-permute-start(f32[256,384]{0,1:T(8,128)} %pad_maximum_fusion.8), channel_id=1, source_target_pairs={{0,1},{1,0},{2,3},{3,2},{4,5},{5,4},{6,7},{7,6},{8,9},{9,8},{10,11... | collective-permute-start | bytes 1179656 | tf_op jit(solution)/shard_map/ppermute | solution.py:438
  102.1 13.8 %collective-permute-start.24 = (bf16[2,256,512]{2,1,0:T(8,128)(2,1)S(1)}, bf16[2,256,512]{2,1,0:T(8,128)(2,1)}, u32[]{:S(2)}, u32[]{:S(2)}) collective-permute-start(bf16[2,256,512]{2,1,0:T(8,128)(2,1)S(1)} %get-tuple-element.100.refs_0_), channel_id=1, source_target_pairs={{0,1},{1,0},{2,3},{3,2},{4,5},{5,4},{6,7},{7,6},{8,9},{9,8},{10,11... | collective-permute-start | bytes 1572872 | tf_op jit(solution)/shard_map/ppermute | solution.py:438
  102.6 14.6 %collective-permute-start.27 = (bf16[2,256,512]{2,1,0:T(8,128)(2,1)S(1)}, bf16[2,256,512]{2,1,0:T(8,128)(2,1)}, u32[]{:S(2)}, u32[]{:S(2)}) collective-permute-start(bf16[2,256,512]{2,1,0:T(8,128)(2,1)S(1)} %collective-permute-done.11.refs_4_), channel_id=1, source_target_pairs={{0,1},{1,0},{2,3},{3,2},{4,5},{5,4},{6,7},{7,6},{8,9},{9,8},{10,11... | collective-permute-start | bytes 1572872 | tf_op jit(solution)/shard_map/ppermute | solution.py:438
  102.6 14.6 %collective-permute-start.25 = (bf16[2,256,512]{2,1,0:T(8,128)(2,1)S(1)}, bf16[2,256,512]{2,1,0:T(8,128)(2,1)}, u32[]{:S(2)}, u32[]{:S(2)}) collective-permute-start(bf16[2,256,512]{2,1,0:T(8,128)(2,1)S(1)} %collective-permute-done.23.refs_1_), channel_id=1, source_target_pairs={{0,1},{1,0},{2,3},{3,2},{4,5},{5,4},{6,7},{7,6},{8,9},{9,8},{10,11... | collective-permute-start | bytes 1572872 | tf_op jit(solution)/shard_map/ppermute | solution.py:438
  113.9 3.3 %collective-permute-start.28 = (bf16[2,256,512]{2,1,0:T(8,128)(2,1)S(1)}, bf16[2,256,512]{2,1,0:T(8,128)(2,1)}, u32[]{:S(2)}, u32[]{:S(2)}) collective-permute-start(bf16[2,256,512]{2,1,0:T(8,128)(2,1)S(1)} %collective-permute-done.26.refs_5_), channel_id=1, source_target_pairs={{0,1},{1,0},{2,3},{3,2},{4,5},{5,4},{6,7},{7,6},{8,9},{9,8},{10,11... | collective-permute-start | bytes 1572872 | tf_op jit(solution)/shard_map/ppermute | solution.py:438
  114.2 36.9 %copy-start.26 = (s32[3]{0:T(128)}, s32[3]{0:T(128)S(1)}, u32[]{:S(2)}) copy-start(s32[3]{0:T(128)S(1)} %pad_add_fusion.spot_ref) | copy-start | bytes 40
  114.2 13.8 %copy-start.36 = (f32[8]{0:T(128)S(1)}, f32[8]{0:T(128)}, u32[]{:S(2)}) copy-start(f32[8]{0:T(128)} %param.19) | copy-start | bytes 100
  114.2 14.6 %collective-permute-start.30 = (bf16[512,512]{1,0:T(8,128)(2,1)S(1)}, bf16[512,512]{1,0:T(8,128)(2,1)S(1)}, u32[]{:S(2)}, u32[]{:S(2)}) collective-permute-start(bf16[512,512]{1,0:T(8,128)(2,1)S(1)} %attention.1.refs_0_.refs_8_), channel_id=1, source_target_pairs={{0,1},{1,0},{2,3},{3,2},{4,5},{5,4},{6,7},{7,6},{8,9},{9,8},{10,11... | collective-permute-start | bytes 1572872 | tf_op jit(solution)/shard_map/ppermute | solution.py:438
  115.9 21.8 %collective-permute-start.22 = (bf16[256,1024]{1,0:T(8,128)(2,1)}, bf16[256,1024]{1,0:T(8,128)(2,1)}, u32[]{:S(2)}, u32[]{:S(2)}) collective-permute-start(bf16[256,1024]{1,0:T(8,128)(2,1)} %copy-done.28), channel_id=1, source_target_pairs={{0,16},{16,0},{1,17},{17,1},{2,18},{18,2},{3,19},{19,3},{4,20},{20... | collective-permute-start | bytes 1572872 | tf_op jit(solution)/shard_map/ppermute | solution.py:441
  126.8 14.5 %collective-permute-start.29 = (bf16[256,1024]{1,0:T(8,128)(2,1)}, bf16[256,1024]{1,0:T(8,128)(2,1)S(1)}, u32[]{:S(2)}, u32[]{:S(2)}) collective-permute-start(bf16[256,1024]{1,0:T(8,128)(2,1)} %get-tuple-element.105), channel_id=1, source_target_pairs={{0,16},{16,0},{1,17},{17,1},{2,18},{18,2},{3,19},{19,3},{4,20},{20... | collective-permute-start | bytes 1572872 | tf_op jit(solution)/shard_map/ppermute | solution.py:441
  133.9 14.8 %collective-permute-start.31 = (bf16[4,64,1024]{2,1,0:T(8,128)(2,1)}, bf16[4,64,1024]{2,1,0:T(8,128)(2,1)S(1)}, u32[]{:S(2)}, u32[]{:S(2)}) collective-permute-start(bf16[4,64,1024]{2,1,0:T(8,128)(2,1)} %get-tuple-element.111), channel_id=1, source_target_pairs={{0,2},{1,3},{2,0},{3,1},{4,6},{5,7},{6,4},{7,5},{8,10},{9,11},{10,... | collective-permute-start | bytes 1572872 | tf_op jit(solution)/shard_map/ppermute | solution.py:438
  139.4 15.7 %copy-start.5 = (bf16[128,512]{1,0:T(8,128)(2,1)}, bf16[128,512]{1,0:T(8,128)(2,1)S(1)}, u32[]{:S(2)}) copy-start(bf16[128,512]{1,0:T(8,128)(2,1)S(1)} %get-tuple-element.97.refs_0_) | copy-start | bytes 393220
  141.3 13.8 %copy-start.6 = (bf16[128,512]{1,0:T(8,128)(2,1)}, bf16[128,512]{1,0:T(8,128)(2,1)S(1)}, u32[]{:S(2)}) copy-start(bf16[128,512]{1,0:T(8,128)(2,1)S(1)} %get-tuple-element.99.refs_1_) | copy-start | bytes 393220
  145.2 1.2 collective-permute-start.37
  146.4 3.7 %collective-permute-start.38 = (f32[4,128]{1,0:T(4,128)S(1)}, f32[4,128]{1,0:T(4,128)S(1)}, u32[]{:S(2)}, u32[]{:S(2)}) collective-permute-start(f32[4,128]{1,0:T(4,128)S(1)} %fusion.9), channel_id=1, source_target_pairs={{0,2},{1,3},{2,0},{3,1},{4,6},{5,7},{6,4},{7,5},{8,10},{9,11},{10,... | collective-permute-start | bytes 6152 | tf_op jit(solution)/shard_map/ppermute | solution.py:438
  148.2 1.9 collective-permute-start.32
  148.2 1.9 collective-permute-start.33
  148.7 2.3 collective-permute-start.35
  149.5 1.5 collective-permute-start.34
  155.1 5.5 %collective-permute-start.41 = (f32[4,128]{1,0:T(4,128)S(1)}, f32[4,128]{1,0:T(4,128)S(1)}, u32[]{:S(2)}, u32[]{:S(2)}) collective-permute-start(f32[4,128]{1,0:T(4,128)S(1)} %fusion.12), channel_id=1, source_target_pairs={{0,12},{1,13},{2,14},{3,15},{4,8},{5,9},{6,10},{7,11},{8,4},{9,5},... | collective-permute-start | bytes 6152 | tf_op jit(solution)/shard_map/ppermute | solution.py:438
  158.1 4.5 %collective-permute-start.40 = (f32[4,128]{1,0:T(4,128)S(1)}, f32[4,128]{1,0:T(4,128)S(1)}, u32[]{:S(2)}, u32[]{:S(2)}) collective-permute-start(f32[4,128]{1,0:T(4,128)S(1)} %fusion.12), channel_id=1, source_target_pairs={{0,8},{1,9},{2,10},{3,11},{4,12},{5,13},{6,14},{7,15},{8,0},{9,1},... | collective-permute-start | bytes 6152 | tf_op jit(solution)/shard_map/ppermute | solution.py:438
  158.2 4.4 %collective-permute-start.39 = (f32[4,128]{1,0:T(4,128)S(1)}, f32[4,128]{1,0:T(4,128)S(1)}, u32[]{:S(2)}, u32[]{:S(2)}) collective-permute-start(f32[4,128]{1,0:T(4,128)S(1)} %fusion.12), channel_id=1, source_target_pairs={{0,4},{1,5},{2,6},{3,7},{4,0},{5,1},{6,2},{7,3},{8,12},{9,13},{10,... | collective-permute-start | bytes 6152 | tf_op jit(solution)/shard_map/ppermute | solution.py:438
  159.6 28.5 %collective-permute-start.36 = (bf16[4,64,1024]{2,1,0:T(8,128)(2,1)}, bf16[4,64,1024]{2,1,0:T(8,128)(2,1)}, u32[]{:S(2)}, u32[]{:S(2)}) collective-permute-start(bf16[4,64,1024]{2,1,0:T(8,128)(2,1)} %get-tuple-element.114), channel_id=1, source_target_pairs={{0,2},{1,3},{2,0},{3,1},{4,6},{5,7},{6,4},{7,5},{8,10},{9,11},{10,... | collective-permute-start | bytes 1572872 | tf_op jit(solution)/shard_map/ppermute | solution.py:438
  170.6 20.5 %collective-permute-start.43 = (bf16[4,64,1024]{2,1,0:T(8,128)(2,1)}, bf16[4,64,1024]{2,1,0:T(8,128)(2,1)}, u32[]{:S(2)}, u32[]{:S(2)}) collective-permute-start(bf16[4,64,1024]{2,1,0:T(8,128)(2,1)} %get-tuple-element.125), channel_id=1, source_target_pairs={{0,2},{1,3},{2,0},{3,1},{4,6},{5,7},{6,4},{7,5},{8,10},{9,11},{10,... | collective-permute-start | bytes 1572872 | tf_op jit(solution)/shard_map/ppermute | solution.py:438
  178.5 23.3 %collective-permute-start.45 = (bf16[4,64,1024]{2,1,0:T(8,128)(2,1)}, bf16[4,64,1024]{2,1,0:T(8,128)(2,1)}, u32[]{:S(2)}, u32[]{:S(2)}) collective-permute-start(bf16[4,64,1024]{2,1,0:T(8,128)(2,1)} %get-tuple-element.130), channel_id=1, source_target_pairs={{0,2},{1,3},{2,0},{3,1},{4,6},{5,7},{6,4},{7,5},{8,10},{9,11},{10,... | collective-permute-start | bytes 1572872 | tf_op jit(solution)/shard_map/ppermute | solution.py:438
  179.8 50.0 %copy-start.27 = (s32[3]{0:T(128)S(1)}, s32[3]{0:T(128)}, u32[]{:S(2)}) copy-start(s32[3]{0:T(128)} %copy-done.26) | copy-start | bytes 40
  186.8 21.1 %copy-start.15 = (f32[4,64,1024]{2,1,0:T(8,128)S(1)}, f32[4,64,1024]{2,1,0:T(8,128)}, u32[]{:S(2)}) copy-start(f32[4,64,1024]{2,1,0:T(8,128)} %get-tuple-element.136.keep_ref) | copy-start | bytes 3145732
  186.8 21.1 %collective-permute-start.47 = (bf16[4,64,1024]{2,1,0:T(8,128)(2,1)}, bf16[4,64,1024]{2,1,0:T(8,128)(2,1)}, u32[]{:S(2)}, u32[]{:S(2)}) collective-permute-start(bf16[4,64,1024]{2,1,0:T(8,128)(2,1)} %get-tuple-element.137), channel_id=1, source_target_pairs={{0,2},{1,3},{2,0},{3,1},{4,6},{5,7},{6,4},{7,5},{8,10},{9,11},{10,... | collective-permute-start | bytes 1572872 | tf_op jit(solution)/shard_map/ppermute | solution.py:438
  190.5 10.5 %collective-permute-start.42 = (bf16[2,64,1024]{2,1,0:T(8,128)(2,1)S(1)}, bf16[2,64,1024]{2,1,0:T(8,128)(2,1)S(1)}, u32[]{:S(2)}, u32[]{:S(2)}) collective-permute-start(bf16[2,64,1024]{2,1,0:T(8,128)(2,1)S(1)} %get-tuple-element.122), channel_id=1, source_target_pairs={{0,4},{1,5},{2,6},{3,7},{4,0},{5,1},{6,2},{7,3},{8,12},{9,13},{10,... | collective-permute-start | bytes 786440 | tf_op jit(solution)/shard_map/ppermute | solution.py:438
  193.5 14.4 %collective-permute-start.44 = (bf16[2,64,1024]{2,1,0:T(8,128)(2,1)S(1)}, bf16[2,64,1024]{2,1,0:T(8,128)(2,1)S(1)}, u32[]{:S(2)}, u32[]{:S(2)}) collective-permute-start(bf16[2,64,1024]{2,1,0:T(8,128)(2,1)S(1)} %get-tuple-element.127), channel_id=1, source_target_pairs={{0,4},{1,5},{2,6},{3,7},{4,0},{5,1},{6,2},{7,3},{8,12},{9,13},{10,... | collective-permute-start | bytes 786440 | tf_op jit(solution)/shard_map/ppermute | solution.py:438
  201.0 6.9 %collective-permute-start.48 = (bf16[64,1024]{1,0:T(8,128)(2,1)S(1)}, bf16[64,1024]{1,0:T(8,128)(2,1)S(1)}, u32[]{:S(2)}, u32[]{:S(2)}) collective-permute-start(bf16[64,1024]{1,0:T(8,128)(2,1)S(1)} %bitcast.70), channel_id=1, source_target_pairs={{0,8},{1,9},{2,10},{3,11},{4,12},{5,13},{6,14},{7,15},{8,0},{9,1},... | collective-permute-start | bytes 393224 | tf_op jit(solution)/shard_map/ppermute | solution.py:438
  204.1 9.0 %collective-permute-start.46 = (bf16[2,64,1024]{2,1,0:T(8,128)(2,1)S(1)}, bf16[2,64,1024]{2,1,0:T(8,128)(2,1)S(1)}, u32[]{:S(2)}, u32[]{:S(2)}) collective-permute-start(bf16[2,64,1024]{2,1,0:T(8,128)(2,1)S(1)} %get-tuple-element.134), channel_id=1, source_target_pairs={{0,4},{1,5},{2,6},{3,7},{4,0},{5,1},{6,2},{7,3},{8,12},{9,13},{10,... | collective-permute-start | bytes 786440 | tf_op jit(solution)/shard_map/ppermute | solution.py:438
  209.1 12.2 %collective-permute-start.49 = (bf16[2,64,1024]{2,1,0:T(8,128)(2,1)S(1)}, bf16[2,64,1024]{2,1,0:T(8,128)(2,1)S(1)}, u32[]{:S(2)}, u32[]{:S(2)}) collective-permute-start(bf16[2,64,1024]{2,1,0:T(8,128)(2,1)S(1)} %get-tuple-element.141), channel_id=1, source_target_pairs={{0,4},{1,5},{2,6},{3,7},{4,0},{5,1},{6,2},{7,3},{8,12},{9,13},{10,... | collective-permute-start | bytes 786440 | tf_op jit(solution)/shard_map/ppermute | solution.py:438
  211.0 11.4 %collective-permute-start.50 = (bf16[64,1024]{1,0:T(8,128)(2,1)S(1)}, bf16[64,1024]{1,0:T(8,128)(2,1)S(1)}, u32[]{:S(2)}, u32[]{:S(2)}) collective-permute-start(bf16[64,1024]{1,0:T(8,128)(2,1)S(1)} %bitcast.69), channel_id=1, source_target_pairs={{0,8},{1,9},{2,10},{3,11},{4,12},{5,13},{6,14},{7,15},{8,0},{9,1},... | collective-permute-start | bytes 393224 | tf_op jit(solution)/shard_map/ppermute | solution.py:438
  213.2 11.2 %collective-permute-start.51 = (bf16[64,1024]{1,0:T(8,128)(2,1)S(1)}, bf16[64,1024]{1,0:T(8,128)(2,1)S(1)}, u32[]{:S(2)}, u32[]{:S(2)}) collective-permute-start(bf16[64,1024]{1,0:T(8,128)(2,1)S(1)} %bitcast.71), channel_id=1, source_target_pairs={{0,8},{1,9},{2,10},{3,11},{4,12},{5,13},{6,14},{7,15},{8,0},{9,1},... | collective-permute-start | bytes 393224 | tf_op jit(solution)/shard_map/ppermute | solution.py:438
  221.4 8.4 %collective-permute-start.52 = (bf16[64,1024]{1,0:T(8,128)(2,1)S(1)}, bf16[64,1024]{1,0:T(8,128)(2,1)S(1)}, u32[]{:S(2)}, u32[]{:S(2)}) collective-permute-start(bf16[64,1024]{1,0:T(8,128)(2,1)S(1)} %bitcast.72), channel_id=1, source_target_pairs={{0,8},{1,9},{2,10},{3,11},{4,12},{5,13},{6,14},{7,15},{8,0},{9,1},... | collective-permute-start | bytes 393224 | tf_op jit(solution)/shard_map/ppermute | solution.py:438
  230.5 1.6 collective-permute-start.53
  (29 other events, 133.2 us)
